TPU v7x, 32 devices: a whole 2x2x4 slice. The times are simulated.
32 devices in a mesh: lon: 4 (over z), lat: 2 (over x), ens: 4 (over y, core).
Axes of the slice: x: 2, y: 2, z: 4, core: 2. Of those that a mesh axis runs over, the one named last changes fastest.
Arguments:
- field: bfloat16 [4, 32, 256, 128], P('ens', 'lat', 'lon'), may hold values from -6 to 6
- cotangent: bfloat16 [4, 32, 256, 128], P('ens', 'lat', 'lon'), may hold values from -6 to 6
- land_mask: int32 [32, 256], P('lat', 'lon'), may hold values from 0 to 1, as said below
- kernel_taps: float32 [49, 128], replicated, may hold values from -0.875 to 0.875
- norm_gain: float32 [128], replicated, may hold values from 0.1 to 1.9
- norm_shift: float32 [128], replicated, may hold values from -3 to 3
- up_weight: bfloat16 [128, 256], replicated, may hold values from -0.5 to 0.5
- down_weight: bfloat16 [256, 128], replicated, may hold values from -0.375 to 0.375
Outputs:
- output: bfloat16 [4, 32, 256, 128], P('ens', 'lat', 'lon')
- field_grad: bfloat16 [4, 32, 256, 128], P('ens', 'lat', 'lon')
- kernel_grad: float32 [49, 128], replicated
- norm_grad: float32 [2, 128], replicated
- up_grad: float32 [128, 256], replicated
- down_grad: float32 [256, 128], replicated
Inputs may be any that keep to these rules, and one draw needn't show every extreme that they name: `land_mask`: 1 marks an ocean cell and 0 a land cell; the share of ocean differs from tile to tile.
All inputs are finite; a program needn't handle non-finite values.
Results may differ from a plain program's by a relative error of at most 0.0062.
Values may be sent and summed in bfloat16 or wider, within the bound.
No kernel may reach another device: no remote copies, remote signals or barrier semaphores. Data moves between devices by JAX's collectives and lax.ppermute only.
A program may use at most 64 MiB of HBM per device.

v0:
```python
import math

import jax
import jax.numpy as jnp
from jax import lax
from jax.sharding import PartitionSpec as P

KERNEL = 7
DILATION = 2
REACH = 6


def partner(shard, axis, bit):
    return lax.ppermute(shard, axis, [(i, i ^ 1 << bit) for i in range(lax.axis_size(axis))])


def extended_2(cells, sides, width, closed):
    for axis, dim in sides:
        count = lax.axis_size(axis)
        ends = count if closed else count - 1
        head = lax.slice_in_dim(cells, 0, width, axis=dim)
        tail = lax.slice_in_dim(cells, cells.shape[dim] - width, cells.shape[dim], axis=dim)
        cells = jnp.concatenate(
            [
                lax.ppermute(tail, axis, [(i, (i + 1) % count) for i in range(ends)]),
                cells,
                lax.ppermute(head, axis, [((i + 1) % count, i) for i in range(ends)]),
            ],
            axis=dim,
        )
    return cells


def shifted(block, axis, distance):
    devices = range(lax.axis_size(axis))
    route = [((i - distance) % len(devices), i) for i in devices]
    return lax.ppermute(block, axis, route)


def passed_along(value, axis, steps):
    count = lax.axis_size(axis)
    leading, last = (max(0, -steps), min(count, count - steps))
    return lax.ppermute(value, axis, [(source, source + steps) for source in range(leading, last)])


def depthwise(widened, kernel_taps, rows, cols):
    total = jnp.zeros((rows, cols, widened.shape[2]), jnp.float32)
    for row_tap in range(KERNEL):
        for col_tap in range(KERNEL):
            window = widened[
                DILATION * row_tap : DILATION * row_tap + rows,
                DILATION * col_tap : DILATION * col_tap + cols,
            ]
            total = total + kernel_taps[row_tap * KERNEL + col_tap] * window
    return total


def fold_forward(strip):
    for bit_pos in range(lax.axis_size("lon").bit_length() - 1):
        strip = partner(strip, "lon", bit_pos)
    return strip


def fold_backward(strip):
    for bit_pos in range(lax.axis_size("lon").bit_length() - 1):
        strip = partner(strip.astype(jnp.bfloat16), "lon", bit_pos).astype(strip.dtype)
    return strip


def is_northern():
    return lax.axis_index("lat") == lax.axis_size("lat") - 1


def extend_rows(block):
    padded = extended_2(block, (("lat", 0),), REACH, False)
    height = block.shape[0]
    folded = fold_forward(block[height - REACH :][::-1, ::-1])
    upper = jnp.where(is_northern(), folded, padded[height + REACH :])
    return jnp.concatenate([padded[: height + REACH], upper], 0)


def extend_cols(block):
    return extended_2(block, (("lon", 1),), REACH, True)


def retract_cols(grads):
    width = grads.shape[1] - 2 * REACH
    own = grads[:, REACH : REACH + width]
    from_east = shifted(grads[:, :REACH].astype(jnp.bfloat16), "lon", -1).astype(jnp.float32)
    from_west = shifted(grads[:, REACH + width :].astype(jnp.bfloat16), "lon", 1).astype(
        jnp.float32
    )
    own = own.at[:, width - REACH :].add(from_east)
    return own.at[:, :REACH].add(from_west)


def retract_rows(grads):
    height = grads.shape[0] - 2 * REACH
    own = grads[REACH : REACH + height]
    upper = grads[REACH + height :]
    from_north = passed_along(grads[:REACH].astype(jnp.bfloat16), "lat", -1).astype(jnp.float32)
    from_south = passed_along(upper.astype(jnp.bfloat16), "lat", 1).astype(upper.dtype)
    folded = fold_backward(upper[::-1, ::-1])
    own = own.at[height - REACH :].add(from_north + jnp.where(is_northern(), folded, 0.0))
    return own.at[:REACH].add(from_south)


def shards(field, cotangent, land_mask, kernel_taps, norm_gain, norm_shift, up_weight, down_weight):
    state = field[0]
    upstream_in = cotangent[0]
    rows, cols, channels = state.shape
    sea = land_mask.astype(jnp.float32)[:, :, None]
    masked = (state.astype(jnp.float32) * sea).astype(jnp.bfloat16)
    extended = extend_cols(extend_rows(masked))
    widened = extended.astype(jnp.float32)
    mixed = depthwise(widened, kernel_taps, rows, cols)
    centered = mixed - jnp.mean(mixed, -1, keepdims=True)
    rstd = lax.rsqrt(jnp.mean(centered * centered, -1, keepdims=True) + 1e-06)
    unit = centered * rstd
    normed = (unit * norm_gain + norm_shift).astype(jnp.bfloat16)
    cells = rows * cols
    flat_norm = normed.reshape(cells, channels)
    pre = jnp.dot(flat_norm, up_weight, preferred_element_type=jnp.float32)
    slope = math.sqrt(2.0 / math.pi)
    tanh_val = jnp.tanh(slope * (pre + 0.044715 * pre * pre * pre))
    activated = (0.5 * pre * (1.0 + tanh_val)).astype(jnp.bfloat16)
    product = jnp.dot(activated, down_weight, preferred_element_type=jnp.float32).reshape(
        rows, cols, channels
    )
    output = ((state.astype(jnp.float32) + product) * sea).astype(jnp.bfloat16)
    upstream = (upstream_in.astype(jnp.float32) * sea).astype(jnp.bfloat16)
    flat_up = upstream.reshape(cells, channels)
    down_part = jnp.dot(activated.T, flat_up, preferred_element_type=jnp.float32)
    act_grad = jnp.dot(flat_up, down_weight.T, preferred_element_type=jnp.float32)
    deriv = 0.5 * (1.0 + tanh_val) + 0.5 * pre * (1.0 - tanh_val * tanh_val) * slope * (
        1.0 + 3.0 * 0.044715 * pre * pre
    )
    pre_grad = (act_grad * deriv).astype(jnp.bfloat16)
    up_part = jnp.dot(flat_norm.T, pre_grad, preferred_element_type=jnp.float32)
    norm_in_grad = jnp.dot(pre_grad, up_weight.T, preferred_element_type=jnp.float32).reshape(
        rows, cols, channels
    )
    norm_part = jnp.stack([jnp.sum(norm_in_grad * unit, (0, 1)), jnp.sum(norm_in_grad, (0, 1))])
    count = cells * lax.axis_size("lon") * lax.axis_size("lat") * lax.axis_size("ens")
    factor = 1.0 / math.sqrt(count)
    scaled = norm_in_grad * norm_gain
    mixed_grad = rstd * (
        scaled
        - jnp.mean(scaled, -1, keepdims=True)
        - unit * jnp.mean(scaled * unit, -1, keepdims=True)
    )
    kernel_rows = []
    for row_tap in range(KERNEL):
        for col_tap in range(KERNEL):
            window = widened[
                DILATION * row_tap : DILATION * row_tap + rows,
                DILATION * col_tap : DILATION * col_tap + cols,
            ]
            kernel_rows.append(jnp.sum(window * mixed_grad, (0, 1)))
    kernel_part = jnp.stack(kernel_rows)
    margin = 2 * REACH
    spread_grad = jnp.pad(mixed_grad, ((margin, margin), (margin, margin), (0, 0)))
    extended_grad = jnp.zeros((rows + margin, cols + margin, channels), jnp.float32)
    for row_tap in range(KERNEL):
        for col_tap in range(KERNEL):
            row_start = margin - DILATION * row_tap
            col_start = margin - DILATION * col_tap
            window = spread_grad[
                row_start : row_start + rows + margin, col_start : col_start + cols + margin
            ]
            extended_grad = extended_grad + kernel_taps[row_tap * KERNEL + col_tap] * window
    masked_grad = retract_rows(retract_cols(extended_grad))
    field_grad = ((upstream_in.astype(jnp.float32) + masked_grad) * sea).astype(jnp.bfloat16)
    kernel_sum, norm_sum, up_sum, down_sum = lax.psum(
        (kernel_part, norm_part, up_part, down_part), ("lon", "lat", "ens")
    )
    return (
        output[None],
        field_grad[None],
        kernel_sum * factor,
        norm_sum * factor,
        up_sum * factor,
        down_sum * factor,
    )


def solution(mesh):
    in_specs = (
        P("ens", "lat", "lon", None),
        P("ens", "lat", "lon", None),
        P("lat", "lon"),
        P(),
        P(),
        P(),
        P(),
        P(),
    )
    out_specs = (P("ens", "lat", "lon", None), P("ens", "lat", "lon", None), P(), P(), P(), P())
    return jax.shard_map(shards, mesh=mesh, in_specs=in_specs, out_specs=out_specs, check_vma=False)
```

profile of v0, /device:TPU:0, one launch (start us, length us, event | category | flops | bytes accessed | tf_op | source)
XLA Modules:
  0.0 243.0 jit_solution(2984634854696554243)
XLA Ops:
  7.3 0.8 convert_element_type.83
  8.0 1.1 fusion.106
  9.2 4.8 %collective-permute-start = (bf16[6,64,128]{2,1,0:T(8,128)(2,1)S(1)}, bf16[6,64,128]{2,1,0:T(8,128)(2,1)S(1)}, u32[]{:S(2)}, u32[]{:S(2)}) collective-permute-start(bf16[6,64,128]{2,1,0:T(8,128)(2,1)S(1)} %get-tuple-element.124), channel_id=1, source_target_pairs={{0,4},{1,5},{2,6},{3,7},{8,12},{9,13},{10,14},{11,15},{16,20},{17,... | collective-permute-start | bytes 294920 | tf_op jit(solution)/shard_map/ppermute | solution.py:25
  14.1 1.6 collective-permute-start.1
  15.7 1.3 collective-permute-start.3
  17.1 0.2 fusion.107
  17.3 1.4 collective-permute-done.1
  18.8 2.6 %collective-permute-start.2 = (bf16[6,64,128]{2,1,0:T(8,128)(2,1)S(1)}, bf16[6,64,128]{2,1,0:T(8,128)(2,1)S(1)}, u32[]{:S(2)}, u32[]{:S(2)}) collective-permute-start(bf16[6,64,128]{2,1,0:T(8,128)(2,1)S(1)} %collective-permute-done.1), channel_id=1, source_target_pairs={{0,16},{8,24},{16,0},{24,8},{1,17},{9,25},{17,1},{25,9},{2,18},{10... | collective-permute-start | bytes 294920 | tf_op jit(solution)/shard_map/ppermute | solution.py:14
  21.4 0.9 collective-permute-done.3
  22.2 2.1 collective-permute-done.2
  24.4 2.4 collective-permute-start.4
  26.7 3.0 %collective-permute-start.5 = (bf16[28,6,128]{2,1,0:T(8,128)(2,1)S(1)}, bf16[28,6,128]{2,1,0:T(8,128)(2,1)S(1)}, u32[]{:S(2)}, u32[]{:S(2)}) collective-permute-start(bf16[28,6,128]{2,1,0:T(8,128)(2,1)S(1)} %get-tuple-element.122), channel_id=1, source_target_pairs={{8,0},{16,8},{24,16},{0,24},{9,1},{17,9},{25,17},{1,25},{10,2},{18... | collective-permute-start | bytes 129032 | tf_op jit(solution)/shard_map/ppermute | solution.py:27
  29.7 2.1 collective-permute-done.4
  31.8 0.2 maximum_convert_fusion
  32.0 3.9 %fusion.116 = (f32[16,64]{1,0:T(8,128)S(1)}, f32[16,64,128]{2,1,0:T(8,128)S(1)}) fusion(f32[28,76,128]{2,1,0:T(8,128)S(1)} %maximum_convert_fusion, f32[128]{0:T(128)S(1)} %get-tuple-element.172, f32[128]{0:T(128)S(1)} %get-tuple-element.173, f32[128]{0:T(128)S(1)} %get-tuple-element.126, f32[128]{0:T(128)S(1)} %get-tuple-element.127, ...), kind=kLoop, calls=%fused_computation.298 | loop fusion | flops 12844032 | bytes 26243584 | tf_op jit(solution)/shard_map/reduce_sum | solution.py:117
  36.0 0.4 multiply_reduce_fusion.52
  36.4 0.3 add_convert_fusion
  36.8 0.5 multiply_convert_fusion
  37.3 1.0 fusion.122
  38.3 0.3 fusion.120
  38.6 0.8 fusion
  39.3 0.9 fusion.121
  40.3 0.4 fusion.113
  40.7 0.5 multiply_reduce_fusion
  41.3 1.5 multiply_reduce_fusion.1
  42.8 0.7 multiply_reduce_fusion.37
  43.4 0.9 multiply_reduce_fusion.19
  44.3 10.4 %fusion.114 = (bf16[28,76,128]{2,1,0:T(8,128)(2,1)S(1)}, f32[28,76,128]{2,1,0:T(8,128)S(1)}) fusion(f32[128]{0:T(128)S(1)} %get-tuple-element.172, f32[128]{0:T(128)S(1)} %get-tuple-element.173, f32[128]{0:T(128)S(1)} %get-tuple-element.126, f32[128]{0:T(128)S(1)} %get-tuple-element.127, f32[128]{0:T(128)S(1)} %get-tuple-element.128, ...), kind=kLoop, calls=%fused_computation.297 | loop fusion | flops 26693632 | bytes 2183680 | tf_op jit(solution)/shard_map/convert.5
  54.8 0.9 fusion.104
  55.7 0.1 stack.208
  55.8 40.0 %all-reduce.1 = (f32[49,128]{1,0:T(8,128)S(1)}, f32[2,128]{1,0:T(2,128)S(1)}) all-reduce(f32[49,128]{1,0:T(8,128)S(1)} %stack.208, f32[2,128]{1,0:T(2,128)S(1)} %pad_maximum_fusion.3), channel_id=1, replica_groups=mesh['lon'=4,'lat'=2,'ens'=4] {'lon','lat','ens'}, use_global_device_ids=true, to_apply=%region_53.54 | all-reduce | flops 6528 | bytes 52224 | tf_op jit(solution)/shard_map/psum | solution.py:174
  95.8 0.6 broadcast_multiply_fusion.2
  96.4 2.2 collective-permute-start.6
  98.7 0.6 broadcast_multiply_fusion.6
  99.2 0.1 slice.883
  99.4 1.4 collective-permute-done.6
  100.8 0.2 scatter-add.14
  101.0 4.5 %collective-permute-done.7 = bf16[28,6,128]{2,1,0:T(8,128)(2,1)S(1)} collective-permute-done((bf16[28,6,128]{2,1,0:T(8,128)(2,1)S(1)}, bf16[28,6,128]{2,1,0:T(8,128)(2,1)S(1)}, u32[]{:S(2)}, u32[]{:S(2)}) %collective-permute-start.7) | collective-permute-done | bytes 43040 | tf_op jit(solution)/shard_map/ppermute | solution.py:37
  105.5 0.2 scatter-add.15
  105.9 0.1 collective-permute-start.9
  106.0 4.2 %collective-permute-start.11 = (bf16[6,64,128]{2,1,0:T(8,128)(2,1)S(1)}, bf16[6,64,128]{2,1,0:T(8,128)(2,1)S(1)}, u32[]{:S(2)}, u32[]{:S(2)}) collective-permute-start(bf16[6,64,128]{2,1,0:T(8,128)(2,1)S(1)} %get-tuple-element.116), channel_id=1, source_target_pairs={{0,4},{1,5},{2,6},{3,7},{8,12},{9,13},{10,14},{11,15},{16,20},{17,... | collective-permute-start | bytes 294920 | tf_op jit(solution)/shard_map/ppermute | solution.py:43
  110.2 1.3 collective-permute-start.8
  111.5 115.5 %all-reduce.5.cloned.1.call-done = (f32[128,256]{1,0:T(8,128)}, f32[256,128]{1,0:T(8,128)}) async-done(((f32[128,256]{1,0:T(8,128)}, f32[256,128]{1,0:T(8,128)}), (f32[128,256]{1,0:T(8,128)}, f32[256,128]{1,0:T(8,128)})) %all-reduce.5.cloned.1.call-update) | async-done | bytes 262160 | tf_op jit(solution)/shard_map/psum | solution.py:174
  227.0 1.6 broadcast_multiply_fusion.1
  228.5 1.4 collective-permute-start.10
  230.0 1.6 broadcast_multiply_fusion
  231.5 3.6 %collective-permute-done.10 = bf16[6,64,128]{2,1,0:T(8,128)(2,1)S(1)} collective-permute-done((bf16[6,64,128]{2,1,0:T(8,128)(2,1)S(1)}, bf16[6,64,128]{2,1,0:T(8,128)(2,1)S(1)}, u32[]{:S(2)}, u32[]{:S(2)}) %collective-permute-start.10) | collective-permute-done | bytes 98336 | tf_op jit(solution)/shard_map/ppermute | solution.py:14
  235.2 0.9 fusion.110
  (46 shorter events, 0.7 us)
Async XLA Ops:
  7.2 29.6 %copy-start = (bf16[128,256]{1,0:T(8,128)(2,1)S(1)}, bf16[128,256]{1,0:T(8,128)(2,1)}, u32[]{:S(2)}) copy-start(bf16[128,256]{1,0:T(8,128)(2,1)} %param.22) | copy-start | bytes 196612
  7.2 9.9 %copy-start.2 = (bf16[1,16,64,128]{3,2,1,0:T(8,128)(2,1)S(1)}, bf16[1,16,64,128]{3,2,1,0:T(8,128)(2,1)}, u32[]{:S(2)}) copy-start(bf16[1,16,64,128]{3,2,1,0:T(8,128)(2,1)} %param.17) | copy-start | bytes 786436
  7.2 10.1 %copy-start.5 = (f32[49,128]{1,0:T(8,128)S(1)}, f32[49,128]{1,0:T(8,128)}, u32[]{:S(2)}) copy-start(f32[49,128]{1,0:T(8,128)} %param.19) | copy-start | bytes 75268
  7.2 219.8 %all-reduce.5.cloned.1.call-start = ((), (), s32[]{:S(2)}) async-start(), calls=%async_computation | async-start | bytes 524288 | tf_op jit(solution)/shard_map/psum | solution.py:174
  9.2 15.1 %collective-permute-start = (bf16[6,64,128]{2,1,0:T(8,128)(2,1)S(1)}, bf16[6,64,128]{2,1,0:T(8,128)(2,1)S(1)}, u32[]{:S(2)}, u32[]{:S(2)}) collective-permute-start(bf16[6,64,128]{2,1,0:T(8,128)(2,1)S(1)} %get-tuple-element.124), channel_id=1, source_target_pairs={{0,4},{1,5},{2,6},{3,7},{8,12},{9,13},{10,14},{11,15},{16,20},{17,... | collective-permute-start | bytes 294920 | tf_op jit(solution)/shard_map/ppermute | solution.py:25
  14.1 4.7 %collective-permute-start.1 = (bf16[6,64,128]{2,1,0:T(8,128)(2,1)S(1)}, bf16[6,64,128]{2,1,0:T(8,128)(2,1)S(1)}, u32[]{:S(2)}, u32[]{:S(2)}) collective-permute-start(bf16[6,64,128]{2,1,0:T(8,128)(2,1)S(1)} %rev.6), channel_id=1, source_target_pairs={{0,8},{8,0},{16,24},{24,16},{1,9},{9,1},{17,25},{25,17},{2,10},{10... | collective-permute-start | bytes 294920 | tf_op jit(solution)/shard_map/ppermute | solution.py:14
  15.7 6.5 %collective-permute-start.3 = (bf16[6,64,128]{2,1,0:T(8,128)(2,1)S(1)}, bf16[6,64,128]{2,1,0:T(8,128)(2,1)S(1)}, u32[]{:S(2)}, u32[]{:S(2)}) collective-permute-start(bf16[6,64,128]{2,1,0:T(8,128)(2,1)S(1)} %get-tuple-element.123), channel_id=1, source_target_pairs={{4,0},{5,1},{6,2},{7,3},{12,8},{13,9},{14,10},{15,11},{20,16},{21,... | collective-permute-start | bytes 294920 | tf_op jit(solution)/shard_map/ppermute | solution.py:27
  18.8 5.5 %collective-permute-start.2 = (bf16[6,64,128]{2,1,0:T(8,128)(2,1)S(1)}, bf16[6,64,128]{2,1,0:T(8,128)(2,1)S(1)}, u32[]{:S(2)}, u32[]{:S(2)}) collective-permute-start(bf16[6,64,128]{2,1,0:T(8,128)(2,1)S(1)} %collective-permute-done.1), channel_id=1, source_target_pairs={{0,16},{8,24},{16,0},{24,8},{1,17},{9,25},{17,1},{25,9},{2,18},{10... | collective-permute-start | bytes 294920 | tf_op jit(solution)/shard_map/ppermute | solution.py:14
  24.4 7.5 %collective-permute-start.4 = (bf16[28,6,128]{2,1,0:T(8,128)(2,1)S(1)}, bf16[28,6,128]{2,1,0:T(8,128)(2,1)S(1)}, u32[]{:S(2)}, u32[]{:S(2)}) collective-permute-start(bf16[28,6,128]{2,1,0:T(8,128)(2,1)S(1)} %get-tuple-element.121), channel_id=1, source_target_pairs={{0,8},{8,16},{16,24},{24,0},{1,9},{9,17},{17,25},{25,1},{2,10},{10... | collective-permute-start | bytes 129032 | tf_op jit(solution)/shard_map/ppermute | solution.py:25
  26.7 5.1 %collective-permute-start.5 = (bf16[28,6,128]{2,1,0:T(8,128)(2,1)S(1)}, bf16[28,6,128]{2,1,0:T(8,128)(2,1)S(1)}, u32[]{:S(2)}, u32[]{:S(2)}) collective-permute-start(bf16[28,6,128]{2,1,0:T(8,128)(2,1)S(1)} %get-tuple-element.122), channel_id=1, source_target_pairs={{8,0},{16,8},{24,16},{0,24},{9,1},{17,9},{25,17},{1,25},{10,2},{18... | collective-permute-start | bytes 129032 | tf_op jit(solution)/shard_map/ppermute | solution.py:27
  32.0 4.4 %copy-start.6 = (f32[128]{0:T(128)S(1)}, f32[128]{0:T(128)}, u32[]{:S(2)}) copy-start(f32[128]{0:T(128)} %param.20) | copy-start | bytes 1540
  32.0 4.4 %copy-start.7 = (f32[128]{0:T(128)S(1)}, f32[128]{0:T(128)}, u32[]{:S(2)}) copy-start(f32[128]{0:T(128)} %param.21) | copy-start | bytes 1540
  36.8 1.5 copy-start.4
  44.3 10.5 %copy-start.1 = (bf16[1,16,64,128]{3,2,1,0:T(8,128)(2,1)S(1)}, bf16[1,16,64,128]{3,2,1,0:T(8,128)(2,1)}, u32[]{:S(2)}) copy-start(bf16[1,16,64,128]{3,2,1,0:T(8,128)(2,1)} %param.16) | copy-start | bytes 786436
  96.4 4.3 %collective-permute-start.6 = (bf16[28,6,128]{2,1,0:T(8,128)(2,1)S(1)}, bf16[28,6,128]{2,1,0:T(8,128)(2,1)S(1)}, u32[]{:S(2)}, u32[]{:S(2)}) collective-permute-start(bf16[28,6,128]{2,1,0:T(8,128)(2,1)S(1)} %get-tuple-element.120), channel_id=1, source_target_pairs={{8,0},{16,8},{24,16},{0,24},{9,1},{17,9},{25,17},{1,25},{10,2},{18... | collective-permute-start | bytes 129032 | tf_op jit(solution)/shard_map/ppermute | solution.py:37
  99.2 6.3 %collective-permute-start.7 = (bf16[28,6,128]{2,1,0:T(8,128)(2,1)S(1)}, bf16[28,6,128]{2,1,0:T(8,128)(2,1)S(1)}, u32[]{:S(2)}, u32[]{:S(2)}) collective-permute-start(bf16[28,6,128]{2,1,0:T(8,128)(2,1)S(1)} %get-tuple-element.119), channel_id=1, source_target_pairs={{24,0},{0,8},{8,16},{16,24},{25,1},{1,9},{9,17},{17,25},{26,2},{2,... | collective-permute-start | bytes 129032 | tf_op jit(solution)/shard_map/ppermute | solution.py:37
  105.8 129.4 %copy-start.3 = (bf16[1,16,64,128]{3,2,1,0:T(8,128)(2,1)S(1)}, bf16[1,16,64,128]{3,2,1,0:T(8,128)(2,1)}, u32[]{:S(2)}) copy-start(bf16[1,16,64,128]{3,2,1,0:T(8,128)(2,1)} %param.17) | copy-start | bytes 786436
  105.9 122.6 %collective-permute-start.9 = (bf16[6,64,128]{2,1,0:T(8,128)(2,1)S(1)}, bf16[6,64,128]{2,1,0:T(8,128)(2,1)S(1)}, u32[]{:S(2)}, u32[]{:S(2)}) collective-permute-start(bf16[6,64,128]{2,1,0:T(8,128)(2,1)S(1)} %rev.7), channel_id=1, source_target_pairs={{0,8},{8,0},{16,24},{24,16},{1,9},{9,1},{17,25},{25,17},{2,10},{10... | collective-permute-start | bytes 294920 | tf_op jit(solution)/shard_map/ppermute | solution.py:14
  106.0 129.2 %collective-permute-start.11 = (bf16[6,64,128]{2,1,0:T(8,128)(2,1)S(1)}, bf16[6,64,128]{2,1,0:T(8,128)(2,1)S(1)}, u32[]{:S(2)}, u32[]{:S(2)}) collective-permute-start(bf16[6,64,128]{2,1,0:T(8,128)(2,1)S(1)} %get-tuple-element.116), channel_id=1, source_target_pairs={{0,4},{1,5},{2,6},{3,7},{8,12},{9,13},{10,14},{11,15},{16,20},{17,... | collective-permute-start | bytes 294920 | tf_op jit(solution)/shard_map/ppermute | solution.py:43
  110.2 121.3 %collective-permute-start.8 = (bf16[6,64,128]{2,1,0:T(8,128)(2,1)S(1)}, bf16[6,64,128]{2,1,0:T(8,128)(2,1)S(1)}, u32[]{:S(2)}, u32[]{:S(2)}) collective-permute-start(bf16[6,64,128]{2,1,0:T(8,128)(2,1)S(1)} %get-tuple-element.118), channel_id=1, source_target_pairs={{4,0},{5,1},{6,2},{7,3},{12,8},{13,9},{14,10},{15,11},{20,16},{21,... | collective-permute-start | bytes 294920 | tf_op jit(solution)/shard_map/ppermute | solution.py:43
  228.5 6.6 %collective-permute-start.10 = (bf16[6,64,128]{2,1,0:T(8,128)(2,1)S(1)}, bf16[6,64,128]{2,1,0:T(8,128)(2,1)S(1)}, u32[]{:S(2)}, u32[]{:S(2)}) collective-permute-start(bf16[6,64,128]{2,1,0:T(8,128)(2,1)S(1)} %collective-permute-done.9), channel_id=1, source_target_pairs={{0,16},{8,24},{16,0},{24,8},{1,17},{9,25},{17,1},{25,9},{2,18},{10... | collective-permute-start | bytes 294920 | tf_op jit(solution)/shard_map/ppermute | solution.py:14
Sparse Core Ops, SparseCore 0:
  99.5 127.4 all-reduce.4
where the time goes:
time: 243 us
  waiting for transfers between devices  131 us (54%)
  blocking collectives  40 us (16%)
  other arithmetic  27.3 us (11%)
  starting transfers between devices  25 us (10%)
  between operations  14.4 us (6%)
  matrix products  3.84 us (2%)
    psum x1, waiting for transfers between devices, shards(): lax.psum((kernel_part, norm_part, up_part, down_part), ('lon', 'lat', 'en...  115 us
    psum x1, blocking collectives, shards(): lax.psum((kernel_part, norm_part, up_part, down_part), ('lon', 'lat', 'en...  40 us
    another operation x1, other arithmetic  10.4 us
    ppermute x2, starting transfers between devices, extended_2(): lax.ppermute(tail, axis, [(i, (i + 1) % count) for i in range(ends)])  7.23 us
    ppermute x4, waiting for transfers between devices, partner(): lax.ppermute(shard, axis, [(i, i ^ 1 << bit) for i in range(lax.axis_size...  7.09 us
    ppermute x2, waiting for transfers between devices, shifted(): return lax.ppermute(block, axis, route)  5.93 us
    ppermute x4, starting transfers between devices, partner(): lax.ppermute(shard, axis, [(i, i ^ 1 << bit) for i in range(lax.axis_size...  5.72 us
    ppermute x2, starting transfers between devices, passed_along(): lax.ppermute(value, axis, [(source, source + steps) for source in range(l...  5.49 us
  transfers between devices with their start and end apart: 13, of which 8 were waited for; matrix products, arithmetic and copies ran while one was open for 2% of the time, Pallas kernels for 0%

commit v1 on v0

v1 whole, which is shorter than its diff:
```python
import functools
import math

import jax
import jax.numpy as jnp
from jax import lax
from jax.experimental import pallas as pl
from jax.experimental.pallas import tpu as pltpu
from jax.sharding import PartitionSpec as P

KERNEL = 7
DILATION = 2
REACH = 6
TAPS = KERNEL * KERNEL
LANE = 8
LEFT = 8
BASE = LEFT - REACH
SLOPE = math.sqrt(2.0 / math.pi)
CUBIC = 0.044715
F32, BF16 = jnp.float32, jnp.bfloat16


def route(axes, target):
    sizes = [lax.axis_size(a) for a in axes]
    pairs = []
    for flat in range(math.prod(sizes)):
        rest, at = flat, []
        for size in reversed(sizes):
            at.append(rest % size)
            rest //= size
        at = at[::-1]
        to = target(*at)
        if to is not None:
            dest = 0
            for size, i in zip(sizes, to):
                dest = dest * size + i
            pairs.append((flat, dest))
    return pairs


def is_northern():
    return lax.axis_index("lat") == lax.axis_size("lat") - 1


def row_halos(block):
    count, width = lax.axis_size("lat"), lax.axis_size("lon")
    top, bottom = block[block.shape[0] - REACH :], block[:REACH]
    northern = is_northern()
    axes = ("lon", "lat")
    fold = route(axes, lambda c, r: (width - 1 - c, r) if r == count - 1 else None)
    folded = lax.ppermute(top[::-1, ::-1], axes, fold)
    if count == 2:
        facing = lax.ppermute(jnp.where(northern, bottom, top), "lat", [(0, 1), (1, 0)])
        south = jnp.where(northern, facing, jnp.zeros_like(facing))
        north = jnp.where(northern, folded, facing)
    else:
        south = lax.ppermute(top, "lat", [(i, i + 1) for i in range(count - 1)])
        above = lax.ppermute(bottom, "lat", [(i + 1, i) for i in range(count - 1)])
        north = jnp.where(northern, folded, above)
    return south, north


def extend(block):
    south, north = row_halos(block)
    cols = block.shape[1]
    count = lax.axis_size("lon")
    first = jnp.concatenate([a[:, :REACH] for a in (south, block, north)], 0)
    last = jnp.concatenate([a[:, cols - REACH :] for a in (south, block, north)], 0)
    west = lax.ppermute(last, "lon", [(i, (i + 1) % count) for i in range(count)])
    east = lax.ppermute(first, "lon", [((i + 1) % count, i) for i in range(count)])
    return south, block, north, west, east


def partners(value, bits):
    axes = tuple(a for a in ("lon", "lat", "ens") if a in [b[0] for b in bits])
    flip = {a: 0 for a in axes}
    for a, b in bits:
        flip[a] ^= b
    return lax.ppermute(value, axes, route(axes, lambda *at: [i ^ flip[a] for a, i in zip(axes, at)]))


def summed(packed):
    axes = ("ens", "lat", "lon")
    bits = [(a, 1 << b) for a in axes for b in range(lax.axis_size(a).bit_length() - 1)]
    if any(lax.axis_size(a) & (lax.axis_size(a) - 1) for a in axes):
        return lax.psum(packed.astype(F32), axes)
    half = packed.shape[0] // 2
    split = bits[0]
    odd = lax.axis_index(split[0]) & 1
    low, high = packed[:half], packed[half:]
    mine = jnp.where(odd == 0, low, high)
    other = jnp.where(odd == 0, high, low)
    total = mine.astype(F32) + partners(other, [split]).astype(F32)
    rest = bits[1:]
    while rest:
        pair, rest = rest[:2], rest[2:]
        sent = total.astype(BF16)
        if len(pair) == 2:
            far = partners(sent, pair)
            one, two = partners(sent, pair[:1]), partners(sent, pair[1:])
            total = (sent.astype(F32) + one.astype(F32)) + (two.astype(F32) + far.astype(F32))
        else:
            total = sent.astype(F32) + partners(sent, pair).astype(F32)
    back = partners(total, [split])
    return jnp.where(odd == 0, jnp.concatenate([total, back]), jnp.concatenate([back, total]))


def fill(wide, south, block, north, west, east):
    rows, cols = block.shape[0], block.shape[1]
    for ref, start, count in ((south, 0, REACH), (block, REACH, rows), (north, REACH + rows, REACH)):

        def one(r, carry, ref=ref, start=start):
            wide[start + r, LEFT : LEFT + cols] = ref[r].astype(F32)
            return carry

        lax.fori_loop(0, count, one, 0, unroll=2)

    def sides(r, carry):
        wide[r, BASE:LEFT] = west[r].astype(F32)
        wide[r, LEFT + cols : LEFT + cols + REACH] = east[r].astype(F32)
        return carry

    lax.fori_loop(0, rows + 2 * REACH, sides, 0, unroll=4)


def conv(wide, tap, rows, cols, store):
    lines = rows // 2
    groups = math.gcd(cols // LANE, 4)

    def parity(q, carry):
        for first in range(0, cols // LANE, groups):
            sums = [[None] * groups for _ in range(lines)]
            for k in range(lines + KERNEL - 1):
                for j in range(KERNEL):
                    at = [BASE + (first + g) * LANE + DILATION * j for g in range(groups)]
                    values = [wide[q + 2 * k, a : a + LANE] for a in at]
                    for i in range(KERNEL):
                        line = k - i
                        if 0 <= line < lines:
                            weight = tap(k, i, j)
                            for g in range(groups):
                                term = weight * values[g]
                                old = sums[line][g]
                                sums[line][g] = term if old is None else old + term
            for line in range(lines):
                for g in range(groups):
                    store(q + 2 * line, (first + g) * LANE, sums[line][g])
        return carry

    lax.fori_loop(0, 2, parity, 0)


def forward_kernel(south, block, north, west, east, upstream, sea, taps, gain, shift, up, down,
                   output, grad, packed, wide, spread, mixed):
    rows, cols, channels = block.shape
    hidden = up.shape[1]
    for k in range(TAPS):
        spread[k] = jnp.broadcast_to(taps[k : k + 1], (LANE, channels))
    fill(wide, south, block, north, west, east)

    def store(row, col, value):
        mixed[row, col : col + LANE] = value

    conv(wide, lambda k, i, j: spread[i * KERNEL + j], rows, cols, store)

    up_w, down_w = up[...], down[...]
    gain_v, shift_v = gain[...], shift[...]
    lines = 4
    cells = lines * cols
    nt = (((1,), (1,)), ((), ()))
    tn = (((0,), (0,)), ((), ()))

    def chunk(n, carry):
        up_sum, down_sum, gain_sum, shift_sum = carry
        at = pl.ds(n * lines, lines)
        value = mixed[at].reshape(cells, channels)
        centered = value - jnp.mean(value, -1, keepdims=True)
        rstd = lax.rsqrt(jnp.mean(centered * centered, -1, keepdims=True) + 1e-06)
        unit = centered * rstd
        normed = (unit * gain_v + shift_v).astype(BF16)
        pre = jnp.dot(normed, up_w, preferred_element_type=F32)
        square = pre * pre
        tanh = jnp.tanh(pre * (SLOPE + (SLOPE * CUBIC) * square))
        gate = 0.5 + 0.5 * tanh
        activated = (pre * gate).astype(BF16)
        product = jnp.dot(activated, down_w, preferred_element_type=F32)
        ocean = sea[at].reshape(cells, channels).astype(F32)
        state = block[at].reshape(cells, channels).astype(F32)
        output[at] = ((state + product) * ocean).astype(BF16).reshape(lines, cols, channels)
        above = upstream[at].reshape(cells, channels)
        down_sum = down_sum + lax.dot_general(above, activated, tn, preferred_element_type=F32)
        act_grad = lax.dot_general(above, down_w, nt, preferred_element_type=F32)
        deriv = gate + pre * (gate * (1.0 - tanh)) * (SLOPE + (3.0 * SLOPE * CUBIC) * square)
        pre_grad = (act_grad * deriv).astype(BF16)
        up_sum = up_sum + lax.dot_general(normed, pre_grad, tn, preferred_element_type=F32)
        norm_in = lax.dot_general(pre_grad, up_w, nt, preferred_element_type=F32)
        gain_sum = gain_sum + jnp.sum((norm_in * unit).reshape(cells // LANE, LANE, channels), 0)
        shift_sum = shift_sum + jnp.sum(norm_in.reshape(cells // LANE, LANE, channels), 0)
        scaled = norm_in * gain_v
        inner = jnp.mean(scaled * unit, -1, keepdims=True)
        result = rstd * (scaled - jnp.mean(scaled, -1, keepdims=True) - unit * inner)
        mixed[at] = result.reshape(lines, cols, channels)
        grad[at] = result.astype(BF16).reshape(lines, cols, channels)
        return up_sum, down_sum, gain_sum, shift_sum

    big = jnp.zeros((channels, hidden), F32)
    small = jnp.zeros((LANE, channels), F32)
    up_sum, down_sum, gain_sum, shift_sum = lax.fori_loop(
        0, rows // lines, chunk, (big, big, small, small)
    )
    packed[0:hidden] = down_sum.T.astype(BF16)
    for n in range(hidden // channels):
        start = hidden + n * channels
        packed[start : start + channels] = up_sum[:, n * channels : (n + 1) * channels].astype(BF16)

    pieces = []
    for taps_i in (range(0, 4), range(4, KERNEL)):

        def quad(n, sums, taps_i=taps_i):
            base = (n // 2) * 8 + n % 2
            sums = list(sums)
            for g in range(cols // LANE):
                grads = [mixed[base + 2 * m, g * LANE : (g + 1) * LANE] for m in range(4)]
                for k in range(taps_i[0], taps_i[-1] + 4):
                    for j in range(KERNEL):
                        a = BASE + g * LANE + DILATION * j
                        value = wide[base + 2 * k, a : a + LANE]
                        for m in range(4):
                            if k - m in taps_i:
                                at = (k - m - taps_i[0]) * KERNEL + j
                                sums[at] = sums[at] + grads[m] * value
            return tuple(sums)

        zero = tuple(small for _ in range(len(taps_i) * KERNEL))
        pieces += list(lax.fori_loop(0, rows // 4, quad, zero))
    pieces += [gain_sum, shift_sum]
    pieces = [jnp.sum(p, 0, keepdims=True) for p in pieces]
    pieces += [jnp.zeros((packed.shape[0] - 2 * hidden - len(pieces), channels), F32)]
    packed[2 * hidden :] = jnp.concatenate(pieces, 0).astype(BF16)


def backward_kernel(northern, south, block, north, west, east, upstream, sea, taps,
                    field_grad, wide, spread, folded):
    rows, cols, channels = block.shape
    for k in range(TAPS):
        flipped = jnp.broadcast_to(taps[TAPS - 1 - k : TAPS - k], (LANE, channels))
        plain = jnp.broadcast_to(taps[k : k + 1], (LANE, channels))
        spread[k] = flipped
        folded[k] = jnp.where(northern[0] == 1, plain, flipped)
    fill(wide, south, block, north, west, east)
    edge = (REACH + rows) // 2

    def tap(k, i, j):
        return (folded if k >= edge else spread)[i * KERNEL + j]

    def store(row, col, value):
        at = (row, slice(col, col + LANE))
        field_grad[at] = ((upstream[at].astype(F32) + value) * sea[at].astype(F32)).astype(BF16)

    conv(wide, tap, rows, cols, store)


def shards(field, cotangent, land_mask, kernel_taps, norm_gain, norm_shift, up_weight, down_weight):
    rows, cols, channels = field.shape[1:]
    hidden = up_weight.shape[1]
    sea = jnp.broadcast_to(land_mask.astype(BF16)[:, :, None], (rows, cols, channels))
    masked = field[0] * sea
    upstream = cotangent[0] * sea
    vmem = pl.BlockSpec(memory_space=pltpu.VMEM)
    smem = pl.BlockSpec(memory_space=pltpu.SMEM)
    wide = pltpu.VMEM((rows + 2 * REACH, cols + 2 * LEFT, channels), F32)
    spread = pltpu.VMEM((TAPS, LANE, channels), F32)
    small = -(-(TAPS + 2) // 64) * 64
    macs = TAPS * rows * cols * channels
    output, grad, packed = pl.pallas_call(
        forward_kernel,
        out_shape=(
            jax.ShapeDtypeStruct((rows, cols, channels), BF16),
            jax.ShapeDtypeStruct((rows, cols, channels), BF16),
            jax.ShapeDtypeStruct((2 * hidden + small, channels), BF16),
        ),
        in_specs=[vmem] * 12,
        out_specs=[vmem] * 3,
        scratch_shapes=[wide, spread, pltpu.VMEM((rows, cols, channels), F32)],
        compiler_params=pltpu.CompilerParams(vmem_limit_bytes=32 * 1024 * 1024),
        cost_estimate=pl.CostEstimate(flops=100 * macs, bytes_accessed=3 << 20, transcendentals=0),
        name="forward",
    )(*extend(masked), upstream, sea, kernel_taps, norm_gain[None], norm_shift[None], up_weight, down_weight)

    northern = is_northern().astype(jnp.int32)[None]
    field_grad = pl.pallas_call(
        backward_kernel,
        out_shape=jax.ShapeDtypeStruct((rows, cols, channels), BF16),
        in_specs=[smem] + [vmem] * 8,
        out_specs=vmem,
        scratch_shapes=[wide, spread, spread],
        compiler_params=pltpu.CompilerParams(vmem_limit_bytes=32 * 1024 * 1024),
        cost_estimate=pl.CostEstimate(flops=40 * macs, bytes_accessed=2 << 20, transcendentals=0),
        name="backward",
    )(northern, *extend(grad), upstream, sea, kernel_taps)

    count = rows * cols * lax.axis_size("lon") * lax.axis_size("lat") * lax.axis_size("ens")
    total = summed(packed) * (1.0 / math.sqrt(count))
    down_grad = total[:hidden]
    up_grad = jnp.concatenate(
        [total[hidden + n * channels : hidden + (n + 1) * channels] for n in range(hidden // channels)], 1
    )
    kernel_grad = total[2 * hidden : 2 * hidden + TAPS]
    norm_grad = total[2 * hidden + TAPS : 2 * hidden + TAPS + 2]
    return output[None], field_grad[None], kernel_grad, norm_grad, up_grad, down_grad


def solution(mesh):
    grid = P("ens", "lat", "lon", None)
    return jax.shard_map(
        shards,
        mesh=mesh,
        in_specs=(grid, grid, P("lat", "lon"), P(), P(), P(), P(), P()),
        out_specs=(grid, grid, P(), P(), P(), P()),
        check_vma=False,
    )
```

time: 243 us -> 62.6 us (0.26)
  waiting for transfers between devices: 131 us -> 13.9 us
  blocking collectives: 40 us -> 0 us
  other arithmetic: 27.3 us -> 2.89 us
  between operations: 14.4 us -> 0.85 us
  Pallas kernels: 0 us -> 11.1 us
  starting transfers between devices: 25 us -> 30.7 us
  matrix products: 3.84 us -> 0 us
    psum x1 -> x0, waiting for transfers between devices: 115 us -> none  [shards(): lax.psum((kernel_part, norm_part, up_part, down_part), ('lon', 'lat', 'en...]
    psum x1 -> x0, blocking collectives: 40 us -> none  [shards(): lax.psum((kernel_part, norm_part, up_part, down_part), ('lon', 'lat', 'en...]
    pallas_call x0 -> x2, Pallas kernels: none -> 11.1 us  [the longest x1 8.22 us: shards(): pl.pallas_call(forward_kernel, out_shape=(jax.ShapeDtypeStruct((rows, col...]
    another operation x2 -> x0, other arithmetic: 10.4 us -> none
    reduce_sum x6 -> x0, other arithmetic: 7.89 us -> none  [the longest x1 3.95 us: shards(): centered = mixed - jnp.mean(mixed, -1, keepdims=True)]
    ppermute x12 -> x16, starting transfers between devices: 24.9 us -> 30.7 us  [the longest x2 15.1 us: row_halos(): lax.ppermute(jnp.where(northern, bottom, top), 'lat', [(0, 1), (1, 0)])]
    dot_general x6 -> x0, matrix products: 3.84 us -> none  [the longest x1 1 us: shards(): jnp.dot(activated.T, flat_up, preferred_element_type=jnp.float32)]
    mul x4 -> x2, other arithmetic: 4.32 us -> 1.26 us  [the longest x1 1.23 us: shards(): upstream = cotangent[0] * sea]
  transfers between devices with their start and end apart: 13 -> 16, of which waited for: 8 -> 9; matrix products, arithmetic and copies ran while one was open for 2% -> 0% of each run, Pallas kernels for 0% -> 5%
where the time goes in v1:
time: 62.6 us; the launch traced here: 62.4 us
  starting transfers between devices  30.7 us (49%)
  waiting for transfers between devices  13.9 us (22%)
  Pallas kernels  11.1 us (18%)
  other arithmetic  2.89 us (5%)
  local copies, waits for them, and re-layouts  2.88 us (5%)
  between operations  0.85 us (1%)
    ppermute x2, starting transfers between devices, row_halos(): lax.ppermute(jnp.where(northern, bottom, top), 'lat', [(0, 1), (1, 0)])  15.1 us
    pallas_call x1, Pallas kernels, shards(): pl.pallas_call(forward_kernel, out_shape=(jax.ShapeDtypeStruct((rows, col...  8.22 us
    ppermute x8, starting transfers between devices, partners(): lax.ppermute(value, axes, route(axes, lambda *at: [i ^ flip[a] for a, i i...  8.15 us
    ppermute x8, waiting for transfers between devices, partners(): lax.ppermute(value, axes, route(axes, lambda *at: [i ^ flip[a] for a, i i...  7.07 us
    ppermute x2, starting transfers between devices, extend(): lax.ppermute(first, 'lon', [((i + 1) % count, i) for i in range(count)])  6.02 us
    pallas_call x1, Pallas kernels, shards(): pl.pallas_call(backward_kernel, out_shape=jax.ShapeDtypeStruct((rows, col...  2.9 us
    ppermute x2, waiting for transfers between devices, row_halos(): lax.ppermute(jnp.where(northern, bottom, top), 'lat', [(0, 1), (1, 0)])  2.57 us
    ppermute x2, waiting for transfers between devices, extend(): lax.ppermute(last, 'lon', [(i, (i + 1) % count) for i in range(count)])  2.44 us
  transfers between devices with their start and end apart: 16, of which 9 were waited for; matrix products, arithmetic and copies ran while one was open for 0% of the time, Pallas kernels for 5%

profile of v1, /device:TPU:0, one launch (start us, length us, event | category | flops | bytes accessed | tf_op | source)
XLA Modules:
  0.0 62.4 jit_solution(13078822971172192902)
XLA Ops:
  0.6 0.7 %convert_element_type.40 = bf16[16,64]{1,0:T(8,128)(2,1)S(1)} convert(s32[16,64]{1,0:T(8,128)} %param.10) | non-fusion elementwise | flops 1024 | bytes 6144 | tf_op jit(solution)/shard_map/convert_element_type | solution.py:266
  1.3 1.2 %bitcast_multiply_fusion = (bf16[16,64,128]{2,1,0:T(8,128)(2,1)S(1)}, bf16[16,64,128]{2,1,0:T(8,128)(2,1)S(1)}) fusion(bf16[1,16,64,128]{3,2,1,0:T(8,128)(2,1)} %param.9, bf16[16,64]{1,0:T(8,128)(2,1)S(1)} %convert_element_type.40, bf16[1,16,64,128]{3,2,1,0:T(8,128)(2,1)} %param.8), kind=kLoop, calls=%fused_computation.2 | loop fusion | flops 262144 | bytes 1050624 | tf_op jit(solution)/shard_map/mul | solution.py:268
  2.6 0.7 %collective-permute-start.1 = (bf16[6,64,128]{2,1,0:T(8,128)(2,1)S(1)}, bf16[6,64,128]{2,1,0:T(8,128)(2,1)S(1)}, u32[]{:S(2)}, u32[]{:S(2)}) collective-permute-start(bf16[6,64,128]{2,1,0:T(8,128)(2,1)S(1)} %rev.6), channel_id=1, source_target_pairs={{4,28},{12,20},{20,12},{28,4},{5,29},{13,21},{21,13},{29,5},{6,30}... | collective-permute-start | bytes 294920 | tf_op jit(solution)/shard_map/ppermute | solution.py:51
  3.3 7.8 %collective-permute-start = (bf16[6,64,128]{2,1,0:T(8,128)(2,1)S(1)}, bf16[6,64,128]{2,1,0:T(8,128)(2,1)S(1)}, u32[]{:S(2)}, u32[]{:S(2)}) collective-permute-start(bf16[6,64,128]{2,1,0:T(8,128)(2,1)S(1)} %get-tuple-element.21), channel_id=1, source_target_pairs={{0,4},{4,0},{1,5},{5,1},{2,6},{6,2},{3,7},{7,3},{8,12},{12,8},{9,1... | collective-permute-start | bytes 294920 | tf_op jit(solution)/shard_map/ppermute | solution.py:53
  11.2 0.0 collective-permute-done.1
  11.2 2.6 %collective-permute-done = bf16[6,64,128]{2,1,0:T(8,128)(2,1)S(1)} collective-permute-done((bf16[6,64,128]{2,1,0:T(8,128)(2,1)S(1)}, bf16[6,64,128]{2,1,0:T(8,128)(2,1)S(1)}, u32[]{:S(2)}, u32[]{:S(2)}) %collective-permute-start) | collective-permute-done | bytes 98336 | tf_op jit(solution)/shard_map/ppermute | solution.py:53
  13.8 0.1 collective-permute-start.2
  13.9 3.9 %collective-permute-start.3 = (bf16[28,6,128]{2,1,0:T(8,128)(2,1)S(1)}, bf16[28,6,128]{2,1,0:T(8,128)(2,1)S(1)}, u32[]{:S(2)}, u32[]{:S(2)}) collective-permute-start(bf16[28,6,128]{2,1,0:T(8,128)(2,1)S(1)} %pad_maximum_fusion.2), channel_id=1, source_target_pairs={{8,0},{16,8},{24,16},{0,24},{9,1},{17,9},{25,17},{1,25},{10,2},{18... | collective-permute-start | bytes 129032 | tf_op jit(solution)/shard_map/ppermute | solution.py:70
  17.8 2.1 %collective-permute-done.2.west = bf16[28,6,128]{2,1,0:T(8,128)(2,1)S(1)} collective-permute-done((bf16[28,6,128]{2,1,0:T(8,128)(2,1)S(1)}, bf16[28,6,128]{2,1,0:T(8,128)(2,1)S(1)}, u32[]{:S(2)}, u32[]{:S(2)}) %collective-permute-start.2) | collective-permute-done | bytes 43040 | tf_op jit(solution)/shard_map/ppermute | solution.py:69
  19.9 0.0 collective-permute-done.3.east
  19.9 0.2 broadcast_in_dim.23.sea
  20.1 0.0 copy-start.3
  20.1 0.0 copy-start.4
  20.1 0.5 copy-done
  20.6 0.1 copy-done.1
  20.7 0.0 copy-done.2
  20.8 0.0 copy-done.3
  20.8 0.0 copy-done.4
  20.8 8.2 %forward.1 = (bf16[16,64,128]{2,1,0:T(8,128)(2,1)}, bf16[16,64,128]{2,1,0:T(8,128)(2,1)S(1)}, bf16[576,128]{1,0:T(8,128)(2,1)S(1)}) custom-call(bf16[6,64,128]{2,1,0:T(8,128)(2,1)S(1)} %get-tuple-element.33.south, bf16[16,64,128]{2,1,0:T(8,128)(2,1)S(1)} %get-tuple-element.35.block, bf16[6,64,128]{2,1,0:T(8,128)(2,1)S(1)} %get-tuple-element.32.north, ...), custom_call_target="tpu_custom_call" | custom-call | flops 642252800 | bytes 3145728 | tf_op jit(solution)/shard_map/forward/pallas_call | solution.py:275
  29.0 0.1 collective-permute-start.8
  29.2 0.7 %collective-permute-start.5 = (bf16[6,64,128]{2,1,0:T(8,128)(2,1)S(1)}, bf16[6,64,128]{2,1,0:T(8,128)(2,1)S(1)}, u32[]{:S(2)}, u32[]{:S(2)}) collective-permute-start(bf16[6,64,128]{2,1,0:T(8,128)(2,1)S(1)} %rev.7), channel_id=1, source_target_pairs={{4,28},{12,20},{20,12},{28,4},{5,29},{13,21},{21,13},{29,5},{6,30}... | collective-permute-start | bytes 294920 | tf_op jit(solution)/shard_map/ppermute | solution.py:51
  29.9 7.2 %collective-permute-start.4 = (bf16[6,64,128]{2,1,0:T(8,128)(2,1)S(1)}, bf16[6,64,128]{2,1,0:T(8,128)(2,1)S(1)}, u32[]{:S(2)}, u32[]{:S(2)}) collective-permute-start(bf16[6,64,128]{2,1,0:T(8,128)(2,1)S(1)} %get-tuple-element.17), channel_id=1, source_target_pairs={{0,4},{4,0},{1,5},{5,1},{2,6},{6,2},{3,7},{7,3},{8,12},{12,8},{9,1... | collective-permute-start | bytes 294920 | tf_op jit(solution)/shard_map/ppermute | solution.py:53
  37.1 0.0 collective-permute-done.8
  37.1 1.0 %collective-permute-start.11 = (bf16[288,128]{1,0:T(8,128)(2,1)S(1)}, bf16[288,128]{1,0:T(8,128)(2,1)S(1)}, u32[]{:S(2)}, u32[]{:S(2)}) collective-permute-start(bf16[288,128]{1,0:T(8,128)(2,1)S(1)} %add_convert_fusion.1), channel_id=1, source_target_pairs={{0,6},{1,7},{2,4},{3,5},{4,2},{5,3},{6,0},{7,1},{8,14},{9,15},{10,... | collective-permute-start | bytes 221192 | tf_op jit(solution)/shard_map/ppermute | solution.py:79
  38.2 2.0 %collective-permute-start.10 = (bf16[288,128]{1,0:T(8,128)(2,1)S(1)}, bf16[288,128]{1,0:T(8,128)(2,1)S(1)}, u32[]{:S(2)}, u32[]{:S(2)}) collective-permute-start(bf16[288,128]{1,0:T(8,128)(2,1)S(1)} %add_convert_fusion.1), channel_id=1, source_target_pairs={{0,4},{4,0},{1,5},{5,1},{2,6},{6,2},{3,7},{7,3},{8,12},{12,8},{9,1... | collective-permute-start | bytes 221192 | tf_op jit(solution)/shard_map/ppermute | solution.py:79
  40.2 0.5 collective-permute-start.9
  40.7 0.0 collective-permute-done.5
  40.7 0.0 collective-permute-done.4
  40.7 2.5 %collective-permute-done.11 = bf16[288,128]{1,0:T(8,128)(2,1)S(1)} collective-permute-done((bf16[288,128]{1,0:T(8,128)(2,1)S(1)}, bf16[288,128]{1,0:T(8,128)(2,1)S(1)}, u32[]{:S(2)}, u32[]{:S(2)}) %collective-permute-start.11) | collective-permute-done | bytes 73760 | tf_op jit(solution)/shard_map/ppermute | solution.py:79
  43.3 0.5 collective-permute-done.10
  43.8 0.7 %collective-permute-done.9 = bf16[288,128]{1,0:T(8,128)(2,1)S(1)} collective-permute-done((bf16[288,128]{1,0:T(8,128)(2,1)S(1)}, bf16[288,128]{1,0:T(8,128)(2,1)S(1)}, u32[]{:S(2)}, u32[]{:S(2)}) %collective-permute-start.9) | collective-permute-done | bytes 73760 | tf_op jit(solution)/shard_map/ppermute | solution.py:79
  44.6 0.2 collective-permute-start.14
  44.8 0.0 collective-permute-start.13
  44.8 4.2 %collective-permute-start.12 = (bf16[288,128]{1,0:T(8,128)(2,1)S(1)}, bf16[288,128]{1,0:T(8,128)(2,1)S(1)}, u32[]{:S(2)}, u32[]{:S(2)}) collective-permute-start(bf16[288,128]{1,0:T(8,128)(2,1)S(1)} %add_convert_fusion), channel_id=1, source_target_pairs={{0,8},{8,0},{16,24},{24,16},{1,9},{9,1},{17,25},{25,17},{2,10},{10... | collective-permute-start | bytes 221192 | tf_op jit(solution)/shard_map/ppermute | solution.py:79
  49.0 0.1 collective-permute-start.6
  49.1 2.3 %collective-permute-done.14 = bf16[288,128]{1,0:T(8,128)(2,1)S(1)} collective-permute-done((bf16[288,128]{1,0:T(8,128)(2,1)S(1)}, bf16[288,128]{1,0:T(8,128)(2,1)S(1)}, u32[]{:S(2)}, u32[]{:S(2)}) %collective-permute-start.14) | collective-permute-done | bytes 73760 | tf_op jit(solution)/shard_map/ppermute | solution.py:79
  51.4 0.0 collective-permute-done.13
  51.4 1.0 %collective-permute-done.12 = bf16[288,128]{1,0:T(8,128)(2,1)S(1)} collective-permute-done((bf16[288,128]{1,0:T(8,128)(2,1)S(1)}, bf16[288,128]{1,0:T(8,128)(2,1)S(1)}, u32[]{:S(2)}, u32[]{:S(2)}) %collective-permute-start.12) | collective-permute-done | bytes 73760 | tf_op jit(solution)/shard_map/ppermute | solution.py:79
  52.4 0.1 collective-permute-start.15
  52.5 2.2 %collective-permute-start.7 = (bf16[28,6,128]{2,1,0:T(8,128)(2,1)S(1)}, bf16[28,6,128]{2,1,0:T(8,128)(2,1)S(1)}, u32[]{:S(2)}, u32[]{:S(2)}) collective-permute-start(bf16[28,6,128]{2,1,0:T(8,128)(2,1)S(1)} %pad_maximum_fusion.4), channel_id=1, source_target_pairs={{8,0},{16,8},{24,16},{0,24},{9,1},{17,9},{25,17},{1,25},{10,2},{18... | collective-permute-start | bytes 129032 | tf_op jit(solution)/shard_map/ppermute | solution.py:70
  54.7 0.4 collective-permute-done.6.west
  55.1 1.8 %collective-permute-done.7.east = bf16[28,6,128]{2,1,0:T(8,128)(2,1)S(1)} collective-permute-done((bf16[28,6,128]{2,1,0:T(8,128)(2,1)S(1)}, bf16[28,6,128]{2,1,0:T(8,128)(2,1)S(1)}, u32[]{:S(2)}, u32[]{:S(2)}) %collective-permute-start.7) | collective-permute-done | bytes 43040 | tf_op jit(solution)/shard_map/ppermute | solution.py:70
  56.9 2.9 %backward.1 = bf16[16,64,128]{2,1,0:T(8,128)(2,1)} custom-call(s32[1]{0:T(128)} %bitcast.5.northern, bf16[6,64,128]{2,1,0:T(8,128)(2,1)S(1)} %get-tuple-element.27.south, bf16[16,64,128]{2,1,0:T(8,128)(2,1)S(1)} %get-tuple-element.10.block, bf16[6,64,128]{2,1,0:T(8,128)(2,1)S(1)} %get-tuple-element.26.north, ...), custom_call_target="tpu_custom_call" | custom-call | flops 256901120 | bytes 2097152 | tf_op jit(solution)/shard_map/backward/pallas_call | solution.py:291
  59.8 0.0 collective-permute-done.15
  59.8 0.6 slice.104
  60.5 0.6 slice.105
  61.0 0.7 %slice.108 = f32[256,128]{1,0:T(8,128)} slice(f32[576,128]{1,0:T(8,128)S(1)} %fusion), slice={[0:256], [0:128]} | slice | bytes 262144 | tf_op jit(solution)/shard_map/slice | solution.py:304
  61.7 0.7 %pad_maximum_fusion = f32[128,256]{1,0:T(8,128)} fusion(f32[128,128]{1,0:T(8,128)S(1)} %get-tuple-element.13, f32[128,128]{1,0:T(8,128)S(1)} %get-tuple-element.12), kind=kLoop, calls=%fused_computation.7 | loop fusion | flops 32768 | bytes 262144 | tf_op jit(solution)/shard_map/concatenate | solution.py:305
  (24 shorter events, 0.5 us)
Async XLA Ops:
  2.6 8.5 %collective-permute-start.1 = (bf16[6,64,128]{2,1,0:T(8,128)(2,1)S(1)}, bf16[6,64,128]{2,1,0:T(8,128)(2,1)S(1)}, u32[]{:S(2)}, u32[]{:S(2)}) collective-permute-start(bf16[6,64,128]{2,1,0:T(8,128)(2,1)S(1)} %rev.6), channel_id=1, source_target_pairs={{4,28},{12,20},{20,12},{28,4},{5,29},{13,21},{21,13},{29,5},{6,30}... | collective-permute-start | bytes 294920 | tf_op jit(solution)/shard_map/ppermute | solution.py:51
  3.3 10.4 %collective-permute-start = (bf16[6,64,128]{2,1,0:T(8,128)(2,1)S(1)}, bf16[6,64,128]{2,1,0:T(8,128)(2,1)S(1)}, u32[]{:S(2)}, u32[]{:S(2)}) collective-permute-start(bf16[6,64,128]{2,1,0:T(8,128)(2,1)S(1)} %get-tuple-element.21), channel_id=1, source_target_pairs={{0,4},{4,0},{1,5},{5,1},{2,6},{6,2},{3,7},{7,3},{8,12},{12,8},{9,1... | collective-permute-start | bytes 294920 | tf_op jit(solution)/shard_map/ppermute | solution.py:53
  13.8 6.0 %collective-permute-start.2 = (bf16[28,6,128]{2,1,0:T(8,128)(2,1)S(1)}, bf16[28,6,128]{2,1,0:T(8,128)(2,1)S(1)}, u32[]{:S(2)}, u32[]{:S(2)}) collective-permute-start(bf16[28,6,128]{2,1,0:T(8,128)(2,1)S(1)} %pad_maximum_fusion.1), channel_id=1, source_target_pairs={{0,8},{8,16},{16,24},{24,0},{1,9},{9,17},{17,25},{25,1},{2,10},{10... | collective-permute-start | bytes 129032 | tf_op jit(solution)/shard_map/ppermute | solution.py:69
  13.9 5.9 %collective-permute-start.3 = (bf16[28,6,128]{2,1,0:T(8,128)(2,1)S(1)}, bf16[28,6,128]{2,1,0:T(8,128)(2,1)S(1)}, u32[]{:S(2)}, u32[]{:S(2)}) collective-permute-start(bf16[28,6,128]{2,1,0:T(8,128)(2,1)S(1)} %pad_maximum_fusion.2), channel_id=1, source_target_pairs={{8,0},{16,8},{24,16},{0,24},{9,1},{17,9},{25,17},{1,25},{10,2},{18... | collective-permute-start | bytes 129032 | tf_op jit(solution)/shard_map/ppermute | solution.py:70
  19.9 0.7 %copy-start = (f32[49,128]{1,0:T(8,128)S(1)}, f32[49,128]{1,0:T(8,128)}, u32[]{:S(2)}) copy-start(f32[49,128]{1,0:T(8,128)} %taps.3) | copy-start | bytes 75268
  19.9 0.9 %copy-start.1 = (bf16[128,256]{1,0:T(8,128)(2,1)S(1)}, bf16[128,256]{1,0:T(8,128)(2,1)}, u32[]{:S(2)}) copy-start(bf16[128,256]{1,0:T(8,128)(2,1)} %up.1) | copy-start | bytes 196612
  19.9 0.9 %copy-start.2 = (bf16[256,128]{1,0:T(8,128)(2,1)S(1)}, bf16[256,128]{1,0:T(8,128)(2,1)}, u32[]{:S(2)}) copy-start(bf16[256,128]{1,0:T(8,128)(2,1)} %down.1) | copy-start | bytes 196612
  20.1 0.7 %copy-start.3 = (f32[128]{0:T(128)S(1)}, f32[128]{0:T(128)}, u32[]{:S(2)}) copy-start(f32[128]{0:T(128)} %param.12) | copy-start | bytes 1540
  20.1 0.7 %copy-start.4 = (f32[128]{0:T(128)S(1)}, f32[128]{0:T(128)}, u32[]{:S(2)}) copy-start(f32[128]{0:T(128)} %param.13) | copy-start | bytes 1540
  29.0 8.0 %collective-permute-start.8 = (bf16[288,128]{1,0:T(8,128)(2,1)S(1)}, bf16[288,128]{1,0:T(8,128)(2,1)S(1)}, u32[]{:S(2)}, u32[]{:S(2)}) collective-permute-start(bf16[288,128]{1,0:T(8,128)(2,1)S(1)} %broadcast_select_fusion.4), channel_id=1, source_target_pairs={{0,1},{1,0},{2,3},{3,2},{4,5},{5,4},{6,7},{7,6},{8,9},{9,8},{10,11... | collective-permute-start | bytes 221192 | tf_op jit(solution)/shard_map/ppermute | solution.py:79
  29.2 11.5 %collective-permute-start.5 = (bf16[6,64,128]{2,1,0:T(8,128)(2,1)S(1)}, bf16[6,64,128]{2,1,0:T(8,128)(2,1)S(1)}, u32[]{:S(2)}, u32[]{:S(2)}) collective-permute-start(bf16[6,64,128]{2,1,0:T(8,128)(2,1)S(1)} %rev.7), channel_id=1, source_target_pairs={{4,28},{12,20},{20,12},{28,4},{5,29},{13,21},{21,13},{29,5},{6,30}... | collective-permute-start | bytes 294920 | tf_op jit(solution)/shard_map/ppermute | solution.py:51
  29.9 10.8 %collective-permute-start.4 = (bf16[6,64,128]{2,1,0:T(8,128)(2,1)S(1)}, bf16[6,64,128]{2,1,0:T(8,128)(2,1)S(1)}, u32[]{:S(2)}, u32[]{:S(2)}) collective-permute-start(bf16[6,64,128]{2,1,0:T(8,128)(2,1)S(1)} %get-tuple-element.17), channel_id=1, source_target_pairs={{0,4},{4,0},{1,5},{5,1},{2,6},{6,2},{3,7},{7,3},{8,12},{12,8},{9,1... | collective-permute-start | bytes 294920 | tf_op jit(solution)/shard_map/ppermute | solution.py:53
  37.1 6.2 %collective-permute-start.11 = (bf16[288,128]{1,0:T(8,128)(2,1)S(1)}, bf16[288,128]{1,0:T(8,128)(2,1)S(1)}, u32[]{:S(2)}, u32[]{:S(2)}) collective-permute-start(bf16[288,128]{1,0:T(8,128)(2,1)S(1)} %add_convert_fusion.1), channel_id=1, source_target_pairs={{0,6},{1,7},{2,4},{3,5},{4,2},{5,3},{6,0},{7,1},{8,14},{9,15},{10,... | collective-permute-start | bytes 221192 | tf_op jit(solution)/shard_map/ppermute | solution.py:79
  38.2 5.7 %collective-permute-start.10 = (bf16[288,128]{1,0:T(8,128)(2,1)S(1)}, bf16[288,128]{1,0:T(8,128)(2,1)S(1)}, u32[]{:S(2)}, u32[]{:S(2)}) collective-permute-start(bf16[288,128]{1,0:T(8,128)(2,1)S(1)} %add_convert_fusion.1), channel_id=1, source_target_pairs={{0,4},{4,0},{1,5},{5,1},{2,6},{6,2},{3,7},{7,3},{8,12},{12,8},{9,1... | collective-permute-start | bytes 221192 | tf_op jit(solution)/shard_map/ppermute | solution.py:79
  40.2 4.4 %collective-permute-start.9 = (bf16[288,128]{1,0:T(8,128)(2,1)S(1)}, bf16[288,128]{1,0:T(8,128)(2,1)S(1)}, u32[]{:S(2)}, u32[]{:S(2)}) collective-permute-start(bf16[288,128]{1,0:T(8,128)(2,1)S(1)} %add_convert_fusion.1), channel_id=1, source_target_pairs={{0,2},{1,3},{2,0},{3,1},{4,6},{5,7},{6,4},{7,5},{8,10},{9,11},{10,... | collective-permute-start | bytes 221192 | tf_op jit(solution)/shard_map/ppermute | solution.py:79
  44.6 6.8 %collective-permute-start.14 = (bf16[288,128]{1,0:T(8,128)(2,1)S(1)}, bf16[288,128]{1,0:T(8,128)(2,1)S(1)}, u32[]{:S(2)}, u32[]{:S(2)}) collective-permute-start(bf16[288,128]{1,0:T(8,128)(2,1)S(1)} %add_convert_fusion), channel_id=1, source_target_pairs={{0,24},{8,16},{16,8},{24,0},{1,25},{9,17},{17,9},{25,1},{2,26},{10... | collective-permute-start | bytes 221192 | tf_op jit(solution)/shard_map/ppermute | solution.py:79
  44.8 6.6 %collective-permute-start.13 = (bf16[288,128]{1,0:T(8,128)(2,1)S(1)}, bf16[288,128]{1,0:T(8,128)(2,1)S(1)}, u32[]{:S(2)}, u32[]{:S(2)}) collective-permute-start(bf16[288,128]{1,0:T(8,128)(2,1)S(1)} %add_convert_fusion), channel_id=1, source_target_pairs={{0,16},{8,24},{16,0},{24,8},{1,17},{9,25},{17,1},{25,9},{2,18},{10... | collective-permute-start | bytes 221192 | tf_op jit(solution)/shard_map/ppermute | solution.py:79
  44.8 7.6 %collective-permute-start.12 = (bf16[288,128]{1,0:T(8,128)(2,1)S(1)}, bf16[288,128]{1,0:T(8,128)(2,1)S(1)}, u32[]{:S(2)}, u32[]{:S(2)}) collective-permute-start(bf16[288,128]{1,0:T(8,128)(2,1)S(1)} %add_convert_fusion), channel_id=1, source_target_pairs={{0,8},{8,0},{16,24},{24,16},{1,9},{9,1},{17,25},{25,17},{2,10},{10... | collective-permute-start | bytes 221192 | tf_op jit(solution)/shard_map/ppermute | solution.py:79
  49.0 6.0 %collective-permute-start.6 = (bf16[28,6,128]{2,1,0:T(8,128)(2,1)S(1)}, bf16[28,6,128]{2,1,0:T(8,128)(2,1)S(1)}, u32[]{:S(2)}, u32[]{:S(2)}) collective-permute-start(bf16[28,6,128]{2,1,0:T(8,128)(2,1)S(1)} %pad_maximum_fusion.3), channel_id=1, source_target_pairs={{0,8},{8,16},{16,24},{24,0},{1,9},{9,17},{17,25},{25,1},{2,10},{10... | collective-permute-start | bytes 129032 | tf_op jit(solution)/shard_map/ppermute | solution.py:69
  52.4 7.4 %collective-permute-start.15 = (f32[288,128]{1,0:T(8,128)S(1)}, f32[288,128]{1,0:T(8,128)S(1)}, u32[]{:S(2)}, u32[]{:S(2)}) collective-permute-start(f32[288,128]{1,0:T(8,128)S(1)} %add_add_fusion), channel_id=1, source_target_pairs={{0,1},{1,0},{2,3},{3,2},{4,5},{5,4},{6,7},{7,6},{8,9},{9,8},{10,11... | collective-permute-start | bytes 442376 | tf_op jit(solution)/shard_map/ppermute | solution.py:79
  52.5 4.4 %collective-permute-start.7 = (bf16[28,6,128]{2,1,0:T(8,128)(2,1)S(1)}, bf16[28,6,128]{2,1,0:T(8,128)(2,1)S(1)}, u32[]{:S(2)}, u32[]{:S(2)}) collective-permute-start(bf16[28,6,128]{2,1,0:T(8,128)(2,1)S(1)} %pad_maximum_fusion.4), channel_id=1, source_target_pairs={{8,0},{16,8},{24,16},{0,24},{9,1},{17,9},{25,17},{1,25},{10,2},{18... | collective-permute-start | bytes 129032 | tf_op jit(solution)/shard_map/ppermute | solution.py:70

commit v2 on v1

--- a/solution.py
+++ b/solution.py
@@ -42,33 +42,54 @@
     return lax.axis_index("lat") == lax.axis_size("lat") - 1
 
 
-def row_halos(block):
-    count, width = lax.axis_size("lat"), lax.axis_size("lon")
+def xor_partner(value, axis, bits):
+    return lax.ppermute(value, axis, [(i, i ^ bits) for i in range(lax.axis_size(axis))])
+
+
+def columns(block, top):
+    count = lax.axis_size("lon")
+    first, last = block[:, :REACH], block[:, block.shape[1] - REACH :]
+    flipped = top[::-1, ::-1]
+    if count == 4:
+        even = lax.axis_index("lon") % 2 == 0
+        near, far = jnp.where(even, last, first), jnp.where(even, first, last)
+        corner = jnp.where(even, flipped[:, :REACH], flipped[:, flipped.shape[1] - REACH :])
+        own = jnp.where(even, flipped[:, flipped.shape[1] - REACH :], flipped[:, :REACH])
+        channels = block.shape[2]
+        cells = far.shape[0] * far.shape[1]
+        joint = jnp.concatenate([far.reshape(-1, channels), flipped.reshape(-1, channels)])
+        joint = xor_partner(joint, "lon", 3)
+        corner = xor_partner(corner, "lon", 2)
+        near = xor_partner(near, "lon", 1)
+        far, folded = joint[:cells].reshape(far.shape), joint[cells:].reshape(flipped.shape)
+        west, east = jnp.where(even, far, near), jnp.where(even, near, far)
+        sides = [jnp.where(even, own, corner), folded, jnp.where(even, corner, own)]
+        return west, east, jnp.concatenate(sides, 1)
+    ring = [(i, (i + 1) % count) for i in range(count)]
+    back = [(j, i) for i, j in ring]
+    folded = lax.ppermute(flipped, "lon", [(i, count - 1 - i) for i in range(count)])
+    west, east = lax.ppermute(last, "lon", ring), lax.ppermute(first, "lon", back)
+    left = lax.ppermute(folded[:, folded.shape[1] - REACH :], "lon", ring)
+    right = lax.ppermute(folded[:, :REACH], "lon", back)
+    return west, east, jnp.concatenate([left, folded, right], 1)
+
+
+def extend(block):
+    count = lax.axis_size("lat")
     top, bottom = block[block.shape[0] - REACH :], block[:REACH]
+    west, east, folded = columns(block, top)
     northern = is_northern()
-    axes = ("lon", "lat")
-    fold = route(axes, lambda c, r: (width - 1 - c, r) if r == count - 1 else None)
-    folded = lax.ppermute(top[::-1, ::-1], axes, fold)
+    top = jnp.concatenate([west[-REACH:], top, east[-REACH:]], 1)
+    bottom = jnp.concatenate([west[:REACH], bottom, east[:REACH]], 1)
     if count == 2:
-        facing = lax.ppermute(jnp.where(northern, bottom, top), "lat", [(0, 1), (1, 0)])
+        facing = xor_partner(jnp.where(northern, bottom, top), "lat", 1)
         south = jnp.where(northern, facing, jnp.zeros_like(facing))
         north = jnp.where(northern, folded, facing)
     else:
         south = lax.ppermute(top, "lat", [(i, i + 1) for i in range(count - 1)])
         above = lax.ppermute(bottom, "lat", [(i + 1, i) for i in range(count - 1)])
         north = jnp.where(northern, folded, above)
-    return south, north
-
-
-def extend(block):
-    south, north = row_halos(block)
-    cols = block.shape[1]
-    count = lax.axis_size("lon")
-    first = jnp.concatenate([a[:, :REACH] for a in (south, block, north)], 0)
-    last = jnp.concatenate([a[:, cols - REACH :] for a in (south, block, north)], 0)
-    west = lax.ppermute(last, "lon", [(i, (i + 1) % count) for i in range(count)])
-    east = lax.ppermute(first, "lon", [((i + 1) % count, i) for i in range(count)])
-    return south, block, north, west, east
+    return south, north, west, east
 
 
 def partners(value, bits):
@@ -79,19 +100,11 @@
     return lax.ppermute(value, axes, route(axes, lambda *at: [i ^ flip[a] for a, i in zip(axes, at)]))
 
 
-def summed(packed):
-    axes = ("ens", "lat", "lon")
+def summed(mine, other):
+    axes = ("ens", "lon", "lat")
     bits = [(a, 1 << b) for a in axes for b in range(lax.axis_size(a).bit_length() - 1)]
-    if any(lax.axis_size(a) & (lax.axis_size(a) - 1) for a in axes):
-        return lax.psum(packed.astype(F32), axes)
-    half = packed.shape[0] // 2
-    split = bits[0]
-    odd = lax.axis_index(split[0]) & 1
-    low, high = packed[:half], packed[half:]
-    mine = jnp.where(odd == 0, low, high)
-    other = jnp.where(odd == 0, high, low)
-    total = mine.astype(F32) + partners(other, [split]).astype(F32)
-    rest = bits[1:]
+    total = mine + partners(other, bits[:1]).astype(F32)
+    rest = bits[2:4] + bits[1:2] + bits[4:] if lax.axis_size("lon") == 4 else bits[1:]
     while rest:
         pair, rest = rest[:2], rest[2:]
         sent = total.astype(BF16)
@@ -101,26 +114,29 @@
             total = (sent.astype(F32) + one.astype(F32)) + (two.astype(F32) + far.astype(F32))
         else:
             total = sent.astype(F32) + partners(sent, pair).astype(F32)
-    back = partners(total, [split])
-    return jnp.where(odd == 0, jnp.concatenate([total, back]), jnp.concatenate([back, total]))
-
-
-def fill(wide, south, block, north, west, east):
+    return total, partners(total, bits[:1])
+
+
+def fill(wide, south, block, north, west, east, sea=None):
     rows, cols = block.shape[0], block.shape[1]
-    for ref, start, count in ((south, 0, REACH), (block, REACH, rows), (north, REACH + rows, REACH)):
-
-        def one(r, carry, ref=ref, start=start):
-            wide[start + r, LEFT : LEFT + cols] = ref[r].astype(F32)
-            return carry
-
-        lax.fori_loop(0, count, one, 0, unroll=2)
-
-    def sides(r, carry):
-        wide[r, BASE:LEFT] = west[r].astype(F32)
-        wide[r, LEFT + cols : LEFT + cols + REACH] = east[r].astype(F32)
+
+    def inner(r, carry):
+        value = block[r].astype(F32)
+        if sea is not None:
+            value = value * sea[r].astype(F32)
+        wide[REACH + r, LEFT : LEFT + cols] = value
+        wide[REACH + r, BASE:LEFT] = west[r].astype(F32)
+        wide[REACH + r, LEFT + cols : LEFT + cols + REACH] = east[r].astype(F32)
         return carry
 
-    lax.fori_loop(0, rows + 2 * REACH, sides, 0, unroll=4)
+    lax.fori_loop(0, rows, inner, 0, unroll=2)
+
+    def outer(r, carry):
+        wide[r, BASE : LEFT + cols + REACH] = south[r].astype(F32)
+        wide[REACH + rows + r, BASE : LEFT + cols + REACH] = north[r].astype(F32)
+        return carry
+
+    lax.fori_loop(0, REACH, outer, 0, unroll=2)
 
 
 def conv(wide, tap, rows, cols, store):
@@ -150,13 +166,13 @@
     lax.fori_loop(0, 2, parity, 0)
 
 
-def forward_kernel(south, block, north, west, east, upstream, sea, taps, gain, shift, up, down,
-                   output, grad, packed, wide, spread, mixed):
+def forward_kernel(south, block, north, west, east, cotangent, sea, taps, gain, shift, up, down,
+                   output, grad, parts, wide, mixed, spread):
     rows, cols, channels = block.shape
     hidden = up.shape[1]
     for k in range(TAPS):
         spread[k] = jnp.broadcast_to(taps[k : k + 1], (LANE, channels))
-    fill(wide, south, block, north, west, east)
+    fill(wide, south, block, north, west, east, sea)
 
     def store(row, col, value):
         mixed[row, col : col + LANE] = value
@@ -187,7 +203,7 @@
         ocean = sea[at].reshape(cells, channels).astype(F32)
         state = block[at].reshape(cells, channels).astype(F32)
         output[at] = ((state + product) * ocean).astype(BF16).reshape(lines, cols, channels)
-        above = upstream[at].reshape(cells, channels)
+        above = (cotangent[at] * sea[at]).reshape(cells, channels)
         down_sum = down_sum + lax.dot_general(above, activated, tn, preferred_element_type=F32)
         act_grad = lax.dot_general(above, down_w, nt, preferred_element_type=F32)
         deriv = gate + pre * (gate * (1.0 - tanh)) * (SLOPE + (3.0 * SLOPE * CUBIC) * square)
@@ -208,11 +224,19 @@
     up_sum, down_sum, gain_sum, shift_sum = lax.fori_loop(
         0, rows // lines, chunk, (big, big, small, small)
     )
-    packed[0:hidden] = down_sum.T.astype(BF16)
+    parts[0:hidden] = down_sum.T
     for n in range(hidden // channels):
         start = hidden + n * channels
-        packed[start : start + channels] = up_sum[:, n * channels : (n + 1) * channels].astype(BF16)
-
+        parts[start : start + channels] = up_sum[:, n * channels : (n + 1) * channels]
+    sums = [jnp.sum(gain_sum, 0, keepdims=True), jnp.sum(shift_sum, 0, keepdims=True)]
+    parts[2 * hidden :] = jnp.concatenate(sums + [jnp.zeros((LANE - 2, channels), F32)], 0)
+
+
+def kernel_kernel(odd, wide, mixed, parts, mine, other):
+    rows, cols, channels = mixed.shape
+    large = parts.shape[0] - LANE
+    half = mine.shape[0]
+    small = jnp.zeros((LANE, channels), F32)
     pieces = []
     for taps_i in (range(0, 4), range(4, KERNEL)):
 
@@ -233,13 +257,46 @@
 
         zero = tuple(small for _ in range(len(taps_i) * KERNEL))
         pieces += list(lax.fori_loop(0, rows // 4, quad, zero))
-    pieces += [gain_sum, shift_sum]
     pieces = [jnp.sum(p, 0, keepdims=True) for p in pieces]
-    pieces += [jnp.zeros((packed.shape[0] - 2 * hidden - len(pieces), channels), F32)]
-    packed[2 * hidden :] = jnp.concatenate(pieces, 0).astype(BF16)
-
-
-def backward_kernel(northern, south, block, north, west, east, upstream, sea, taps,
+    pieces += [parts[large : large + 2], jnp.zeros((2 * half - large - TAPS - 2, channels), F32)]
+    end = jnp.concatenate(pieces, 0)
+
+    @pl.when(odd[0] == 0)
+    def _():
+        mine[...] = parts[0:half]
+        other[0 : large - half] = parts[half:large].astype(BF16)
+        other[large - half :] = end.astype(BF16)
+
+    @pl.when(odd[0] != 0)
+    def _():
+        other[...] = parts[0:half].astype(BF16)
+        mine[0 : large - half] = parts[half:large]
+        mine[large - half :] = end
+
+
+def final_kernel(odd, total, back, kernel_grad, norm_grad, up_grad, down_grad, whole, *, factor):
+    half = total.shape[0]
+    hidden, channels = down_grad.shape
+
+    @pl.when(odd[0] == 0)
+    def _():
+        whole[0:half] = total[...] * factor
+        whole[half:] = back[...] * factor
+
+    @pl.when(odd[0] != 0)
+    def _():
+        whole[0:half] = back[...] * factor
+        whole[half:] = total[...] * factor
+
+    down_grad[...] = whole[0:hidden]
+    for n in range(hidden // channels):
+        start = hidden + n * channels
+        up_grad[:, n * channels : (n + 1) * channels] = whole[start : start + channels]
+    kernel_grad[...] = whole[2 * hidden : 2 * hidden + TAPS]
+    norm_grad[...] = whole[2 * hidden + TAPS : 2 * hidden + TAPS + 2]
+
+
+def backward_kernel(northern, south, block, north, west, east, cotangent, sea, taps,
                     field_grad, wide, spread, folded):
     rows, cols, channels = block.shape
     for k in range(TAPS):
@@ -255,58 +312,76 @@
 
     def store(row, col, value):
         at = (row, slice(col, col + LANE))
-        field_grad[at] = ((upstream[at].astype(F32) + value) * sea[at].astype(F32)).astype(BF16)
+        field_grad[at] = ((cotangent[at].astype(F32) + value) * sea[at].astype(F32)).astype(BF16)
 
     conv(wide, tap, rows, cols, store)
+
+
+def call(kernel, outs, operands, scratch=(), flags=0, work=0, name=None):
+    vmem, smem = pl.BlockSpec(memory_space=pltpu.VMEM), pl.BlockSpec(memory_space=pltpu.SMEM)
+    moved = sum(math.prod(a.shape) * a.dtype.itemsize for a in (*operands, *outs))
+    return pl.pallas_call(
+        kernel,
+        out_shape=outs,
+        in_specs=[smem] * flags + [vmem] * (len(operands) - flags),
+        out_specs=[vmem] * len(outs),
+        scratch_shapes=scratch,
+        compiler_params=pltpu.CompilerParams(vmem_limit_bytes=24 * 1024 * 1024),
+        cost_estimate=pl.CostEstimate(flops=work, bytes_accessed=moved, transcendentals=0),
+        name=name,
+    )(*operands)
 
 
 def shards(field, cotangent, land_mask, kernel_taps, norm_gain, norm_shift, up_weight, down_weight):
     rows, cols, channels = field.shape[1:]
     hidden = up_weight.shape[1]
+    shape = jax.ShapeDtypeStruct
     sea = jnp.broadcast_to(land_mask.astype(BF16)[:, :, None], (rows, cols, channels))
-    masked = field[0] * sea
-    upstream = cotangent[0] * sea
-    vmem = pl.BlockSpec(memory_space=pltpu.VMEM)
-    smem = pl.BlockSpec(memory_space=pltpu.SMEM)
-    wide = pltpu.VMEM((rows + 2 * REACH, cols + 2 * LEFT, channels), F32)
+    state = field[0]
+    south, north, west, east = extend(state * sea)
+    tile = (rows, cols, channels)
+    wide = (rows + 2 * REACH, cols + 2 * LEFT, channels)
     spread = pltpu.VMEM((TAPS, LANE, channels), F32)
-    small = -(-(TAPS + 2) // 64) * 64
+    half = hidden + 32
     macs = TAPS * rows * cols * channels
-    output, grad, packed = pl.pallas_call(
+    odd = (lax.axis_index("ens") % 2).astype(jnp.int32)[None]
+    northern = is_northern().astype(jnp.int32)[None]
+    output, grad, parts, widened, mixed_grad = call(
         forward_kernel,
-        out_shape=(
-            jax.ShapeDtypeStruct((rows, cols, channels), BF16),
-            jax.ShapeDtypeStruct((rows, cols, channels), BF16),
-            jax.ShapeDtypeStruct((2 * hidden + small, channels), BF16),
-        ),
-        in_specs=[vmem] * 12,
-        out_specs=[vmem] * 3,
-        scratch_shapes=[wide, spread, pltpu.VMEM((rows, cols, channels), F32)],
-        compiler_params=pltpu.CompilerParams(vmem_limit_bytes=32 * 1024 * 1024),
-        cost_estimate=pl.CostEstimate(flops=100 * macs, bytes_accessed=3 << 20, transcendentals=0),
+        (shape(tile, BF16), shape(tile, BF16), shape((2 * hidden + LANE, channels), F32), shape(wide, F32), shape(tile, F32)),
+        (south, state, north, west, east, cotangent[0], sea, kernel_taps, norm_gain[None], norm_shift[None], up_weight, down_weight),
+        [spread],
+        work=80 * macs,
         name="forward",
-    )(*extend(masked), upstream, sea, kernel_taps, norm_gain[None], norm_shift[None], up_weight, down_weight)
-
-    northern = is_northern().astype(jnp.int32)[None]
-    field_grad = pl.pallas_call(
+    )
+    mine, other = call(
+        kernel_kernel,
+        (shape((half, channels), F32), shape((half, channels), BF16)),
+        (odd, widened, mixed_grad, parts),
+        flags=1,
+        work=20 * macs,
+        name="kernel_gradient",
+    )
+    south, north, west, east = extend(grad)
+    (field_grad,) = call(
         backward_kernel,
-        out_shape=jax.ShapeDtypeStruct((rows, cols, channels), BF16),
-        in_specs=[smem] + [vmem] * 8,
-        out_specs=vmem,
-        scratch_shapes=[wide, spread, spread],
-        compiler_params=pltpu.CompilerParams(vmem_limit_bytes=32 * 1024 * 1024),
-        cost_estimate=pl.CostEstimate(flops=40 * macs, bytes_accessed=2 << 20, transcendentals=0),
+        (shape(tile, BF16),),
+        (northern, south, grad, north, west, east, cotangent[0], sea, kernel_taps),
+        [pltpu.VMEM(wide, F32), spread, spread],
+        flags=1,
+        work=30 * macs,
         name="backward",
-    )(northern, *extend(grad), upstream, sea, kernel_taps)
-
+    )
     count = rows * cols * lax.axis_size("lon") * lax.axis_size("lat") * lax.axis_size("ens")
-    total = summed(packed) * (1.0 / math.sqrt(count))
-    down_grad = total[:hidden]
-    up_grad = jnp.concatenate(
-        [total[hidden + n * channels : hidden + (n + 1) * channels] for n in range(hidden // channels)], 1
-    )
-    kernel_grad = total[2 * hidden : 2 * hidden + TAPS]
-    norm_grad = total[2 * hidden + TAPS : 2 * hidden + TAPS + 2]
+    total, back = summed(mine, other)
+    kernel_grad, norm_grad, up_grad, down_grad = call(
+        functools.partial(final_kernel, factor=1.0 / math.sqrt(count)),
+        (shape((TAPS, channels), F32), shape((2, channels), F32), shape((channels, hidden), F32), shape((hidden, channels), F32)),
+        (odd, total, back),
+        [pltpu.VMEM((2 * half, channels), F32)],
+        flags=1,
+        name="final",
+    )
     return output[None], field_grad[None], kernel_grad, norm_grad, up_grad, down_grad
 
 

time: 62.6 us -> 55.3 us (0.88)
  starting transfers between devices: 30.7 us -> 21 us
  waiting for transfers between devices: 13.9 us -> 18.6 us
  local copies, waits for them, and re-layouts: 2.88 us -> 0.62 us
    ppermute x8, starting transfers between devices: 22.5 us -> 13.1 us  [xor_partner(): lax.ppermute(value, axis, [(i, i ^ bits) for i in range(lax.axis_size(axi...]
    ppermute x8, waiting for transfers between devices: 6.86 us -> 9.68 us  [xor_partner(): lax.ppermute(value, axis, [(i, i ^ bits) for i in range(lax.axis_size(axi...]
    ppermute x8, waiting for transfers between devices: 7.07 us -> 8.95 us  [partners(): lax.ppermute(value, axes, route(axes, lambda *at: [i ^ flip[a] for a, i i...]
    slice x9 -> x15, local copies, waits for them, and re-layouts: 1.92 us -> 0.22 us  [the longest x4 0.08 us: columns(): flipped[:, flipped.shape[1] - REACH:]]
    concatenate x5 -> x2, other arithmetic: 0.73 us -> 0.02 us  [columns(): jnp.concatenate([far.reshape(-1, channels), flipped.reshape(-1, channels)])]
    unnamed x10 -> x14, local copies, waits for them, and re-layouts: 0.67 us -> 0.04 us
    pallas_call x2 -> x4, Pallas kernels: 11.1 us -> 11.5 us  [call(): pl.pallas_call(kernel, out_shape=outs, in_specs=[smem] * flags + [vmem] *...]
    mul x2 -> x1, other arithmetic: 1.26 us -> 1.15 us  [shards(): south, north, west, east = extend(state * sea)]
  transfers between devices with their start and end apart: 16 -> 16, of which waited for: 9 -> 9; matrix products, arithmetic and copies ran while one was open for 0% -> 1% of each run, Pallas kernels for 5% -> 5%
where the time goes in v2:
time: 55.3 us; the launch traced here: 55.1 us
  starting transfers between devices  21 us (38%)
  waiting for transfers between devices  18.6 us (34%)
  Pallas kernels  11.5 us (21%)
  other arithmetic  2.37 us (4%)
  between operations  0.98 us (2%)
  local copies, waits for them, and re-layouts  0.62 us (1%)
    ppermute x8, starting transfers between devices, xor_partner(): lax.ppermute(value, axis, [(i, i ^ bits) for i in range(lax.axis_size(axi...  13.1 us
    pallas_call x4, Pallas kernels, call(): pl.pallas_call(kernel, out_shape=outs, in_specs=[smem] * flags + [vmem] *...  11.5 us
    ppermute x8, waiting for transfers between devices, xor_partner(): lax.ppermute(value, axis, [(i, i ^ bits) for i in range(lax.axis_size(axi...  9.68 us
    ppermute x8, waiting for transfers between devices, partners(): lax.ppermute(value, axes, route(axes, lambda *at: [i ^ flip[a] for a, i i...  8.95 us
    ppermute x8, starting transfers between devices, partners(): lax.ppermute(value, axes, route(axes, lambda *at: [i ^ flip[a] for a, i i...  7.84 us
    mul x1, other arithmetic, shards(): south, north, west, east = extend(state * sea)  1.15 us
  transfers between devices with their start and end apart: 16, of which 9 were waited for; matrix products, arithmetic and copies ran while one was open for 1% of the time, Pallas kernels for 5%

profile of v2, /device:TPU:0, one launch (start us, length us, event | category | flops | bytes accessed | tf_op | source)
XLA Modules:
  0.0 55.1 jit_solution(2500646342294845391)
XLA Ops:
  0.6 0.7 %convert_element_type.37 = bf16[16,64]{1,0:T(8,128)(2,1)S(1)} convert(s32[16,64]{1,0:T(8,128)} %param.10) | non-fusion elementwise | flops 1024 | bytes 6144 | tf_op jit(solution)/shard_map/convert_element_type | solution.py:339
  1.3 1.1 %broadcast_multiply_fusion = bf16[16,64,128]{2,1,0:T(8,128)(2,1)S(1)} fusion(bf16[16,64]{1,0:T(8,128)(2,1)S(1)} %convert_element_type.37, bf16[1,16,64,128]{3,2,1,0:T(8,128)(2,1)} %param.8), kind=kLoop, calls=%fused_computation.3 | loop fusion | flops 131072 | bytes 526336 | tf_op jit(solution)/shard_map/mul | solution.py:341
  2.6 0.0 copy-start
  2.6 0.0 copy-start.1
  2.6 0.0 copy-start.2
  2.6 0.0 copy-start.3
  2.6 0.0 copy-start.4
  2.6 0.0 copy-start.5
  2.6 0.0 copy-start.6
  2.7 5.1 %collective-permute-start = (bf16[480,128]{1,0:T(8,128)(2,1)S(1)}, bf16[480,128]{1,0:T(8,128)(2,1)S(1)}, u32[]{:S(2)}, u32[]{:S(2)}) collective-permute-start(bf16[480,128]{1,0:T(8,128)(2,1)S(1)} %pad_maximum_fusion), channel_id=1, source_target_pairs={{0,24},{8,16},{16,8},{24,0},{1,25},{9,17},{17,9},{25,1},{2,26},{10... | collective-permute-start | bytes 368648 | tf_op jit(solution)/shard_map/ppermute | solution.py:46
  7.8 0.0 collective-permute-start.1
  7.9 0.7 %collective-permute-start.3 = (bf16[6,6,128]{2,1,0:T(8,128)(2,1)S(1)}, bf16[6,6,128]{2,1,0:T(8,128)(2,1)S(1)}, u32[]{:S(2)}, u32[]{:S(2)}) collective-permute-start(bf16[6,6,128]{2,1,0:T(8,128)(2,1)S(1)} %broadcast_select_fusion.16), channel_id=1, source_target_pairs={{0,16},{8,24},{16,0},{24,8},{1,17},{9,25},{17,1},{25,9},{2,18},{10... | collective-permute-start | bytes 27656 | tf_op jit(solution)/shard_map/ppermute | solution.py:46
  8.6 3.0 %collective-permute-done = bf16[480,128]{1,0:T(8,128)(2,1)S(1)} collective-permute-done((bf16[480,128]{1,0:T(8,128)(2,1)S(1)}, bf16[480,128]{1,0:T(8,128)(2,1)S(1)}, u32[]{:S(2)}, u32[]{:S(2)}) %collective-permute-start) | collective-permute-done | bytes 122912 | tf_op jit(solution)/shard_map/ppermute | solution.py:46
  11.6 0.3 collective-permute-done.1
  12.0 0.1 maximum_select_fusion
  12.1 1.6 %collective-permute-start.2 = (bf16[6,76,128]{2,1,0:T(8,128)(2,1)S(1)}, bf16[6,76,128]{2,1,0:T(8,128)(2,1)S(1)}, u32[]{:S(2)}, u32[]{:S(2)}) collective-permute-start(bf16[6,76,128]{2,1,0:T(8,128)(2,1)S(1)} %maximum_select_fusion), channel_id=1, source_target_pairs={{0,4},{4,0},{1,5},{5,1},{2,6},{6,2},{3,7},{7,3},{8,12},{12,8},{9,1... | collective-permute-start | bytes 350216 | tf_op jit(solution)/shard_map/ppermute | solution.py:46
  13.6 0.0 collective-permute-done.3
  13.7 3.5 %collective-permute-done.2 = bf16[6,76,128]{2,1,0:T(8,128)(2,1)S(1)} collective-permute-done((bf16[6,76,128]{2,1,0:T(8,128)(2,1)S(1)}, bf16[6,76,128]{2,1,0:T(8,128)(2,1)S(1)}, u32[]{:S(2)}, u32[]{:S(2)}) %collective-permute-start.2) | collective-permute-done | bytes 116768 | tf_op jit(solution)/shard_map/ppermute | solution.py:46
  17.2 0.1 maximum_select_fusion.1
  17.2 0.2 broadcast_in_dim.26.sea
  17.5 6.0 %forward.1 = (bf16[16,64,128]{2,1,0:T(8,128)(2,1)}, bf16[16,64,128]{2,1,0:T(8,128)(2,1)S(1)}, f32[520,128]{1,0:T(8,128)S(1)}, f32[28,80,128]{2,1,0:T(8,128)S(1)}, f32[16,64,128]{2,1,0:T(8,128)S(1)}) custom-call(bf16[6,76,128]{2,1,0:T(8,128)(2,1)S(1)} %get-tuple-element.43.south, bf16[16,64,128]{2,1,0:T(8,128)(2,1)S(1)} %bitcast.15, ...), custom_call_target="tpu_custom_call" | custom-call | flops 513802240 | bytes 3687936 | tf_op jit(solution)/shard_map/forward/pallas_call | solution.py:323
  23.6 1.9 %kernel_gradient.1 = (f32[288,128]{1,0:T(8,128)S(1)}, bf16[288,128]{1,0:T(8,128)(2,1)S(1)}) custom-call(s32[1]{0:T(128)} %bitcast.11.odd, f32[28,80,128]{2,1,0:T(8,128)S(1)} %get-tuple-element.19.wide, f32[16,64,128]{2,1,0:T(8,128)S(1)} %get-tuple-element.20.mixed, f32[520,128]{1,0:T(8,128)S(1)} %get-tuple-element.21.parts), custom_call_target="tpu_custom_call" | custom-call | flops 128450560 | bytes 2158596 | tf_op jit(solution)/shard_map/kernel_gradient/pallas_call | solution.py:323
  25.5 0.1 collective-permute-start.8
  25.6 2.9 %collective-permute-start.7 = (bf16[6,6,128]{2,1,0:T(8,128)(2,1)S(1)}, bf16[6,6,128]{2,1,0:T(8,128)(2,1)S(1)}, u32[]{:S(2)}, u32[]{:S(2)}) collective-permute-start(bf16[6,6,128]{2,1,0:T(8,128)(2,1)S(1)} %broadcast_select_fusion.12), channel_id=1, source_target_pairs={{0,16},{8,24},{16,0},{24,8},{1,17},{9,25},{17,1},{25,9},{2,18},{10... | collective-permute-start | bytes 27656 | tf_op jit(solution)/shard_map/ppermute | solution.py:46
  28.6 1.3 %collective-permute-start.4 = (bf16[480,128]{1,0:T(8,128)(2,1)S(1)}, bf16[480,128]{1,0:T(8,128)(2,1)S(1)}, u32[]{:S(2)}, u32[]{:S(2)}) collective-permute-start(bf16[480,128]{1,0:T(8,128)(2,1)S(1)} %pad_maximum_fusion.1), channel_id=1, source_target_pairs={{0,24},{8,16},{16,8},{24,0},{1,25},{9,17},{17,9},{25,1},{2,26},{10... | collective-permute-start | bytes 368648 | tf_op jit(solution)/shard_map/ppermute | solution.py:46
  29.9 0.0 collective-permute-start.5
  29.9 0.4 collective-permute-done.7
  30.3 0.0 collective-permute-done.8
  30.3 2.9 %collective-permute-start.10 = (bf16[288,128]{1,0:T(8,128)(2,1)S(1)}, bf16[288,128]{1,0:T(8,128)(2,1)S(1)}, u32[]{:S(2)}, u32[]{:S(2)}) collective-permute-start(bf16[288,128]{1,0:T(8,128)(2,1)S(1)} %add_convert_fusion.1), channel_id=1, source_target_pairs={{0,16},{8,24},{16,0},{24,8},{1,17},{9,25},{17,1},{25,9},{2,18},{10... | collective-permute-start | bytes 221192 | tf_op jit(solution)/shard_map/ppermute | solution.py:100
  33.3 1.2 %collective-permute-start.11 = (bf16[288,128]{1,0:T(8,128)(2,1)S(1)}, bf16[288,128]{1,0:T(8,128)(2,1)S(1)}, u32[]{:S(2)}, u32[]{:S(2)}) collective-permute-start(bf16[288,128]{1,0:T(8,128)(2,1)S(1)} %add_convert_fusion.1), channel_id=1, source_target_pairs={{0,24},{8,16},{16,8},{24,0},{1,25},{9,17},{17,9},{25,1},{2,26},{10... | collective-permute-start | bytes 221192 | tf_op jit(solution)/shard_map/ppermute | solution.py:100
  34.5 2.3 %collective-permute-done.4 = bf16[480,128]{1,0:T(8,128)(2,1)S(1)} collective-permute-done((bf16[480,128]{1,0:T(8,128)(2,1)S(1)}, bf16[480,128]{1,0:T(8,128)(2,1)S(1)}, u32[]{:S(2)}, u32[]{:S(2)}) %collective-permute-start.4) | collective-permute-done | bytes 122912 | tf_op jit(solution)/shard_map/ppermute | solution.py:46
  36.8 0.0 collective-permute-done.5
  36.8 5.8 %collective-permute-done.10 = bf16[288,128]{1,0:T(8,128)(2,1)S(1)} collective-permute-done((bf16[288,128]{1,0:T(8,128)(2,1)S(1)}, bf16[288,128]{1,0:T(8,128)(2,1)S(1)}, u32[]{:S(2)}, u32[]{:S(2)}) %collective-permute-start.10) | collective-permute-done | bytes 73760 | tf_op jit(solution)/shard_map/ppermute | solution.py:100
  42.6 0.0 collective-permute-done.11
  42.6 1.6 %collective-permute-start.12 = (bf16[288,128]{1,0:T(8,128)(2,1)S(1)}, bf16[288,128]{1,0:T(8,128)(2,1)S(1)}, u32[]{:S(2)}, u32[]{:S(2)}) collective-permute-start(bf16[288,128]{1,0:T(8,128)(2,1)S(1)} %add_convert_fusion), channel_id=1, source_target_pairs={{0,2},{1,3},{2,0},{3,1},{4,6},{5,7},{6,4},{7,5},{8,10},{9,11},{10,... | collective-permute-start | bytes 221192 | tf_op jit(solution)/shard_map/ppermute | solution.py:100
  44.2 1.5 %collective-permute-start.13 = (bf16[288,128]{1,0:T(8,128)(2,1)S(1)}, bf16[288,128]{1,0:T(8,128)(2,1)S(1)}, u32[]{:S(2)}, u32[]{:S(2)}) collective-permute-start(bf16[288,128]{1,0:T(8,128)(2,1)S(1)} %add_convert_fusion), channel_id=1, source_target_pairs={{0,4},{4,0},{1,5},{5,1},{2,6},{6,2},{3,7},{7,3},{8,12},{12,8},{9,1... | collective-permute-start | bytes 221192 | tf_op jit(solution)/shard_map/ppermute | solution.py:100
  45.7 0.5 collective-permute-start.14
  46.2 0.1 maximum_select_fusion.2
  46.3 1.6 %collective-permute-start.6 = (bf16[6,76,128]{2,1,0:T(8,128)(2,1)S(1)}, bf16[6,76,128]{2,1,0:T(8,128)(2,1)S(1)}, u32[]{:S(2)}, u32[]{:S(2)}) collective-permute-start(bf16[6,76,128]{2,1,0:T(8,128)(2,1)S(1)} %maximum_select_fusion.2), channel_id=1, source_target_pairs={{0,4},{4,0},{1,5},{5,1},{2,6},{6,2},{3,7},{7,3},{8,12},{12,8},{9,1... | collective-permute-start | bytes 350216 | tf_op jit(solution)/shard_map/ppermute | solution.py:46
  47.8 0.0 collective-permute-done.12
  47.8 1.4 %collective-permute-done.13 = bf16[288,128]{1,0:T(8,128)(2,1)S(1)} collective-permute-done((bf16[288,128]{1,0:T(8,128)(2,1)S(1)}, bf16[288,128]{1,0:T(8,128)(2,1)S(1)}, u32[]{:S(2)}, u32[]{:S(2)}) %collective-permute-start.13) | collective-permute-done | bytes 73760 | tf_op jit(solution)/shard_map/ppermute | solution.py:100
  49.3 1.7 %collective-permute-done.14 = bf16[288,128]{1,0:T(8,128)(2,1)S(1)} collective-permute-done((bf16[288,128]{1,0:T(8,128)(2,1)S(1)}, bf16[288,128]{1,0:T(8,128)(2,1)S(1)}, u32[]{:S(2)}, u32[]{:S(2)}) %collective-permute-start.14) | collective-permute-done | bytes 73760 | tf_op jit(solution)/shard_map/ppermute | solution.py:100
  51.1 0.1 collective-permute-start.15
  51.1 0.2 collective-permute-done.6
  51.4 0.1 maximum_select_fusion.3
  51.5 2.9 %backward.1 = bf16[16,64,128]{2,1,0:T(8,128)(2,1)} custom-call(s32[1]{0:T(128)} %bitcast.7.northern, bf16[6,76,128]{2,1,0:T(8,128)(2,1)S(1)} %get-tuple-element.41.south, bf16[16,64,128]{2,1,0:T(8,128)(2,1)S(1)} %get-tuple-element.18.block, bf16[6,76,128]{2,1,0:T(8,128)(2,1)S(1)} %get-tuple-element.40.north, bf16[16,6,128]{2,1,0:T(8,128)(2,1)S(1)} %get-tuple-element.44.west, ...), custom_call_target="tpu_custom_call" | custom-call | flops 192675840 | bytes 1356292 | tf_op jit(solution)/shard_map/backward/pallas_call | solution.py:323
  54.3 0.0 collective-permute-done.15.back
  54.3 0.7 %final.1 = (f32[49,128]{1,0:T(8,128)}, f32[2,128]{1,0:T(2,128)}, f32[128,256]{1,0:T(8,128)}, f32[256,128]{1,0:T(8,128)}) custom-call(s32[1]{0:T(128)} %bitcast.11.odd, f32[288,128]{1,0:T(8,128)S(1)} %add_add_fusion.total, f32[288,128]{1,0:T(8,128)S(1)} %collective-permute-done.15.back), custom_call_target="tpu_custom_call" | custom-call | bytes 583172 | tf_op jit(solution)/shard_map/final/pallas_call | solution.py:323
  (43 shorter events, 0.6 us)
Async XLA Ops:
  2.6 14.9 %copy-start = (bf16[1,16,64,128]{3,2,1,0:T(8,128)(2,1)S(1)}, bf16[1,16,64,128]{3,2,1,0:T(8,128)(2,1)}, u32[]{:S(2)}) copy-start(bf16[1,16,64,128]{3,2,1,0:T(8,128)(2,1)} %param.9) | copy-start | bytes 786436
  2.6 14.9 %copy-start.1 = (bf16[1,16,64,128]{3,2,1,0:T(8,128)(2,1)S(1)}, bf16[1,16,64,128]{3,2,1,0:T(8,128)(2,1)}, u32[]{:S(2)}) copy-start(bf16[1,16,64,128]{3,2,1,0:T(8,128)(2,1)} %param.8) | copy-start | bytes 786436
  2.6 14.9 %copy-start.2 = (f32[49,128]{1,0:T(8,128)S(1)}, f32[49,128]{1,0:T(8,128)}, u32[]{:S(2)}) copy-start(f32[49,128]{1,0:T(8,128)} %taps.3) | copy-start | bytes 75268
  2.6 14.9 %copy-start.3 = (bf16[128,256]{1,0:T(8,128)(2,1)S(1)}, bf16[128,256]{1,0:T(8,128)(2,1)}, u32[]{:S(2)}) copy-start(bf16[128,256]{1,0:T(8,128)(2,1)} %up.1) | copy-start | bytes 196612
  2.6 14.9 %copy-start.4 = (bf16[256,128]{1,0:T(8,128)(2,1)S(1)}, bf16[256,128]{1,0:T(8,128)(2,1)}, u32[]{:S(2)}) copy-start(bf16[256,128]{1,0:T(8,128)(2,1)} %down.1) | copy-start | bytes 196612
  2.6 14.9 %copy-start.5 = (f32[128]{0:T(128)S(1)}, f32[128]{0:T(128)}, u32[]{:S(2)}) copy-start(f32[128]{0:T(128)} %param.12) | copy-start | bytes 1540
  2.6 14.9 %copy-start.6 = (f32[128]{0:T(128)S(1)}, f32[128]{0:T(128)}, u32[]{:S(2)}) copy-start(f32[128]{0:T(128)} %param.13) | copy-start | bytes 1540
  2.7 8.9 %collective-permute-start = (bf16[480,128]{1,0:T(8,128)(2,1)S(1)}, bf16[480,128]{1,0:T(8,128)(2,1)S(1)}, u32[]{:S(2)}, u32[]{:S(2)}) collective-permute-start(bf16[480,128]{1,0:T(8,128)(2,1)S(1)} %pad_maximum_fusion), channel_id=1, source_target_pairs={{0,24},{8,16},{16,8},{24,0},{1,25},{9,17},{17,9},{25,1},{2,26},{10... | collective-permute-start | bytes 368648 | tf_op jit(solution)/shard_map/ppermute | solution.py:46
  7.8 4.1 %collective-permute-start.1 = (bf16[16,6,128]{2,1,0:T(8,128)(2,1)S(1)}, bf16[16,6,128]{2,1,0:T(8,128)(2,1)S(1)}, u32[]{:S(2)}, u32[]{:S(2)}) collective-permute-start(bf16[16,6,128]{2,1,0:T(8,128)(2,1)S(1)} %get-tuple-element.39), channel_id=1, source_target_pairs={{0,8},{8,0},{16,24},{24,16},{1,9},{9,1},{17,25},{25,17},{2,10},{10... | collective-permute-start | bytes 73736 | tf_op jit(solution)/shard_map/ppermute | solution.py:46
  7.9 5.7 %collective-permute-start.3 = (bf16[6,6,128]{2,1,0:T(8,128)(2,1)S(1)}, bf16[6,6,128]{2,1,0:T(8,128)(2,1)S(1)}, u32[]{:S(2)}, u32[]{:S(2)}) collective-permute-start(bf16[6,6,128]{2,1,0:T(8,128)(2,1)S(1)} %broadcast_select_fusion.16), channel_id=1, source_target_pairs={{0,16},{8,24},{16,0},{24,8},{1,17},{9,25},{17,1},{25,9},{2,18},{10... | collective-permute-start | bytes 27656 | tf_op jit(solution)/shard_map/ppermute | solution.py:46
  12.1 5.1 %collective-permute-start.2 = (bf16[6,76,128]{2,1,0:T(8,128)(2,1)S(1)}, bf16[6,76,128]{2,1,0:T(8,128)(2,1)S(1)}, u32[]{:S(2)}, u32[]{:S(2)}) collective-permute-start(bf16[6,76,128]{2,1,0:T(8,128)(2,1)S(1)} %maximum_select_fusion), channel_id=1, source_target_pairs={{0,4},{4,0},{1,5},{5,1},{2,6},{6,2},{3,7},{7,3},{8,12},{12,8},{9,1... | collective-permute-start | bytes 350216 | tf_op jit(solution)/shard_map/ppermute | solution.py:46
  25.5 4.8 %collective-permute-start.8 = (bf16[288,128]{1,0:T(8,128)(2,1)S(1)}, bf16[288,128]{1,0:T(8,128)(2,1)S(1)}, u32[]{:S(2)}, u32[]{:S(2)}) collective-permute-start(bf16[288,128]{1,0:T(8,128)(2,1)S(1)} %get-tuple-element.23), channel_id=1, source_target_pairs={{0,1},{1,0},{2,3},{3,2},{4,5},{5,4},{6,7},{7,6},{8,9},{9,8},{10,11... | collective-permute-start | bytes 221192 | tf_op jit(solution)/shard_map/ppermute | solution.py:100
  25.6 4.7 %collective-permute-start.7 = (bf16[6,6,128]{2,1,0:T(8,128)(2,1)S(1)}, bf16[6,6,128]{2,1,0:T(8,128)(2,1)S(1)}, u32[]{:S(2)}, u32[]{:S(2)}) collective-permute-start(bf16[6,6,128]{2,1,0:T(8,128)(2,1)S(1)} %broadcast_select_fusion.12), channel_id=1, source_target_pairs={{0,16},{8,24},{16,0},{24,8},{1,17},{9,25},{17,1},{25,9},{2,18},{10... | collective-permute-start | bytes 27656 | tf_op jit(solution)/shard_map/ppermute | solution.py:46
  28.6 8.1 %collective-permute-start.4 = (bf16[480,128]{1,0:T(8,128)(2,1)S(1)}, bf16[480,128]{1,0:T(8,128)(2,1)S(1)}, u32[]{:S(2)}, u32[]{:S(2)}) collective-permute-start(bf16[480,128]{1,0:T(8,128)(2,1)S(1)} %pad_maximum_fusion.1), channel_id=1, source_target_pairs={{0,24},{8,16},{16,8},{24,0},{1,25},{9,17},{17,9},{25,1},{2,26},{10... | collective-permute-start | bytes 368648 | tf_op jit(solution)/shard_map/ppermute | solution.py:46
  29.9 6.9 %collective-permute-start.5 = (bf16[16,6,128]{2,1,0:T(8,128)(2,1)S(1)}, bf16[16,6,128]{2,1,0:T(8,128)(2,1)S(1)}, u32[]{:S(2)}, u32[]{:S(2)}) collective-permute-start(bf16[16,6,128]{2,1,0:T(8,128)(2,1)S(1)} %get-tuple-element.33), channel_id=1, source_target_pairs={{0,8},{8,0},{16,24},{24,16},{1,9},{9,1},{17,25},{25,17},{2,10},{10... | collective-permute-start | bytes 73736 | tf_op jit(solution)/shard_map/ppermute | solution.py:46
  30.3 12.3 %collective-permute-start.10 = (bf16[288,128]{1,0:T(8,128)(2,1)S(1)}, bf16[288,128]{1,0:T(8,128)(2,1)S(1)}, u32[]{:S(2)}, u32[]{:S(2)}) collective-permute-start(bf16[288,128]{1,0:T(8,128)(2,1)S(1)} %add_convert_fusion.1), channel_id=1, source_target_pairs={{0,16},{8,24},{16,0},{24,8},{1,17},{9,25},{17,1},{25,9},{2,18},{10... | collective-permute-start | bytes 221192 | tf_op jit(solution)/shard_map/ppermute | solution.py:100
  33.3 9.3 %collective-permute-start.11 = (bf16[288,128]{1,0:T(8,128)(2,1)S(1)}, bf16[288,128]{1,0:T(8,128)(2,1)S(1)}, u32[]{:S(2)}, u32[]{:S(2)}) collective-permute-start(bf16[288,128]{1,0:T(8,128)(2,1)S(1)} %add_convert_fusion.1), channel_id=1, source_target_pairs={{0,24},{8,16},{16,8},{24,0},{1,25},{9,17},{17,9},{25,1},{2,26},{10... | collective-permute-start | bytes 221192 | tf_op jit(solution)/shard_map/ppermute | solution.py:100
  34.5 8.1 %collective-permute-start.9 = (bf16[288,128]{1,0:T(8,128)(2,1)S(1)}, bf16[288,128]{1,0:T(8,128)(2,1)S(1)}, u32[]{:S(2)}, u32[]{:S(2)}) collective-permute-start(bf16[288,128]{1,0:T(8,128)(2,1)S(1)} %add_convert_fusion.1), channel_id=1, source_target_pairs={{0,8},{8,0},{16,24},{24,16},{1,9},{9,1},{17,25},{25,17},{2,10},{10... | collective-permute-start | bytes 221192 | tf_op jit(solution)/shard_map/ppermute | solution.py:100
  42.6 5.2 %collective-permute-start.12 = (bf16[288,128]{1,0:T(8,128)(2,1)S(1)}, bf16[288,128]{1,0:T(8,128)(2,1)S(1)}, u32[]{:S(2)}, u32[]{:S(2)}) collective-permute-start(bf16[288,128]{1,0:T(8,128)(2,1)S(1)} %add_convert_fusion), channel_id=1, source_target_pairs={{0,2},{1,3},{2,0},{3,1},{4,6},{5,7},{6,4},{7,5},{8,10},{9,11},{10,... | collective-permute-start | bytes 221192 | tf_op jit(solution)/shard_map/ppermute | solution.py:100
  44.2 5.0 %collective-permute-start.13 = (bf16[288,128]{1,0:T(8,128)(2,1)S(1)}, bf16[288,128]{1,0:T(8,128)(2,1)S(1)}, u32[]{:S(2)}, u32[]{:S(2)}) collective-permute-start(bf16[288,128]{1,0:T(8,128)(2,1)S(1)} %add_convert_fusion), channel_id=1, source_target_pairs={{0,4},{4,0},{1,5},{5,1},{2,6},{6,2},{3,7},{7,3},{8,12},{12,8},{9,1... | collective-permute-start | bytes 221192 | tf_op jit(solution)/shard_map/ppermute | solution.py:100
  45.7 5.3 %collective-permute-start.14 = (bf16[288,128]{1,0:T(8,128)(2,1)S(1)}, bf16[288,128]{1,0:T(8,128)(2,1)S(1)}, u32[]{:S(2)}, u32[]{:S(2)}) collective-permute-start(bf16[288,128]{1,0:T(8,128)(2,1)S(1)} %add_convert_fusion), channel_id=1, source_target_pairs={{0,6},{1,7},{2,4},{3,5},{4,2},{5,3},{6,0},{7,1},{8,14},{9,15},{10,... | collective-permute-start | bytes 221192 | tf_op jit(solution)/shard_map/ppermute | solution.py:100
  46.3 5.1 %collective-permute-start.6 = (bf16[6,76,128]{2,1,0:T(8,128)(2,1)S(1)}, bf16[6,76,128]{2,1,0:T(8,128)(2,1)S(1)}, u32[]{:S(2)}, u32[]{:S(2)}) collective-permute-start(bf16[6,76,128]{2,1,0:T(8,128)(2,1)S(1)} %maximum_select_fusion.2), channel_id=1, source_target_pairs={{0,4},{4,0},{1,5},{5,1},{2,6},{6,2},{3,7},{7,3},{8,12},{12,8},{9,1... | collective-permute-start | bytes 350216 | tf_op jit(solution)/shard_map/ppermute | solution.py:46
  51.1 3.3 %collective-permute-start.15 = (f32[288,128]{1,0:T(8,128)S(1)}, f32[288,128]{1,0:T(8,128)S(1)}, u32[]{:S(2)}, u32[]{:S(2)}) collective-permute-start(f32[288,128]{1,0:T(8,128)S(1)} %add_add_fusion.total), channel_id=1, source_target_pairs={{0,1},{1,0},{2,3},{3,2},{4,5},{5,4},{6,7},{7,6},{8,9},{9,8},{10,11... | collective-permute-start | bytes 442376 | tf_op jit(solution)/shard_map/ppermute | solution.py:100

commit v3 on v2

--- a/solution.py
+++ b/solution.py
@@ -46,50 +46,55 @@
     return lax.ppermute(value, axis, [(i, i ^ bits) for i in range(lax.axis_size(axis))])
 
 
-def columns(block, top):
-    count = lax.axis_size("lon")
-    first, last = block[:, :REACH], block[:, block.shape[1] - REACH :]
-    flipped = top[::-1, ::-1]
-    if count == 4:
-        even = lax.axis_index("lon") % 2 == 0
-        near, far = jnp.where(even, last, first), jnp.where(even, first, last)
-        corner = jnp.where(even, flipped[:, :REACH], flipped[:, flipped.shape[1] - REACH :])
-        own = jnp.where(even, flipped[:, flipped.shape[1] - REACH :], flipped[:, :REACH])
-        channels = block.shape[2]
-        cells = far.shape[0] * far.shape[1]
-        joint = jnp.concatenate([far.reshape(-1, channels), flipped.reshape(-1, channels)])
-        joint = xor_partner(joint, "lon", 3)
-        corner = xor_partner(corner, "lon", 2)
-        near = xor_partner(near, "lon", 1)
-        far, folded = joint[:cells].reshape(far.shape), joint[cells:].reshape(flipped.shape)
-        west, east = jnp.where(even, far, near), jnp.where(even, near, far)
-        sides = [jnp.where(even, own, corner), folded, jnp.where(even, corner, own)]
-        return west, east, jnp.concatenate(sides, 1)
-    ring = [(i, (i + 1) % count) for i in range(count)]
-    back = [(j, i) for i, j in ring]
-    folded = lax.ppermute(flipped, "lon", [(i, count - 1 - i) for i in range(count)])
-    west, east = lax.ppermute(last, "lon", ring), lax.ppermute(first, "lon", back)
-    left = lax.ppermute(folded[:, folded.shape[1] - REACH :], "lon", ring)
-    right = lax.ppermute(folded[:, :REACH], "lon", back)
-    return west, east, jnp.concatenate([left, folded, right], 1)
-
-
-def extend(block):
-    count = lax.axis_size("lat")
-    top, bottom = block[block.shape[0] - REACH :], block[:REACH]
-    west, east, folded = columns(block, top)
-    northern = is_northern()
-    top = jnp.concatenate([west[-REACH:], top, east[-REACH:]], 1)
-    bottom = jnp.concatenate([west[:REACH], bottom, east[:REACH]], 1)
-    if count == 2:
+def across(block):
+    lats, lons = lax.axis_size("lat"), lax.axis_size("lon")
+    top, bottom, northern = block[block.shape[0] - REACH :], block[:REACH], is_northern()
+    folded = lax.ppermute(top[::-1, ::-1], "lon", [(i, lons - 1 - i) for i in range(lons)])
+    if lats == 2:
         facing = xor_partner(jnp.where(northern, bottom, top), "lat", 1)
-        south = jnp.where(northern, facing, jnp.zeros_like(facing))
-        north = jnp.where(northern, folded, facing)
-    else:
-        south = lax.ppermute(top, "lat", [(i, i + 1) for i in range(count - 1)])
-        above = lax.ppermute(bottom, "lat", [(i + 1, i) for i in range(count - 1)])
-        north = jnp.where(northern, folded, above)
-    return south, north, west, east
+        return facing, facing, folded
+    below = lax.ppermute(top, "lat", [(i, i + 1) for i in range(lats - 1)])
+    return below, lax.ppermute(bottom, "lat", [(i + 1, i) for i in range(lats - 1)]), folded
+
+
+def sides_kernel(flags, below, above, folded, block, *refs):
+    south, north, first, last = refs[-4:]
+    rows, cols = block.shape[0], block.shape[1]
+    northern, swap = flags[0] == 1, flags[1] == 1
+
+    def put(row, value):
+        head, tail = value[:REACH], value[cols - REACH :]
+        first[row] = jnp.where(swap, tail, head).astype(BF16)
+        last[row] = jnp.where(swap, head, tail).astype(BF16)
+
+    for r in range(REACH):
+        low = below[r].astype(F32)
+        low = jnp.where(flags[2] == 1, low, 0.0)
+        high = jnp.where(northern, folded[r].astype(F32), above[r].astype(F32))
+        south[r], north[r] = low.astype(BF16), high.astype(BF16)
+        put(r, low)
+        put(REACH + rows + r, high)
+    for r in range(rows):
+        put(REACH + r, block[r].astype(F32))
+
+
+def along(rows_in, block, *after):
+    lons = lax.axis_size("lon")
+    rows, cols, channels = block.shape
+    pairs = lons == 4
+    odd = lax.axis_index("lon") % 2 if pairs else 0
+    flags = jnp.stack([is_northern().astype(jnp.int32), jnp.asarray(odd, jnp.int32), (lax.axis_index("lat") > 0).astype(jnp.int32)])
+    shape = jax.ShapeDtypeStruct
+    strip, side = shape((REACH, cols, channels), BF16), shape((rows + 2 * REACH, REACH, channels), BF16)
+    south, north, first, last = call(
+        sides_kernel, (strip, strip, side, side), (flags, *rows_in, block, *after), flags=1, name="sides"
+    )
+    if pairs:
+        far, near = xor_partner(first, "lon", 3), xor_partner(last, "lon", 1)
+        return south, north, jnp.where(odd == 0, far, near), jnp.where(odd == 0, near, far)
+    ring = [(i, (i + 1) % lons) for i in range(lons)]
+    west = lax.ppermute(last, "lon", ring)
+    return south, north, west, lax.ppermute(first, "lon", [(j, i) for i, j in ring])
 
 
 def partners(value, bits):
@@ -100,43 +105,45 @@
     return lax.ppermute(value, axes, route(axes, lambda *at: [i ^ flip[a] for a, i in zip(axes, at)]))
 
 
-def summed(mine, other):
-    axes = ("ens", "lon", "lat")
-    bits = [(a, 1 << b) for a in axes for b in range(lax.axis_size(a).bit_length() - 1)]
-    total = mine + partners(other, bits[:1]).astype(F32)
-    rest = bits[2:4] + bits[1:2] + bits[4:] if lax.axis_size("lon") == 4 else bits[1:]
-    while rest:
-        pair, rest = rest[:2], rest[2:]
-        sent = total.astype(BF16)
-        if len(pair) == 2:
-            far = partners(sent, pair)
-            one, two = partners(sent, pair[:1]), partners(sent, pair[1:])
-            total = (sent.astype(F32) + one.astype(F32)) + (two.astype(F32) + far.astype(F32))
-        else:
-            total = sent.astype(F32) + partners(sent, pair).astype(F32)
-    return total, partners(total, bits[:1])
-
-
-def fill(wide, south, block, north, west, east, sea=None):
+def add_kernel(*refs):
+    refs[-1][...] = added([ref[...] for ref in refs[:-2]])
+
+
+def stages():
+    bits = {a: [(a, 1 << b) for b in range(lax.axis_size(a).bit_length() - 1)] for a in ("ens", "lat", "lon")}
+    rest = bits["ens"][1:] + bits["lat"] + bits["lon"]
+    return bits["ens"][:1], [rest[n : n + 2] for n in range(0, len(rest), 2)]
+
+
+def stage(total, pair):
+    sent = total.astype(BF16)
+    if len(pair) == 1:
+        return [sent, partners(sent, pair)]
+    far = partners(sent, pair)
+    return [sent, partners(sent, pair[:1]), partners(sent, pair[1:]), far]
+
+
+def added(values):
+    values = [v.astype(F32) for v in values]
+    return sum(values) if len(values) == 2 else (values[0] + values[1]) + (values[2] + values[3])
+
+
+def fill(wide, south, block, north, west, east):
     rows, cols = block.shape[0], block.shape[1]
-
-    def inner(r, carry):
-        value = block[r].astype(F32)
-        if sea is not None:
-            value = value * sea[r].astype(F32)
-        wide[REACH + r, LEFT : LEFT + cols] = value
-        wide[REACH + r, BASE:LEFT] = west[r].astype(F32)
-        wide[REACH + r, LEFT + cols : LEFT + cols + REACH] = east[r].astype(F32)
+    for ref, start, count in ((south, 0, REACH), (block, REACH, rows), (north, REACH + rows, REACH)):
+
+        def one(r, carry, ref=ref, start=start):
+            wide[start + r, LEFT : LEFT + cols] = ref[r].astype(F32)
+            return carry
+
+        lax.fori_loop(0, count, one, 0, unroll=2)
+
+    def sides(r, carry):
+        wide[r, BASE:LEFT] = west[r].astype(F32)
+        wide[r, LEFT + cols : LEFT + cols + REACH] = east[r].astype(F32)
         return carry
 
-    lax.fori_loop(0, rows, inner, 0, unroll=2)
-
-    def outer(r, carry):
-        wide[r, BASE : LEFT + cols + REACH] = south[r].astype(F32)
-        wide[REACH + rows + r, BASE : LEFT + cols + REACH] = north[r].astype(F32)
-        return carry
-
-    lax.fori_loop(0, REACH, outer, 0, unroll=2)
+    lax.fori_loop(0, rows + 2 * REACH, sides, 0, unroll=4)
 
 
 def conv(wide, tap, rows, cols, store):
@@ -166,13 +173,32 @@
     lax.fori_loop(0, 2, parity, 0)
 
 
+def mask_kernel(field, mask, masked, sea, state, ocean, sems):
+    rows, cols, channels = state.shape
+    copies = [pltpu.make_async_copy(field, state, sems.at[0]), pltpu.make_async_copy(mask, ocean, sems.at[1])]
+    for copy in copies:
+        copy.start()
+    copies[1].wait()
+    value = ocean[...].astype(BF16)
+    at = lax.broadcasted_iota(jnp.int32, (rows, channels), 0)
+    for r in range(rows):
+        pick = jnp.where(at == r, 1.0, 0.0).astype(BF16)
+        row = lax.dot_general(value, pick, (((0,), (0,)), ((), ())), preferred_element_type=F32)
+        sea[r] = row.astype(BF16)
+    copies[0].wait()
+    for r in range(rows):
+        masked[r] = state[r] * sea[r]
+
+
 def forward_kernel(south, block, north, west, east, cotangent, sea, taps, gain, shift, up, down,
-                   output, grad, parts, wide, mixed, spread):
+                   output, grad, parts, wide, mixed, spread, upstream, result, sems):
     rows, cols, channels = block.shape
     hidden = up.shape[1]
+    fetch = pltpu.make_async_copy(cotangent, upstream, sems.at[0])
+    fetch.start()
     for k in range(TAPS):
         spread[k] = jnp.broadcast_to(taps[k : k + 1], (LANE, channels))
-    fill(wide, south, block, north, west, east, sea)
+    fill(wide, south, block, north, west, east)
 
     def store(row, col, value):
         mixed[row, col : col + LANE] = value
@@ -185,6 +211,10 @@
     cells = lines * cols
     nt = (((1,), (1,)), ((), ()))
     tn = (((0,), (0,)), ((), ()))
+
+    def send(n):
+        at = pl.ds(n * lines, lines)
+        return pltpu.make_async_copy(result.at[at], output.at[at], sems.at[1 + n])
 
     def chunk(n, carry):
         up_sum, down_sum, gain_sum, shift_sum = carry
@@ -202,8 +232,9 @@
         product = jnp.dot(activated, down_w, preferred_element_type=F32)
         ocean = sea[at].reshape(cells, channels).astype(F32)
         state = block[at].reshape(cells, channels).astype(F32)
-        output[at] = ((state + product) * ocean).astype(BF16).reshape(lines, cols, channels)
-        above = (cotangent[at] * sea[at]).reshape(cells, channels)
+        result[at] = ((state + product) * ocean).astype(BF16).reshape(lines, cols, channels)
+        send(n).start()
+        above = (upstream[at] * sea[at]).reshape(cells, channels)
         down_sum = down_sum + lax.dot_general(above, activated, tn, preferred_element_type=F32)
         act_grad = lax.dot_general(above, down_w, nt, preferred_element_type=F32)
         deriv = gate + pre * (gate * (1.0 - tanh)) * (SLOPE + (3.0 * SLOPE * CUBIC) * square)
@@ -214,13 +245,14 @@
         shift_sum = shift_sum + jnp.sum(norm_in.reshape(cells // LANE, LANE, channels), 0)
         scaled = norm_in * gain_v
         inner = jnp.mean(scaled * unit, -1, keepdims=True)
-        result = rstd * (scaled - jnp.mean(scaled, -1, keepdims=True) - unit * inner)
-        mixed[at] = result.reshape(lines, cols, channels)
-        grad[at] = result.astype(BF16).reshape(lines, cols, channels)
+        moved = rstd * (scaled - jnp.mean(scaled, -1, keepdims=True) - unit * inner)
+        mixed[at] = moved.reshape(lines, cols, channels)
+        grad[at] = moved.astype(BF16).reshape(lines, cols, channels)
         return up_sum, down_sum, gain_sum, shift_sum
 
     big = jnp.zeros((channels, hidden), F32)
     small = jnp.zeros((LANE, channels), F32)
+    fetch.wait()
     up_sum, down_sum, gain_sum, shift_sum = lax.fori_loop(
         0, rows // lines, chunk, (big, big, small, small)
     )
@@ -230,6 +262,8 @@
         parts[start : start + channels] = up_sum[:, n * channels : (n + 1) * channels]
     sums = [jnp.sum(gain_sum, 0, keepdims=True), jnp.sum(shift_sum, 0, keepdims=True)]
     parts[2 * hidden :] = jnp.concatenate(sums + [jnp.zeros((LANE - 2, channels), F32)], 0)
+    for n in range(rows // lines):
+        send(n).wait()
 
 
 def kernel_kernel(odd, wide, mixed, parts, mine, other):
@@ -297,7 +331,7 @@
 
 
 def backward_kernel(northern, south, block, north, west, east, cotangent, sea, taps,
-                    field_grad, wide, spread, folded):
+                    field_grad, token, wide, spread, folded):
     rows, cols, channels = block.shape
     for k in range(TAPS):
         flipped = jnp.broadcast_to(taps[TAPS - 1 - k : TAPS - k], (LANE, channels))
@@ -315,16 +349,18 @@
         field_grad[at] = ((cotangent[at].astype(F32) + value) * sea[at].astype(F32)).astype(BF16)
 
     conv(wide, tap, rows, cols, store)
-
-
-def call(kernel, outs, operands, scratch=(), flags=0, work=0, name=None):
+    token[...] = jnp.zeros_like(token)
+
+
+def call(kernel, outs, operands, scratch=(), flags=0, far=(), far_outs=(), work=0, name=None):
     vmem, smem = pl.BlockSpec(memory_space=pltpu.VMEM), pl.BlockSpec(memory_space=pltpu.SMEM)
+    anywhere = pl.BlockSpec(memory_space=pl.ANY)
     moved = sum(math.prod(a.shape) * a.dtype.itemsize for a in (*operands, *outs))
     return pl.pallas_call(
         kernel,
         out_shape=outs,
-        in_specs=[smem] * flags + [vmem] * (len(operands) - flags),
-        out_specs=[vmem] * len(outs),
+        in_specs=[smem if n < flags else anywhere if n in far else vmem for n in range(len(operands))],
+        out_specs=[anywhere if n in far_outs else vmem for n in range(len(outs))],
         scratch_shapes=scratch,
         compiler_params=pltpu.CompilerParams(vmem_limit_bytes=24 * 1024 * 1024),
         cost_estimate=pl.CostEstimate(flops=work, bytes_accessed=moved, transcendentals=0),
@@ -336,44 +372,60 @@
     rows, cols, channels = field.shape[1:]
     hidden = up_weight.shape[1]
     shape = jax.ShapeDtypeStruct
-    sea = jnp.broadcast_to(land_mask.astype(BF16)[:, :, None], (rows, cols, channels))
-    state = field[0]
-    south, north, west, east = extend(state * sea)
     tile = (rows, cols, channels)
+    near = pltpu.VMEM(tile, BF16)
+    state, sea = call(
+        mask_kernel,
+        (shape(tile, BF16), shape(tile, BF16)),
+        (field[0], land_mask),
+        [near, pltpu.VMEM((rows, cols), jnp.int32), pltpu.SemaphoreType.DMA((2,))],
+        far=(0, 1),
+        work=10**9,
+        name="mask",
+    )
+    south, north, west, east = along(across(state), state)
     wide = (rows + 2 * REACH, cols + 2 * LEFT, channels)
     spread = pltpu.VMEM((TAPS, LANE, channels), F32)
     half = hidden + 32
-    macs = TAPS * rows * cols * channels
     odd = (lax.axis_index("ens") % 2).astype(jnp.int32)[None]
     northern = is_northern().astype(jnp.int32)[None]
     output, grad, parts, widened, mixed_grad = call(
         forward_kernel,
         (shape(tile, BF16), shape(tile, BF16), shape((2 * hidden + LANE, channels), F32), shape(wide, F32), shape(tile, F32)),
         (south, state, north, west, east, cotangent[0], sea, kernel_taps, norm_gain[None], norm_shift[None], up_weight, down_weight),
-        [spread],
-        work=80 * macs,
+        [spread, near, near, pltpu.SemaphoreType.DMA((1 + rows,))],
+        far=(5,),
+        far_outs=(0,),
+        work=6 * 10**9,
         name="forward",
     )
+    crossed = across(grad)
     mine, other = call(
         kernel_kernel,
         (shape((half, channels), F32), shape((half, channels), BF16)),
         (odd, widened, mixed_grad, parts),
         flags=1,
-        work=20 * macs,
+        work=2 * 10**9,
         name="kernel_gradient",
     )
-    south, north, west, east = extend(grad)
-    (field_grad,) = call(
+    core, rest = stages()
+    total = mine + partners(other, core).astype(F32)
+    values = stage(total, rest[0])
+    south, north, west, east = along(crossed, grad, values[-1])
+    for pair in rest[1:]:
+        values = stage(added(values), pair)
+    field_grad, token = call(
         backward_kernel,
-        (shape(tile, BF16),),
+        (shape(tile, BF16), shape((LANE, channels), F32)),
         (northern, south, grad, north, west, east, cotangent[0], sea, kernel_taps),
         [pltpu.VMEM(wide, F32), spread, spread],
         flags=1,
-        work=30 * macs,
+        work=3 * 10**9,
         name="backward",
     )
+    (total,) = call(add_kernel, (shape(mine.shape, F32),), (*values, token), name="add")
+    back = partners(total, core)
     count = rows * cols * lax.axis_size("lon") * lax.axis_size("lat") * lax.axis_size("ens")
-    total, back = summed(mine, other)
     kernel_grad, norm_grad, up_grad, down_grad = call(
         functools.partial(final_kernel, factor=1.0 / math.sqrt(count)),
         (shape((TAPS, channels), F32), shape((2, channels), F32), shape((channels, hidden), F32), shape((hidden, channels), F32)),

time: 55.3 us -> 52.8 us (0.955)
  waiting for transfers between devices: 18.6 us -> 14.3 us
  other arithmetic: 2.37 us -> 0.21 us
  Pallas kernels: 11.5 us -> 13.3 us
  local copies, waits for them, and re-layouts: 0.62 us -> 1.77 us
  starting transfers between devices: 21 us -> 22.1 us
    ppermute x0 -> x2, starting transfers between devices: none -> 7.03 us  [across(): lax.ppermute(top[::-1, ::-1], 'lon', [(i, lons - 1 - i) for i in range(lo...]
    ppermute x8 -> x6, starting transfers between devices: 13.1 us -> 6.97 us  [xor_partner(): lax.ppermute(value, axis, [(i, i ^ bits) for i in range(lax.axis_size(axi...]
    ppermute x8, waiting for transfers between devices: 8.95 us -> 4.41 us  [partners(): lax.ppermute(value, axes, route(axes, lambda *at: [i ^ flip[a] for a, i i...]
    pallas_call x4 -> x8, Pallas kernels: 11.5 us -> 13.3 us  [call(): pl.pallas_call(kernel, out_shape=outs, in_specs=[smem if n < flags else a...]
    unnamed x14 -> x16, local copies, waits for them, and re-layouts: 0.04 us -> 1.68 us
    ppermute x0 -> x2, waiting for transfers between devices: none -> 1.37 us  [across(): lax.ppermute(top[::-1, ::-1], 'lon', [(i, lons - 1 - i) for i in range(lo...]
    ppermute x8 -> x6, waiting for transfers between devices: 9.68 us -> 8.5 us  [xor_partner(): lax.ppermute(value, axis, [(i, i ^ bits) for i in range(lax.axis_size(axi...]
    mul x1 -> x0, other arithmetic: 1.15 us -> none  [shards(): south, north, west, east = extend(state * sea)]
  transfers between devices with their start and end apart: 16 -> 16, of which waited for: 9 -> 8; matrix products, arithmetic and copies ran while one was open for 1% -> 0% of each run, Pallas kernels for 5% -> 7%
where the time goes in v3:
time: 52.8 us; the launch traced here: 52.6 us
  starting transfers between devices  22.1 us (42%)
  waiting for transfers between devices  14.3 us (27%)
  Pallas kernels  13.3 us (25%)
  local copies, waits for them, and re-layouts  1.77 us (3%)
  between operations  0.85 us (2%)
    pallas_call x8, Pallas kernels, call(): pl.pallas_call(kernel, out_shape=outs, in_specs=[smem if n < flags else a...  13.3 us
    ppermute x6, waiting for transfers between devices, xor_partner(): lax.ppermute(value, axis, [(i, i ^ bits) for i in range(lax.axis_size(axi...  8.5 us
    ppermute x8, starting transfers between devices, partners(): lax.ppermute(value, axes, route(axes, lambda *at: [i ^ flip[a] for a, i i...  8.15 us
    ppermute x2, starting transfers between devices, across(): lax.ppermute(top[::-1, ::-1], 'lon', [(i, lons - 1 - i) for i in range(lo...  7.03 us
    ppermute x6, starting transfers between devices, xor_partner(): lax.ppermute(value, axis, [(i, i ^ bits) for i in range(lax.axis_size(axi...  6.97 us
    ppermute x8, waiting for transfers between devices, partners(): lax.ppermute(value, axes, route(axes, lambda *at: [i ^ flip[a] for a, i i...  4.41 us
    unnamed x16, local copies, waits for them, and re-layouts  1.68 us
    ppermute x2, waiting for transfers between devices, across(): lax.ppermute(top[::-1, ::-1], 'lon', [(i, lons - 1 - i) for i in range(lo...  1.37 us
  transfers between devices with their start and end apart: 16, of which 8 were waited for; matrix products, arithmetic and copies ran while one was open for 0% of the time, Pallas kernels for 7%

profile of v3, /device:TPU:0, one launch (start us, length us, event | category | flops | bytes accessed | tf_op | source)
XLA Modules:
  0.0 52.6 jit_solution(6470657944634412561)
XLA Ops:
  0.6 0.9 %copy-done = bf16[1,16,64,128]{3,2,1,0:T(8,128)(2,1)S(1)} copy-done((bf16[1,16,64,128]{3,2,1,0:T(8,128)(2,1)S(1)}, bf16[1,16,64,128]{3,2,1,0:T(8,128)(2,1)}, u32[]{:S(2)}) %copy-start) | copy-done | bytes 262168
  1.6 0.7 %copy-done.5 = s32[16,64]{1,0:T(8,128)S(1)} copy-done((s32[16,64]{1,0:T(8,128)S(1)}, s32[16,64]{1,0:T(8,128)}, u32[]{:S(2)}) %copy-start.5) | copy-done | bytes 4120
  2.3 0.4 mask.2
  2.7 0.0 copy-start.1
  2.7 0.0 copy-start.2
  2.7 0.0 copy-start.3
  2.7 0.0 copy-start.4
  2.7 0.0 copy-start.6
  2.7 0.0 copy-start.7
  2.8 5.1 %collective-permute-start.1 = (bf16[6,64,128]{2,1,0:T(8,128)(2,1)S(1)}, bf16[6,64,128]{2,1,0:T(8,128)(2,1)S(1)}, u32[]{:S(2)}, u32[]{:S(2)}) collective-permute-start(bf16[6,64,128]{2,1,0:T(8,128)(2,1)S(1)} %rev.6), channel_id=1, source_target_pairs={{0,24},{8,16},{16,8},{24,0},{1,25},{9,17},{17,9},{25,1},{2,26},{10... | collective-permute-start | bytes 294920 | tf_op jit(solution)/shard_map/ppermute | solution.py:52
  7.9 1.5 %collective-permute-start = (bf16[6,64,128]{2,1,0:T(8,128)(2,1)S(1)}, bf16[6,64,128]{2,1,0:T(8,128)(2,1)S(1)}, u32[]{:S(2)}, u32[]{:S(2)}) collective-permute-start(bf16[6,64,128]{2,1,0:T(8,128)(2,1)S(1)} %get-tuple-element.55), channel_id=1, source_target_pairs={{0,4},{4,0},{1,5},{5,1},{2,6},{6,2},{3,7},{7,3},{8,12},{12,8},{9,1... | collective-permute-start | bytes 294920 | tf_op jit(solution)/shard_map/ppermute | solution.py:46
  9.4 0.1 pad_add_fusion.flags
  9.5 1.3 %collective-permute-done.1.folded = bf16[6,64,128]{2,1,0:T(8,128)(2,1)S(1)} collective-permute-done((bf16[6,64,128]{2,1,0:T(8,128)(2,1)S(1)}, bf16[6,64,128]{2,1,0:T(8,128)(2,1)S(1)}, u32[]{:S(2)}, u32[]{:S(2)}) %collective-permute-start.1) | collective-permute-done | bytes 98336 | tf_op jit(solution)/shard_map/ppermute | solution.py:52
  10.8 1.7 %collective-permute-done.below.above = bf16[6,64,128]{2,1,0:T(8,128)(2,1)S(1)} collective-permute-done((bf16[6,64,128]{2,1,0:T(8,128)(2,1)S(1)}, bf16[6,64,128]{2,1,0:T(8,128)(2,1)S(1)}, u32[]{:S(2)}, u32[]{:S(2)}) %collective-permute-start) | collective-permute-done | bytes 98336 | tf_op jit(solution)/shard_map/ppermute | solution.py:46
  12.5 0.6 %sides.2 = (bf16[6,64,128]{2,1,0:T(8,128)(2,1)S(1)}, bf16[6,64,128]{2,1,0:T(8,128)(2,1)S(1)}, bf16[28,6,128]{2,1,0:T(8,128)(2,1)S(1)}, bf16[28,6,128]{2,1,0:T(8,128)(2,1)S(1)}) custom-call(s32[3]{0:T(128)S(1)} %pad_add_fusion.flags, bf16[6,64,128]{2,1,0:T(8,128)(2,1)S(1)} %collective-permute-done.below.above, ...), custom_call_target="tpu_custom_call" | custom-call | bytes 839692 | tf_op jit(solution)/shard_map/sides/pallas_call | solution.py:359
  13.1 1.9 %collective-permute-start.2 = (bf16[28,6,128]{2,1,0:T(8,128)(2,1)S(1)}, bf16[28,6,128]{2,1,0:T(8,128)(2,1)S(1)}, u32[]{:S(2)}, u32[]{:S(2)}) collective-permute-start(bf16[28,6,128]{2,1,0:T(8,128)(2,1)S(1)} %get-tuple-element.32), channel_id=1, source_target_pairs={{0,24},{8,16},{16,8},{24,0},{1,25},{9,17},{17,9},{25,1},{2,26},{10... | collective-permute-start | bytes 129032 | tf_op jit(solution)/shard_map/ppermute | solution.py:46
  15.1 0.0 collective-permute-start.3
  15.1 4.2 %collective-permute-done.2 = bf16[28,6,128]{2,1,0:T(8,128)(2,1)S(1)} collective-permute-done((bf16[28,6,128]{2,1,0:T(8,128)(2,1)S(1)}, bf16[28,6,128]{2,1,0:T(8,128)(2,1)S(1)}, u32[]{:S(2)}, u32[]{:S(2)}) %collective-permute-start.2) | collective-permute-done | bytes 43040 | tf_op jit(solution)/shard_map/ppermute | solution.py:46
  19.2 0.6 %collective-permute-done.3 = bf16[28,6,128]{2,1,0:T(8,128)(2,1)S(1)} collective-permute-done((bf16[28,6,128]{2,1,0:T(8,128)(2,1)S(1)}, bf16[28,6,128]{2,1,0:T(8,128)(2,1)S(1)}, u32[]{:S(2)}, u32[]{:S(2)}) %collective-permute-start.3) | collective-permute-done | bytes 43040 | tf_op jit(solution)/shard_map/ppermute | solution.py:46
  19.9 6.1 %forward.1 = (bf16[16,64,128]{2,1,0:T(8,128)(2,1)}, bf16[16,64,128]{2,1,0:T(8,128)(2,1)S(1)}, f32[520,128]{1,0:T(8,128)S(1)}, f32[28,80,128]{2,1,0:T(8,128)S(1)}, f32[16,64,128]{2,1,0:T(8,128)S(1)}) custom-call(bf16[6,64,128]{2,1,0:T(8,128)(2,1)S(1)} %get-tuple-element.30.south, bf16[16,64,128]{2,1,0:T(8,128)(2,1)S(1)} %get-tuple-element.29.block, ...), custom_call_target="tpu_custom_call" | custom-call | flops 6000000000 | bytes 3687936 | tf_op jit(solution)/shard_map/forward/pallas_call | solution.py:359
  26.0 1.9 %kernel_gradient.1 = (f32[288,128]{1,0:T(8,128)S(1)}, bf16[288,128]{1,0:T(8,128)(2,1)S(1)}) custom-call(s32[1]{0:T(128)} %bitcast.8.odd, f32[28,80,128]{2,1,0:T(8,128)S(1)} %get-tuple-element.37.wide, f32[16,64,128]{2,1,0:T(8,128)S(1)} %get-tuple-element.38.mixed, f32[520,128]{1,0:T(8,128)S(1)} %get-tuple-element.39.parts), custom_call_target="tpu_custom_call" | custom-call | flops 2000000000 | bytes 2158596 | tf_op jit(solution)/shard_map/kernel_gradient/pallas_call | solution.py:359
  27.9 0.1 collective-permute-start.6
  28.0 1.9 %collective-permute-start.5 = (bf16[6,64,128]{2,1,0:T(8,128)(2,1)S(1)}, bf16[6,64,128]{2,1,0:T(8,128)(2,1)S(1)}, u32[]{:S(2)}, u32[]{:S(2)}) collective-permute-start(bf16[6,64,128]{2,1,0:T(8,128)(2,1)S(1)} %rev.7), channel_id=1, source_target_pairs={{0,24},{8,16},{16,8},{24,0},{1,25},{9,17},{17,9},{25,1},{2,26},{10... | collective-permute-start | bytes 294920 | tf_op jit(solution)/shard_map/ppermute | solution.py:52
  30.0 1.5 %collective-permute-start.4 = (bf16[6,64,128]{2,1,0:T(8,128)(2,1)S(1)}, bf16[6,64,128]{2,1,0:T(8,128)(2,1)S(1)}, u32[]{:S(2)}, u32[]{:S(2)}) collective-permute-start(bf16[6,64,128]{2,1,0:T(8,128)(2,1)S(1)} %get-tuple-element.53), channel_id=1, source_target_pairs={{0,4},{4,0},{1,5},{5,1},{2,6},{6,2},{3,7},{7,3},{8,12},{12,8},{9,1... | collective-permute-start | bytes 294920 | tf_op jit(solution)/shard_map/ppermute | solution.py:46
  31.5 0.0 collective-permute-done.6
  31.5 1.6 %collective-permute-start.7 = (bf16[288,128]{1,0:T(8,128)(2,1)S(1)}, bf16[288,128]{1,0:T(8,128)(2,1)S(1)}, u32[]{:S(2)}, u32[]{:S(2)}) collective-permute-start(bf16[288,128]{1,0:T(8,128)(2,1)S(1)} %add_convert_fusion.1), channel_id=1, source_target_pairs={{0,6},{1,7},{2,4},{3,5},{4,2},{5,3},{6,0},{7,1},{8,14},{9,15},{10,... | collective-permute-start | bytes 221192 | tf_op jit(solution)/shard_map/ppermute | solution.py:105
  33.1 1.5 %collective-permute-start.11 = (bf16[288,128]{1,0:T(8,128)(2,1)S(1)}, bf16[288,128]{1,0:T(8,128)(2,1)S(1)}, u32[]{:S(2)}, u32[]{:S(2)}) collective-permute-start(bf16[288,128]{1,0:T(8,128)(2,1)S(1)} %add_convert_fusion.1), channel_id=1, source_target_pairs={{0,4},{4,0},{1,5},{5,1},{2,6},{6,2},{3,7},{7,3},{8,12},{12,8},{9,1... | collective-permute-start | bytes 221192 | tf_op jit(solution)/shard_map/ppermute | solution.py:105
  34.6 0.5 collective-permute-start.10
  35.1 0.0 collective-permute-done.5.folded
  35.1 0.0 collective-permute-done.4.below.above
  35.1 3.0 %collective-permute-done.7.refs_0_ = bf16[288,128]{1,0:T(8,128)(2,1)S(1)} collective-permute-done((bf16[288,128]{1,0:T(8,128)(2,1)S(1)}, bf16[288,128]{1,0:T(8,128)(2,1)S(1)}, u32[]{:S(2)}, u32[]{:S(2)}) %collective-permute-start.7) | collective-permute-done | bytes 73760 | tf_op jit(solution)/shard_map/ppermute | solution.py:105
  38.1 0.6 %sides.3 = (bf16[6,64,128]{2,1,0:T(8,128)(2,1)S(1)}, bf16[6,64,128]{2,1,0:T(8,128)(2,1)S(1)}, bf16[28,6,128]{2,1,0:T(8,128)(2,1)S(1)}, bf16[28,6,128]{2,1,0:T(8,128)(2,1)S(1)}) custom-call(s32[3]{0:T(128)S(1)} %pad_add_fusion.flags, bf16[6,64,128]{2,1,0:T(8,128)(2,1)S(1)} %collective-permute-done.4.below.above, ...), custom_call_target="tpu_custom_call" | custom-call | bytes 913420 | tf_op jit(solution)/shard_map/sides/pallas_call | solution.py:359
  38.8 2.0 %collective-permute-start.8 = (bf16[28,6,128]{2,1,0:T(8,128)(2,1)S(1)}, bf16[28,6,128]{2,1,0:T(8,128)(2,1)S(1)}, u32[]{:S(2)}, u32[]{:S(2)}) collective-permute-start(bf16[28,6,128]{2,1,0:T(8,128)(2,1)S(1)} %get-tuple-element.44), channel_id=1, source_target_pairs={{0,24},{8,16},{16,8},{24,0},{1,25},{9,17},{17,9},{25,1},{2,26},{10... | collective-permute-start | bytes 129032 | tf_op jit(solution)/shard_map/ppermute | solution.py:46
  40.8 0.0 collective-permute-start.9
  40.8 0.0 collective-permute-done.11
  40.8 0.0 collective-permute-done.10
  40.9 1.9 %collective-permute-start.14 = (bf16[288,128]{1,0:T(8,128)(2,1)S(1)}, bf16[288,128]{1,0:T(8,128)(2,1)S(1)}, u32[]{:S(2)}, u32[]{:S(2)}) collective-permute-start(bf16[288,128]{1,0:T(8,128)(2,1)S(1)} %add_convert_fusion.refs_0_), channel_id=1, source_target_pairs={{0,24},{8,16},{16,8},{24,0},{1,25},{9,17},{17,9},{25,1},{2,26},{10... | collective-permute-start | bytes 221192 | tf_op jit(solution)/shard_map/ppermute | solution.py:105
  42.8 1.6 %collective-permute-start.13 = (bf16[288,128]{1,0:T(8,128)(2,1)S(1)}, bf16[288,128]{1,0:T(8,128)(2,1)S(1)}, u32[]{:S(2)}, u32[]{:S(2)}) collective-permute-start(bf16[288,128]{1,0:T(8,128)(2,1)S(1)} %add_convert_fusion.refs_0_), channel_id=1, source_target_pairs={{0,16},{8,24},{16,0},{24,8},{1,17},{9,25},{17,1},{25,9},{2,18},{10... | collective-permute-start | bytes 221192 | tf_op jit(solution)/shard_map/ppermute | solution.py:105
  44.4 0.9 %collective-permute-start.12 = (bf16[288,128]{1,0:T(8,128)(2,1)S(1)}, bf16[288,128]{1,0:T(8,128)(2,1)S(1)}, u32[]{:S(2)}, u32[]{:S(2)}) collective-permute-start(bf16[288,128]{1,0:T(8,128)(2,1)S(1)} %add_convert_fusion.refs_0_), channel_id=1, source_target_pairs={{0,8},{8,0},{16,24},{24,16},{1,9},{9,1},{17,25},{25,17},{2,10},{10... | collective-permute-start | bytes 221192 | tf_op jit(solution)/shard_map/ppermute | solution.py:105
  45.3 0.1 collective-permute-done.8
  45.4 1.9 %collective-permute-done.9 = bf16[28,6,128]{2,1,0:T(8,128)(2,1)S(1)} collective-permute-done((bf16[28,6,128]{2,1,0:T(8,128)(2,1)S(1)}, bf16[28,6,128]{2,1,0:T(8,128)(2,1)S(1)}, u32[]{:S(2)}, u32[]{:S(2)}) %collective-permute-start.9) | collective-permute-done | bytes 43040 | tf_op jit(solution)/shard_map/ppermute | solution.py:46
  47.4 2.9 %backward.1 = (bf16[16,64,128]{2,1,0:T(8,128)(2,1)}, f32[8,128]{1,0:T(8,128)S(1)}) custom-call(s32[1]{0:T(128)} %bitcast.northern, bf16[6,64,128]{2,1,0:T(8,128)(2,1)S(1)} %get-tuple-element.42.south, bf16[16,64,128]{2,1,0:T(8,128)(2,1)S(1)} %get-tuple-element.36.block, bf16[6,64,128]{2,1,0:T(8,128)(2,1)S(1)} %get-tuple-element.43.north, ...), custom_call_target="tpu_custom_call" | custom-call | flops 3000000000 | bytes 1360388 | tf_op jit(solution)/shard_map/backward/pallas_call | solution.py:359
  50.3 0.0 collective-permute-done.14.refs_3_
  50.3 0.0 collective-permute-done.13.refs_2_
  50.3 0.0 collective-permute-done.12.refs_1_
  50.4 0.1 collective-permute-start.15
  50.5 1.4 %collective-permute-done.15.back = f32[288,128]{1,0:T(8,128)S(1)} collective-permute-done((f32[288,128]{1,0:T(8,128)S(1)}, f32[288,128]{1,0:T(8,128)S(1)}, u32[]{:S(2)}, u32[]{:S(2)}) %collective-permute-start.15) | collective-permute-done | bytes 147488 | tf_op jit(solution)/shard_map/ppermute | solution.py:105
  51.8 0.7 %final.1 = (f32[49,128]{1,0:T(8,128)}, f32[2,128]{1,0:T(2,128)}, f32[128,256]{1,0:T(8,128)}, f32[256,128]{1,0:T(8,128)}) custom-call(s32[1]{0:T(128)} %bitcast.8.odd, f32[288,128]{1,0:T(8,128)S(1)} %add.35.total, f32[288,128]{1,0:T(8,128)S(1)} %collective-permute-done.15.back), custom_call_target="tpu_custom_call" | custom-call | bytes 583172 | tf_op jit(solution)/shard_map/final/pallas_call | solution.py:359
  (17 shorter events, 0.3 us)
Async XLA Ops:
  0.6 1.0 %copy-start = (bf16[1,16,64,128]{3,2,1,0:T(8,128)(2,1)S(1)}, bf16[1,16,64,128]{3,2,1,0:T(8,128)(2,1)}, u32[]{:S(2)}) copy-start(bf16[1,16,64,128]{3,2,1,0:T(8,128)(2,1)} %param.8) | copy-start | bytes 786436
  1.6 0.7 %copy-start.5 = (s32[16,64]{1,0:T(8,128)S(1)}, s32[16,64]{1,0:T(8,128)}, u32[]{:S(2)}) copy-start(s32[16,64]{1,0:T(8,128)} %mask.3) | copy-start | bytes 12292
  2.7 17.2 %copy-start.1 = (bf16[1,16,64,128]{3,2,1,0:T(8,128)(2,1)S(1)}, bf16[1,16,64,128]{3,2,1,0:T(8,128)(2,1)}, u32[]{:S(2)}) copy-start(bf16[1,16,64,128]{3,2,1,0:T(8,128)(2,1)} %param.9) | copy-start | bytes 786436
  2.7 17.2 %copy-start.2 = (bf16[128,256]{1,0:T(8,128)(2,1)S(1)}, bf16[128,256]{1,0:T(8,128)(2,1)}, u32[]{:S(2)}) copy-start(bf16[128,256]{1,0:T(8,128)(2,1)} %up.1) | copy-start | bytes 196612
  2.7 17.2 %copy-start.3 = (bf16[256,128]{1,0:T(8,128)(2,1)S(1)}, bf16[256,128]{1,0:T(8,128)(2,1)}, u32[]{:S(2)}) copy-start(bf16[256,128]{1,0:T(8,128)(2,1)} %down.1) | copy-start | bytes 196612
  2.7 17.2 %copy-start.4 = (f32[49,128]{1,0:T(8,128)S(1)}, f32[49,128]{1,0:T(8,128)}, u32[]{:S(2)}) copy-start(f32[49,128]{1,0:T(8,128)} %taps.3) | copy-start | bytes 75268
  2.7 17.2 %copy-start.6 = (f32[128]{0:T(128)S(1)}, f32[128]{0:T(128)}, u32[]{:S(2)}) copy-start(f32[128]{0:T(128)} %param.12) | copy-start | bytes 1540
  2.7 17.2 %copy-start.7 = (f32[128]{0:T(128)S(1)}, f32[128]{0:T(128)}, u32[]{:S(2)}) copy-start(f32[128]{0:T(128)} %param.13) | copy-start | bytes 1540
  2.8 8.0 %collective-permute-start.1 = (bf16[6,64,128]{2,1,0:T(8,128)(2,1)S(1)}, bf16[6,64,128]{2,1,0:T(8,128)(2,1)S(1)}, u32[]{:S(2)}, u32[]{:S(2)}) collective-permute-start(bf16[6,64,128]{2,1,0:T(8,128)(2,1)S(1)} %rev.6), channel_id=1, source_target_pairs={{0,24},{8,16},{16,8},{24,0},{1,25},{9,17},{17,9},{25,1},{2,26},{10... | collective-permute-start | bytes 294920 | tf_op jit(solution)/shard_map/ppermute | solution.py:52
  7.9 4.6 %collective-permute-start = (bf16[6,64,128]{2,1,0:T(8,128)(2,1)S(1)}, bf16[6,64,128]{2,1,0:T(8,128)(2,1)S(1)}, u32[]{:S(2)}, u32[]{:S(2)}) collective-permute-start(bf16[6,64,128]{2,1,0:T(8,128)(2,1)S(1)} %get-tuple-element.55), channel_id=1, source_target_pairs={{0,4},{4,0},{1,5},{5,1},{2,6},{6,2},{3,7},{7,3},{8,12},{12,8},{9,1... | collective-permute-start | bytes 294920 | tf_op jit(solution)/shard_map/ppermute | solution.py:46
  13.1 6.1 %collective-permute-start.2 = (bf16[28,6,128]{2,1,0:T(8,128)(2,1)S(1)}, bf16[28,6,128]{2,1,0:T(8,128)(2,1)S(1)}, u32[]{:S(2)}, u32[]{:S(2)}) collective-permute-start(bf16[28,6,128]{2,1,0:T(8,128)(2,1)S(1)} %get-tuple-element.32), channel_id=1, source_target_pairs={{0,24},{8,16},{16,8},{24,0},{1,25},{9,17},{17,9},{25,1},{2,26},{10... | collective-permute-start | bytes 129032 | tf_op jit(solution)/shard_map/ppermute | solution.py:46
  15.1 4.7 %collective-permute-start.3 = (bf16[28,6,128]{2,1,0:T(8,128)(2,1)S(1)}, bf16[28,6,128]{2,1,0:T(8,128)(2,1)S(1)}, u32[]{:S(2)}, u32[]{:S(2)}) collective-permute-start(bf16[28,6,128]{2,1,0:T(8,128)(2,1)S(1)} %get-tuple-element.33), channel_id=1, source_target_pairs={{0,8},{8,0},{16,24},{24,16},{1,9},{9,1},{17,25},{25,17},{2,10},{10... | collective-permute-start | bytes 129032 | tf_op jit(solution)/shard_map/ppermute | solution.py:46
  27.9 3.6 %collective-permute-start.6 = (bf16[288,128]{1,0:T(8,128)(2,1)S(1)}, bf16[288,128]{1,0:T(8,128)(2,1)S(1)}, u32[]{:S(2)}, u32[]{:S(2)}) collective-permute-start(bf16[288,128]{1,0:T(8,128)(2,1)S(1)} %get-tuple-element.41), channel_id=1, source_target_pairs={{0,1},{1,0},{2,3},{3,2},{4,5},{5,4},{6,7},{7,6},{8,9},{9,8},{10,11... | collective-permute-start | bytes 221192 | tf_op jit(solution)/shard_map/ppermute | solution.py:105
  28.0 7.1 %collective-permute-start.5 = (bf16[6,64,128]{2,1,0:T(8,128)(2,1)S(1)}, bf16[6,64,128]{2,1,0:T(8,128)(2,1)S(1)}, u32[]{:S(2)}, u32[]{:S(2)}) collective-permute-start(bf16[6,64,128]{2,1,0:T(8,128)(2,1)S(1)} %rev.7), channel_id=1, source_target_pairs={{0,24},{8,16},{16,8},{24,0},{1,25},{9,17},{17,9},{25,1},{2,26},{10... | collective-permute-start | bytes 294920 | tf_op jit(solution)/shard_map/ppermute | solution.py:52
  30.0 5.1 %collective-permute-start.4 = (bf16[6,64,128]{2,1,0:T(8,128)(2,1)S(1)}, bf16[6,64,128]{2,1,0:T(8,128)(2,1)S(1)}, u32[]{:S(2)}, u32[]{:S(2)}) collective-permute-start(bf16[6,64,128]{2,1,0:T(8,128)(2,1)S(1)} %get-tuple-element.53), channel_id=1, source_target_pairs={{0,4},{4,0},{1,5},{5,1},{2,6},{6,2},{3,7},{7,3},{8,12},{12,8},{9,1... | collective-permute-start | bytes 294920 | tf_op jit(solution)/shard_map/ppermute | solution.py:46
  31.5 6.6 %collective-permute-start.7 = (bf16[288,128]{1,0:T(8,128)(2,1)S(1)}, bf16[288,128]{1,0:T(8,128)(2,1)S(1)}, u32[]{:S(2)}, u32[]{:S(2)}) collective-permute-start(bf16[288,128]{1,0:T(8,128)(2,1)S(1)} %add_convert_fusion.1), channel_id=1, source_target_pairs={{0,6},{1,7},{2,4},{3,5},{4,2},{5,3},{6,0},{7,1},{8,14},{9,15},{10,... | collective-permute-start | bytes 221192 | tf_op jit(solution)/shard_map/ppermute | solution.py:105
  33.1 7.8 %collective-permute-start.11 = (bf16[288,128]{1,0:T(8,128)(2,1)S(1)}, bf16[288,128]{1,0:T(8,128)(2,1)S(1)}, u32[]{:S(2)}, u32[]{:S(2)}) collective-permute-start(bf16[288,128]{1,0:T(8,128)(2,1)S(1)} %add_convert_fusion.1), channel_id=1, source_target_pairs={{0,4},{4,0},{1,5},{5,1},{2,6},{6,2},{3,7},{7,3},{8,12},{12,8},{9,1... | collective-permute-start | bytes 221192 | tf_op jit(solution)/shard_map/ppermute | solution.py:105
  34.6 6.3 %collective-permute-start.10 = (bf16[288,128]{1,0:T(8,128)(2,1)S(1)}, bf16[288,128]{1,0:T(8,128)(2,1)S(1)}, u32[]{:S(2)}, u32[]{:S(2)}) collective-permute-start(bf16[288,128]{1,0:T(8,128)(2,1)S(1)} %add_convert_fusion.1), channel_id=1, source_target_pairs={{0,2},{1,3},{2,0},{3,1},{4,6},{5,7},{6,4},{7,5},{8,10},{9,11},{10,... | collective-permute-start | bytes 221192 | tf_op jit(solution)/shard_map/ppermute | solution.py:105
  38.8 6.7 %collective-permute-start.8 = (bf16[28,6,128]{2,1,0:T(8,128)(2,1)S(1)}, bf16[28,6,128]{2,1,0:T(8,128)(2,1)S(1)}, u32[]{:S(2)}, u32[]{:S(2)}) collective-permute-start(bf16[28,6,128]{2,1,0:T(8,128)(2,1)S(1)} %get-tuple-element.44), channel_id=1, source_target_pairs={{0,24},{8,16},{16,8},{24,0},{1,25},{9,17},{17,9},{25,1},{2,26},{10... | collective-permute-start | bytes 129032 | tf_op jit(solution)/shard_map/ppermute | solution.py:46
  40.8 6.6 %collective-permute-start.9 = (bf16[28,6,128]{2,1,0:T(8,128)(2,1)S(1)}, bf16[28,6,128]{2,1,0:T(8,128)(2,1)S(1)}, u32[]{:S(2)}, u32[]{:S(2)}) collective-permute-start(bf16[28,6,128]{2,1,0:T(8,128)(2,1)S(1)} %get-tuple-element.45), channel_id=1, source_target_pairs={{0,8},{8,0},{16,24},{24,16},{1,9},{9,1},{17,25},{25,17},{2,10},{10... | collective-permute-start | bytes 129032 | tf_op jit(solution)/shard_map/ppermute | solution.py:46
  40.9 9.5 %collective-permute-start.14 = (bf16[288,128]{1,0:T(8,128)(2,1)S(1)}, bf16[288,128]{1,0:T(8,128)(2,1)S(1)}, u32[]{:S(2)}, u32[]{:S(2)}) collective-permute-start(bf16[288,128]{1,0:T(8,128)(2,1)S(1)} %add_convert_fusion.refs_0_), channel_id=1, source_target_pairs={{0,24},{8,16},{16,8},{24,0},{1,25},{9,17},{17,9},{25,1},{2,26},{10... | collective-permute-start | bytes 221192 | tf_op jit(solution)/shard_map/ppermute | solution.py:105
  42.8 7.6 %collective-permute-start.13 = (bf16[288,128]{1,0:T(8,128)(2,1)S(1)}, bf16[288,128]{1,0:T(8,128)(2,1)S(1)}, u32[]{:S(2)}, u32[]{:S(2)}) collective-permute-start(bf16[288,128]{1,0:T(8,128)(2,1)S(1)} %add_convert_fusion.refs_0_), channel_id=1, source_target_pairs={{0,16},{8,24},{16,0},{24,8},{1,17},{9,25},{17,1},{25,9},{2,18},{10... | collective-permute-start | bytes 221192 | tf_op jit(solution)/shard_map/ppermute | solution.py:105
  44.4 5.9 %collective-permute-start.12 = (bf16[288,128]{1,0:T(8,128)(2,1)S(1)}, bf16[288,128]{1,0:T(8,128)(2,1)S(1)}, u32[]{:S(2)}, u32[]{:S(2)}) collective-permute-start(bf16[288,128]{1,0:T(8,128)(2,1)S(1)} %add_convert_fusion.refs_0_), channel_id=1, source_target_pairs={{0,8},{8,0},{16,24},{24,16},{1,9},{9,1},{17,25},{25,17},{2,10},{10... | collective-permute-start | bytes 221192 | tf_op jit(solution)/shard_map/ppermute | solution.py:105
  50.4 1.4 %collective-permute-start.15 = (f32[288,128]{1,0:T(8,128)S(1)}, f32[288,128]{1,0:T(8,128)S(1)}, u32[]{:S(2)}, u32[]{:S(2)}) collective-permute-start(f32[288,128]{1,0:T(8,128)S(1)} %add.35.total), channel_id=1, source_target_pairs={{0,1},{1,0},{2,3},{3,2},{4,5},{5,4},{6,7},{7,6},{8,9},{9,8},{10,11... | collective-permute-start | bytes 442376 | tf_op jit(solution)/shard_map/ppermute | solution.py:105

commit v4 on v3

v4 whole, which is shorter than its diff:
```python
import functools
import math

import jax
import jax.numpy as jnp
from jax import lax
from jax.experimental import pallas as pl
from jax.experimental.pallas import tpu as pltpu
from jax.sharding import PartitionSpec as P

KERNEL = 7
DILATION = 2
REACH = 6
TAPS = KERNEL * KERNEL
LANE = 8
LEFT = 8
BASE = LEFT - REACH
LOWER_WORK, UPPER_WORK, KERNEL_WORK = 10**8, 2 * 10**9, 10**8
SLOPE = math.sqrt(2.0 / math.pi)
CUBIC = 0.044715
F32, BF16 = jnp.float32, jnp.bfloat16


def route(axes, target):
    sizes = [lax.axis_size(a) for a in axes]
    pairs = []
    for flat in range(math.prod(sizes)):
        rest, at = flat, []
        for size in reversed(sizes):
            at.append(rest % size)
            rest //= size
        at = at[::-1]
        to = target(*at)
        if to is not None:
            dest = 0
            for size, i in zip(sizes, to):
                dest = dest * size + i
            pairs.append((flat, dest))
    return pairs


def is_northern():
    return lax.axis_index("lat") == lax.axis_size("lat") - 1


def xor_partner(value, axis, bits):
    return lax.ppermute(value, axis, [(i, i ^ bits) for i in range(lax.axis_size(axis))])


NORTHERN, ODD, INNER, CORE = range(4)


def flags_of():
    odd = lax.axis_index("lon") % 2 if lax.axis_size("lon") == 4 else 0
    values = (is_northern(), odd, lax.axis_index("lat") > 0, lax.axis_index("ens") % 2)
    row = lax.broadcasted_iota(jnp.int32, (LANE, 128), 0)
    return sum(jnp.where(row == n, jnp.asarray(v, jnp.int32), 0) for n, v in enumerate(values))


def on(flags, n):
    return flags[n : n + 1] == 1


def rim_kernel(block, flags, facing, near, far):
    rows, cols = block.shape[0], block.shape[1]
    northern, odd = on(flags, NORTHERN), on(flags, ODD)
    for k in range(REACH):
        low, high = block[k].astype(F32), block[rows - REACH + k].astype(F32)
        facing[k] = jnp.where(northern, low, high).astype(BF16)
    for r in range(rows):
        head = block[r, : 2 * LANE].astype(F32)[:LANE]
        tail = block[r, cols - 2 * LANE :].astype(F32)[LANE:]
        near[r] = jnp.where(odd, head, tail).astype(BF16)
        far[r] = jnp.where(odd, tail, head).astype(BF16)


def fold_kernel(block, flags, far, *refs):
    joint, corner, own = refs[-3:]
    rows, cols, channels = block.shape
    start = 0
    odd = on(flags, ODD)
    down = lax.broadcasted_iota(jnp.int32, (cols, cols), 0)
    across = lax.broadcasted_iota(jnp.int32, (cols, cols), 1)
    turn = jnp.where(down + across == cols - 1, 1.0, 0.0).astype(BF16)
    if joint.shape[0] > REACH * cols:
        start = rows * LANE
        joint[:start] = far[...].astype(F32).reshape(start, channels).astype(BF16)
    for k in range(REACH):
        row = jnp.dot(turn, block[rows - 1 - k], preferred_element_type=F32)
        joint[start + k * cols : start + (k + 1) * cols] = row.astype(BF16)
        head, tail = row[:LANE], row[cols - LANE :]
        corner[k] = jnp.where(odd, tail, head).astype(BF16)
        own[k] = jnp.where(odd, head, tail).astype(BF16)


def put_corners(near, far, flags, facing, start=None):
    rows = near.shape[0]
    northern, odd = on(flags, NORTHERN), on(flags, ODD)
    for k in range(REACH):
        one, two = (
            jnp.where(northern, a[k].astype(F32), a[rows - REACH + k].astype(F32)) for a in (far, near)
        )
        sides = [jnp.where(odd, two, one), jnp.where(odd, one, two)]
        at = k if start is None else slice(start + k * 2 * LANE, start + (k + 1) * 2 * LANE)
        facing[at] = jnp.concatenate(sides, 0).astype(BF16)


def corner_kernel(near, far, flags, *refs):
    put_corners(near, far, flags, refs[-1])


def is_pairs():
    return (lax.axis_size("lat"), lax.axis_size("lon"), lax.axis_size("ens")) == (2, 4, 4)


def ring(axis, step, closed=True):
    count = lax.axis_size(axis)
    return [(i, (i + step) % count) for i in range(count) if closed or 0 <= i + step < count]


def extend_any(block):
    rows, cols, channels = block.shape
    lons = lax.axis_size("lon")
    top, bottom, flipped = block[rows - REACH :], block[:REACH], block[rows - REACH :][::-1, ::-1]
    west = lax.ppermute(block[:, cols - LANE :], "lon", ring("lon", 1))
    east = lax.ppermute(block[:, :LANE], "lon", ring("lon", -1))
    folded = lax.ppermute(flipped, "lon", [(i, lons - 1 - i) for i in range(lons)])
    left = lax.ppermute(folded[:, cols - LANE :], "lon", ring("lon", 1))
    right = lax.ppermute(folded[:, :LANE], "lon", ring("lon", -1))
    below = lax.ppermute(top, "lat", ring("lat", 1, False))
    above = lax.ppermute(bottom, "lat", ring("lat", -1, False))
    sides = [jnp.concatenate([west[at], east[at]], 1) for at in (slice(rows - REACH, rows), slice(REACH))]
    low = lax.ppermute(sides[0], "lat", ring("lat", 1, False))
    high = lax.ppermute(sides[1], "lat", ring("lat", -1, False))
    return below, above, folded, west, east, left, right, low, high


def shapes_of(block):
    rows, cols, channels = block.shape
    sizes = ((REACH, cols), (rows, LANE), (REACH, LANE), (REACH, 2 * LANE))
    return [jax.ShapeDtypeStruct((*size, channels), BF16) for size in sizes]


def extend(block, flags):
    if not is_pairs():
        return extend_any(block)
    strip, side, corner, corners = shapes_of(block)
    cells = side.shape[0] * side.shape[1]
    facing, near, far = call(rim_kernel, (strip, side, side), (block, flags), name="rim")
    facing, near = xor_partner(facing, "lat", 1), xor_partner(near, "lon", 1)
    both = jax.ShapeDtypeStruct((cells + strip.shape[0] * strip.shape[1], block.shape[2]), BF16)
    both, corner, own = call(fold_kernel, (both, corner, corner), (block, flags, far), name="fold")
    both, corner = xor_partner(both, "lon", 3), xor_partner(corner, "lon", 2)
    far, folded = both[:cells].reshape(side.shape), both[cells:].reshape(strip.shape)
    (corners,) = call(corner_kernel, (corners,), (near, far, flags, corner), name="corners")
    corners = xor_partner(corners, "lat", 1)
    return facing, facing, folded, far, near, own, corner, corners, corners


def partners(value, bits):
    axes = tuple(a for a in ("lon", "lat", "ens") if a in [b[0] for b in bits])
    flip = {a: 0 for a in axes}
    for a, b in bits:
        flip[a] ^= b
    return lax.ppermute(value, axes, route(axes, lambda *at: [i ^ flip[a] for a, i in zip(axes, at)]))


def add_kernel(*refs):
    rows, out = refs[-1].shape[0], refs[-1]
    out[...] = added([ref[:rows] for ref in refs[:-2]]).astype(out.dtype)


def stages():
    bits = {a: [(a, 1 << b) for b in range(lax.axis_size(a).bit_length() - 1)] for a in ("ens", "lat", "lon")}
    rest = bits["ens"][1:] + bits["lat"] + bits["lon"]
    return bits["ens"][:1], [rest[n : n + 2] for n in range(0, len(rest), 2)]


def stage(sent, pair):
    if len(pair) == 1:
        return [sent, partners(sent, pair)]
    far = partners(sent, pair)
    return [sent, partners(sent, pair[:1]), partners(sent, pair[1:]), far]


def added(values):
    values = [v.astype(F32) for v in values]
    return sum(values) if len(values) == 2 else (values[0] + values[1]) + (values[2] + values[3])


def add_kernel(*refs):
    rows, out = refs[-1].shape[0], refs[-1]
    out[...] = added([ref[:rows] for ref in refs[:-2]]).astype(out.dtype)


def join_corners_kernel(mine, core, small, near, far, flags, token, joined, wider):
    join_kernel(mine, core, small, joined)
    rows = joined.shape[0]
    wider[:rows] = joined[...]
    put_corners(near, far, flags, wider, rows)


def join_kernel(mine, core, small, *refs):
    (joined,) = refs[-1:]
    half = mine.shape[0]
    joined[:half] = (mine[...] + core[...].astype(F32)).astype(BF16)
    joined[half:] = small[...].astype(BF16)


def fill_own(wide, flags, block, below):
    rows, cols = block.shape[0], block.shape[1]
    inner = on(flags, INNER)
    for r in range(rows):
        wide[REACH + r, LEFT : LEFT + cols] = block[r].astype(F32)
    for k in range(REACH):
        wide[k, LEFT : LEFT + cols] = jnp.where(inner, below[k].astype(F32), 0.0)


def fill_top(wide, flags, above, folded):
    cols = above.shape[1]
    northern = on(flags, NORTHERN)
    for k in range(REACH):
        value = jnp.where(northern, folded[k].astype(F32), above[k].astype(F32))
        wide[wide.shape[0] - REACH + k, LEFT : LEFT + cols] = value


def fill_sides(wide, flags, far, near, own, corner, low, high):
    rows, right = far.shape[0], wide.shape[1] - LEFT
    northern, odd, inner = on(flags, NORTHERN), on(flags, ODD), on(flags, INNER)
    for r in range(rows):
        one, two = far[r].astype(F32), near[r].astype(F32)
        wide[REACH + r, :LEFT] = jnp.where(odd, two, one)
        wide[REACH + r, right:] = jnp.where(odd, one, two)
    for k in range(REACH):
        sides = jnp.where(inner, low[k].astype(F32), 0.0)
        wide[k, :LEFT], wide[k, right:] = sides[:LANE], sides[LANE:]
        sides, one, two = high[k].astype(F32), own[k].astype(F32), corner[k].astype(F32)
        top = REACH + rows + k
        wide[top, :LEFT] = jnp.where(northern, jnp.where(odd, two, one), sides[:LANE])
        wide[top, right:] = jnp.where(northern, jnp.where(odd, one, two), sides[LANE:])


def conv(wide, tap, first, rows, starts, store):
    lines = rows // 2
    chunk = max(1, 32 // lines)

    def parity(q, carry):
        for n in range(0, len(starts), chunk):
            cols = starts[n : n + chunk]
            sums = [[None] * len(cols) for _ in range(lines)]
            for k in range(lines + KERNEL - 1):
                for j in range(KERNEL):
                    at = [BASE + c + DILATION * j for c in cols]
                    values = [wide[first + q + 2 * k, a : a + LANE] for a in at]
                    for i in range(KERNEL):
                        line = k - i
                        if 0 <= line < lines:
                            weight = tap(k, i, j)
                            for g, value in enumerate(values):
                                term, old = weight * value, sums[line][g]
                                sums[line][g] = term if old is None else old + term
            for line in range(lines):
                for g, c in enumerate(cols):
                    store(first + q + 2 * line, c, sums[line][g])
        return carry

    lax.fori_loop(0, 2, parity, 0)


def mask_kernel(field, mask, masked, sea, state, ocean, sems):
    rows, cols, channels = state.shape
    copies = [pltpu.make_async_copy(field, state, sems.at[0]), pltpu.make_async_copy(mask, ocean, sems.at[1])]
    for copy in copies:
        copy.start()
    copies[1].wait()
    value = ocean[...].astype(BF16)
    at = lax.broadcasted_iota(jnp.int32, (rows, channels), 0)
    for r in range(rows):
        pick = jnp.where(at == r, 1.0, 0.0).astype(BF16)
        row = lax.dot_general(value, pick, (((0,), (0,)), ((), ())), preferred_element_type=F32)
        sea[r] = row.astype(BF16)
    copies[0].wait()
    for r in range(rows):
        masked[r] = state[r] * sea[r]


def block_pass(first, rows, blocks, spread, sea, weights, state, arrive=None):
    wide, mixed, result, grad, upstream, up_part, down_part, sums = state
    taps, gain, shift, up, down = weights
    channels = wide.shape[2]
    for k in range(TAPS):
        spread[k] = jnp.broadcast_to(taps[k : k + 1], (LANE, channels))

    def store(row, col, value):
        mixed[row, col : col + LANE] = value

    starts = [c for col, cols in blocks for c in range(col, col + cols, LANE)]
    conv(wide, lambda k, i, j: spread[i * KERNEL + j], first, rows, starts, store)
    width = sum(cols for _, cols in blocks)
    cells = rows * width

    def take(ref, row=0, col=0):
        parts = [ref[first + row : first + row + rows, col + c : col + c + n].astype(F32) for c, n in blocks]
        return jnp.concatenate(parts, 1).reshape(cells, channels)

    def put(ref, value):
        value, at = value.reshape(rows, width, channels), 0
        for c, n in blocks:
            ref[first : first + rows, c : c + n] = value[:, at : at + n].astype(ref.dtype)
            at += n

    up_w, down_w, gain_v = up[...], down[...], gain[...]
    nt = (((1,), (1,)), ((), ()))
    tn = (((0,), (0,)), ((), ()))
    value = take(mixed)
    centered = value - jnp.mean(value, -1, keepdims=True)
    rstd = lax.rsqrt(jnp.mean(centered * centered, -1, keepdims=True) + 1e-06)
    unit = centered * rstd
    normed = (unit * gain_v + shift[...]).astype(BF16)
    pre = jnp.dot(normed, up_w, preferred_element_type=F32)
    square = pre * pre
    tanh = jnp.tanh(pre * (SLOPE + (SLOPE * CUBIC) * square))
    gate = 0.5 + 0.5 * tanh
    activated = (pre * gate).astype(BF16)
    product = jnp.dot(activated, down_w, preferred_element_type=F32)
    ocean = take(sea)
    put(result, (take(wide, REACH, LEFT) + product) * ocean)
    if arrive is not None:
        arrive()
    above = (take(upstream) * ocean).astype(BF16)
    down_part[...] += lax.dot_general(above, activated, tn, preferred_element_type=F32)
    act_grad = lax.dot_general(above, down_w, nt, preferred_element_type=F32)
    deriv = gate + pre * (gate * (1.0 - tanh)) * (SLOPE + (3.0 * SLOPE * CUBIC) * square)
    pre_grad = (act_grad * deriv).astype(BF16)
    up_part[...] += lax.dot_general(normed, pre_grad, tn, preferred_element_type=F32)
    norm_in = lax.dot_general(pre_grad, up_w, nt, preferred_element_type=F32)
    sums[0] += jnp.sum((norm_in * unit).reshape(cells // LANE, LANE, channels), 0)
    sums[1] += jnp.sum(norm_in.reshape(cells // LANE, LANE, channels), 0)
    scaled = norm_in * gain_v
    inner = jnp.mean(scaled * unit, -1, keepdims=True)
    moved = rstd * (scaled - jnp.mean(scaled, -1, keepdims=True) - unit * inner)
    put(mixed, moved)
    put(grad, moved)


STATE = 8


def lower_kernel(block, below, cotangent, sea, flags, *refs):
    weights, state, (spread, sem) = refs[:5], refs[5:-2], refs[-2:]
    rows, cols = block.shape[0], block.shape[1]
    upstream, up_part, down_part, sums = state[4:]
    fetch = pltpu.make_async_copy(cotangent, upstream, sem)
    fetch.start()
    for ref in (up_part, down_part, sums):
        ref[...] = jnp.zeros_like(ref)
    fill_own(state[0], flags, block, below)
    block_pass(0, rows // 2, [(LANE, cols - 2 * LANE)], spread, sea, weights, state, fetch.wait)


def upper_kernel(*refs):
    above, folded, sea, flags = refs[STATE : STATE + 4]
    weights, state, spread = refs[STATE + 4 : STATE + 9], refs[STATE + 9 : -1], refs[-1]
    rows, cols = sea.shape[0], sea.shape[1]
    fill_top(state[0], flags, above, folded)
    block_pass(rows // 2, rows // 2, [(LANE, cols - 2 * LANE)], spread, sea, weights, state)


def edge_kernel(*refs):
    sides, sea, flags = refs[STATE : STATE + 6], refs[STATE + 6], refs[STATE + 7]
    weights, state, (mine, other, spread) = refs[STATE + 8 : STATE + 13], refs[STATE + 13 : -3], refs[-3:]
    rows, cols = sea.shape[0], sea.shape[1]
    hidden, channels = mine.shape
    fill_sides(state[0], flags, *sides)
    block_pass(0, rows, [(0, LANE), (cols - LANE, LANE)], spread, sea, weights, state)
    up_part, down_part = state[5:7]
    down_sum = down_part[...].T
    up_sum = jnp.concatenate([up_part[:, n : n + channels] for n in range(0, hidden, channels)], 0)
    odd = on(flags, CORE)
    mine[...] = jnp.where(odd, up_sum, down_sum)
    other[...] = jnp.where(odd, down_sum, up_sum).astype(BF16)


def kernel_kernel(wide, mixed, result, norm, output, small_out, sem):
    rows, cols, channels = mixed.shape
    send = pltpu.make_async_copy(result, output, sem)
    send.start()
    small = jnp.zeros((LANE, channels), F32)
    pieces = []
    for taps_i in (range(0, 4), range(4, KERNEL)):

        def quad(n, sums, taps_i=taps_i):
            base = (n // 2) * 8 + n % 2
            sums = list(sums)
            for g in range(cols // LANE):
                grads = [mixed[base + 2 * m, g * LANE : (g + 1) * LANE] for m in range(4)]
                for k in range(taps_i[0], taps_i[-1] + 4):
                    for j in range(KERNEL):
                        a = BASE + g * LANE + DILATION * j
                        value = wide[base + 2 * k, a : a + LANE]
                        for m in range(4):
                            if k - m in taps_i:
                                at = (k - m - taps_i[0]) * KERNEL + j
                                sums[at] = sums[at] + grads[m] * value
            return tuple(sums)

        zero = tuple(small for _ in range(len(taps_i) * KERNEL))
        pieces += list(lax.fori_loop(0, rows // 4, quad, zero))
    pieces += [norm[0], norm[1]]
    pieces = [jnp.sum(p, 0, keepdims=True) for p in pieces]
    pieces += [jnp.zeros((small_out.shape[0] - TAPS - 2, channels), F32)]
    small_out[...] = jnp.concatenate(pieces, 0)
    send.wait()


def final_kernel(total, back, flags, kernel_grad, norm_grad, up_grad, down_grad, *, factor):
    hidden, channels = down_grad.shape
    odd = on(flags, CORE)
    own, theirs = total[:hidden] * factor, back[:hidden] * factor
    down_grad[...] = jnp.where(odd, theirs, own)
    up = jnp.where(odd, own, theirs)
    for n in range(hidden // channels):
        up_grad[:, n * channels : (n + 1) * channels] = up[n * channels : (n + 1) * channels]
    small = (total[hidden:] + back[hidden:]) * factor
    kernel_grad[...] = small[:TAPS]
    norm_grad[...] = small[TAPS : TAPS + 2]


def backward_kernel(block, below, above, folded, far, near, own, corner, low, high, cotangent, sea, taps, flags,
                    field_grad, token, wide, spread, upper):
    rows, cols, channels = block.shape
    northern = on(flags, NORTHERN)
    for k in range(TAPS):
        flipped = jnp.broadcast_to(taps[TAPS - 1 - k : TAPS - k], (LANE, channels))
        plain = jnp.broadcast_to(taps[k : k + 1], (LANE, channels))
        spread[k] = flipped
        upper[k] = jnp.where(northern, plain, flipped)
    fill_own(wide, flags, block, below)
    fill_top(wide, flags, above, folded)
    fill_sides(wide, flags, far, near, own, corner, low, high)
    edge = (REACH + rows) // 2

    def tap(k, i, j):
        return (upper if k >= edge else spread)[i * KERNEL + j]

    def store(row, col, value):
        at = (row, slice(col, col + LANE))
        field_grad[at] = ((cotangent[at].astype(F32) + value) * sea[at].astype(F32)).astype(BF16)

    conv(wide, tap, 0, rows, list(range(0, cols, LANE)), store)
    token[...] = jnp.zeros_like(token)


def call(kernel, outs, operands, scratch=(), far=(), far_outs=(), aliases=(), work=0, name=None):
    vmem, hbm = pl.BlockSpec(memory_space=pltpu.VMEM), pl.BlockSpec(memory_space=pltpu.HBM)
    moved = sum(math.prod(a.shape) * a.dtype.itemsize for a in (*operands, *outs))
    return pl.pallas_call(
        kernel,
        out_shape=outs,
        in_specs=[hbm if n in far else vmem for n in range(len(operands))],
        out_specs=[hbm if n in far_outs else vmem for n in range(len(outs))],
        scratch_shapes=scratch,
        input_output_aliases=dict(aliases),
        compiler_params=pltpu.CompilerParams(vmem_limit_bytes=24 * 1024 * 1024),
        cost_estimate=pl.CostEstimate(flops=work, bytes_accessed=moved, transcendentals=0),
        name=name,
    )(*operands)


def shards(field, cotangent, land_mask, kernel_taps, norm_gain, norm_shift, up_weight, down_weight):
    rows, cols, channels = field.shape[1:]
    hidden = up_weight.shape[1]
    shape = jax.ShapeDtypeStruct
    tile = (rows, cols, channels)
    near = pltpu.VMEM(tile, BF16)
    masked, sea = call(
        mask_kernel,
        (shape(tile, BF16), shape(tile, BF16)),
        (field[0], land_mask),
        [near, pltpu.VMEM((rows, cols), jnp.int32), pltpu.SemaphoreType.DMA((2,))],
        far=(0, 1),
        work=10**9,
        name="mask",
    )
    flags = flags_of()
    below, above, folded, far, near, own, corner, low, high = extend(masked, flags)
    wide = (rows + 2 * REACH, cols + 2 * LEFT, channels)
    spread = pltpu.VMEM((TAPS, LANE, channels), F32)
    large, small = (hidden, channels), (64, channels)
    weights = (kernel_taps, norm_gain[None], norm_shift[None], up_weight, down_weight)
    part = shape((channels, hidden), F32)
    state = (shape(wide, F32), shape(tile, F32), shape(tile, BF16), shape(tile, BF16), shape(tile, BF16), part, part, shape((2, LANE, channels), F32))
    same = tuple((n, n) for n in range(STATE))
    passed = call(
        lower_kernel,
        state,
        (masked, below, cotangent[0], sea, flags, *weights),
        [spread, pltpu.SemaphoreType.DMA],
        far=(2,),
        work=LOWER_WORK,
        name="lower",
    )
    passed = call(upper_kernel, state, (*passed, above, folded, sea, flags, *weights), [spread], aliases=same, work=UPPER_WORK, name="upper")
    *passed, mine, other = call(
        edge_kernel,
        (*state, shape(large, F32), shape(large, BF16)),
        (*passed, far, near, own, corner, low, high, sea, flags, *weights),
        [spread],
        aliases=same,
        work=10**9,
        name="edge",
    )
    widened, mixed_grad, result, grad, upstream, _, _, sums = passed
    core, rest = stages()
    received = partners(other, core)
    output, last_sums = call(
        kernel_kernel,
        (shape(tile, BF16), shape(small, F32)),
        (widened, mixed_grad, result, sums),
        [pltpu.SemaphoreType.DMA],
        far_outs=(0,),
        work=KERNEL_WORK,
        name="kernel_gradient",
    )
    joined = shape((hidden + small[0], channels), BF16)
    if is_pairs():
        strip, side, corner, corners = shapes_of(grad)
        facing, near, far = call(rim_kernel, (strip, side, side), (grad, flags), name="rim")
        far_sent = far
        facing, near, far = xor_partner(facing, "lat", 1), xor_partner(near, "lon", 1), xor_partner(far, "lon", 3)
        folded, corner, own = call(
            fold_kernel,
            (shape((strip.shape[0] * strip.shape[1], channels), BF16), corner, corner),
            (grad, flags, far_sent, facing, received, last_sums),
            name="fold",
        )
        folded, corner = xor_partner(folded, "lon", 3), xor_partner(corner, "lon", 2)
        wider = shape((joined.shape[0] + corners.shape[0] * corners.shape[1], channels), BF16)
        sent, wider = call(
            join_corners_kernel, (joined, wider), (mine, received, last_sums, near, far, flags, own), name="join"
        )
        (one, two), cells = rest[0], joined.shape[0]
        wider = partners(wider, [two])
        values = [sent, partners(sent, [one]), wider, partners(sent, [one, two])]
        corners = wider[cells:].reshape(corners.shape)
        halo = (facing, facing, folded.reshape(strip.shape), far, near, own, corner, corners, corners)
    else:
        (sent,) = call(join_kernel, (joined,), (mine, received, last_sums), name="join")
        values = stage(sent, rest[0])
        halo = extend(grad, flags)
    for pair in rest[1:]:
        (sent,) = call(add_kernel, (shape(sent.shape, BF16),), (*values, halo[2]), name="add")
        values = stage(sent, pair)
    field_grad, token = call(
        backward_kernel,
        (shape(tile, BF16), shape((LANE, channels), F32)),
        (grad, *halo, upstream, sea, kernel_taps, flags),
        [pltpu.VMEM(wide, F32), spread, spread],
        work=3 * 10**9,
        name="backward",
    )
    (total,) = call(add_kernel, (shape(joined.shape, F32),), (*values, token), name="add")
    back = partners(total, core)
    count = rows * cols * lax.axis_size("lon") * lax.axis_size("lat") * lax.axis_size("ens")
    kernel_grad, norm_grad, up_grad, down_grad = call(
        functools.partial(final_kernel, factor=1.0 / math.sqrt(count)),
        (shape((TAPS, channels), F32), shape((2, channels), F32), shape((channels, hidden), F32), shape((hidden, channels), F32)),
        (total, back, flags),
        name="final",
    )
    return output[None], field_grad[None], kernel_grad, norm_grad, up_grad, down_grad


def solution(mesh):
    grid = P("ens", "lat", "lon", None)
    return jax.shard_map(
        shards,
        mesh=mesh,
        in_specs=(grid, grid, P("lat", "lon"), P(), P(), P(), P(), P()),
        out_specs=(grid, grid, P(), P(), P(), P()),
        check_vma=False,
    )
```

time: 52.8 us -> 48.3 us (0.915)
  waiting for transfers between devices: 14.3 us -> 11.4 us
  Pallas kernels: 13.3 us -> 11.3 us
  starting transfers between devices: 22.1 us -> 22.7 us
    ppermute x2 -> x0, starting transfers between devices: 7.03 us -> none  [across(): lax.ppermute(top[::-1, ::-1], 'lon', [(i, lons - 1 - i) for i in range(lo...]
    ppermute x6 -> x10, starting transfers between devices: 6.97 us -> 13.7 us  [xor_partner(): lax.ppermute(value, axis, [(i, i ^ bits) for i in range(lax.axis_size(axi...]
    ppermute x6 -> x10, waiting for transfers between devices: 8.5 us -> 4.94 us  [xor_partner(): lax.ppermute(value, axis, [(i, i ^ bits) for i in range(lax.axis_size(axi...]
    ppermute x8, waiting for transfers between devices: 4.41 us -> 6.49 us  [partners(): lax.ppermute(value, axes, route(axes, lambda *at: [i ^ flip[a] for a, i i...]
    pallas_call x8 -> x15, Pallas kernels: 13.3 us -> 11.3 us  [call(): pl.pallas_call(kernel, out_shape=outs, in_specs=[hbm if n in far else vme...]
    ppermute x2 -> x0, waiting for transfers between devices: 1.37 us -> none  [across(): lax.ppermute(top[::-1, ::-1], 'lon', [(i, lons - 1 - i) for i in range(lo...]
    ppermute x8, starting transfers between devices: 8.15 us -> 9.05 us  [partners(): lax.ppermute(value, axes, route(axes, lambda *at: [i ^ flip[a] for a, i i...]
  transfers between devices with their start and end apart: 16 -> 18, of which waited for: 8 -> 7; matrix products, arithmetic and copies ran while one was open for 0% -> 0% of each run, Pallas kernels for 7% -> 17%
where the time goes in v4:
time: 48.3 us; the launch traced here: 48.1 us
  starting transfers between devices  22.7 us (47%)
  waiting for transfers between devices  11.4 us (24%)
  Pallas kernels  11.3 us (23%)
  local copies, waits for them, and re-layouts  1.75 us (4%)
  between operations  0.88 us (2%)
    ppermute x10, starting transfers between devices, xor_partner(): lax.ppermute(value, axis, [(i, i ^ bits) for i in range(lax.axis_size(axi...  13.7 us
    pallas_call x15, Pallas kernels, call(): pl.pallas_call(kernel, out_shape=outs, in_specs=[hbm if n in far else vme...  11.3 us
    ppermute x8, starting transfers between devices, partners(): lax.ppermute(value, axes, route(axes, lambda *at: [i ^ flip[a] for a, i i...  9.05 us
    ppermute x8, waiting for transfers between devices, partners(): lax.ppermute(value, axes, route(axes, lambda *at: [i ^ flip[a] for a, i i...  6.49 us
    ppermute x10, waiting for transfers between devices, xor_partner(): lax.ppermute(value, axis, [(i, i ^ bits) for i in range(lax.axis_size(axi...  4.94 us
    unnamed x16, local copies, waits for them, and re-layouts  1.66 us
  transfers between devices with their start and end apart: 18, of which 7 were waited for; matrix products, arithmetic and copies ran while one was open for 0% of the time, Pallas kernels for 17%

profile of v4, /device:TPU:0, one launch (start us, length us, event | category | flops | bytes accessed | tf_op | source)
XLA Modules:
  0.0 48.1 jit_solution(17157369966690626766)
XLA Ops:
  0.7 0.9 %copy-done.6 = bf16[1,16,64,128]{3,2,1,0:T(8,128)(2,1)S(1)} copy-done((bf16[1,16,64,128]{3,2,1,0:T(8,128)(2,1)S(1)}, bf16[1,16,64,128]{3,2,1,0:T(8,128)(2,1)}, u32[]{:S(2)}) %copy-start.6) | copy-done | bytes 262168
  1.6 0.7 %copy-done.7 = s32[16,64]{1,0:T(8,128)S(1)} copy-done((s32[16,64]{1,0:T(8,128)S(1)}, s32[16,64]{1,0:T(8,128)}, u32[]{:S(2)}) %copy-start.7) | copy-done | bytes 4120
  2.3 0.4 mask.2
  2.8 0.1 iota.16.flags.refs_11_.refs_15_
  2.9 0.2 fold.2
  3.0 5.1 %collective-permute-start.1 = (bf16[512,128]{1,0:T(8,128)(2,1)S(1)}, bf16[512,128]{1,0:T(8,128)(2,1)S(1)}, u32[]{:S(2)}, u32[]{:S(2)}) collective-permute-start(bf16[512,128]{1,0:T(8,128)(2,1)S(1)} %get-tuple-element.66), channel_id=1, source_target_pairs={{0,24},{8,16},{16,8},{24,0},{1,25},{9,17},{17,9},{25,1},{2,26},{10... | collective-permute-start | bytes 393224 | tf_op jit(solution)/shard_map/ppermute | solution.py:47
  8.1 1.5 %collective-permute-start = (bf16[6,64,128]{2,1,0:T(8,128)(2,1)S(1)}, bf16[6,64,128]{2,1,0:T(8,128)(2,1)S(1)}, u32[]{:S(2)}, u32[]{:S(2)}) collective-permute-start(bf16[6,64,128]{2,1,0:T(8,128)(2,1)S(1)} %get-tuple-element.55), channel_id=1, source_target_pairs={{0,4},{4,0},{1,5},{5,1},{2,6},{6,2},{3,7},{7,3},{8,12},{12,8},{9,1... | collective-permute-start | bytes 294920 | tf_op jit(solution)/shard_map/ppermute | solution.py:47
  9.6 0.0 collective-permute-start.2
  9.6 0.8 %collective-permute-start.3 = (bf16[6,8,128]{2,1,0:T(8,128)(2,1)S(1)}, bf16[6,8,128]{2,1,0:T(8,128)(2,1)S(1)}, u32[]{:S(2)}, u32[]{:S(2)}) collective-permute-start(bf16[6,8,128]{2,1,0:T(8,128)(2,1)S(1)} %get-tuple-element.77), channel_id=1, source_target_pairs={{0,16},{8,24},{16,0},{24,8},{1,17},{9,25},{17,1},{25,9},{2,18},{10... | collective-permute-start | bytes 36872 | tf_op jit(solution)/shard_map/ppermute | solution.py:47
  10.4 2.3 %collective-permute-done.below.refs_8_ = bf16[6,64,128]{2,1,0:T(8,128)(2,1)S(1)} collective-permute-done((bf16[6,64,128]{2,1,0:T(8,128)(2,1)S(1)}, bf16[6,64,128]{2,1,0:T(8,128)(2,1)S(1)}, u32[]{:S(2)}, u32[]{:S(2)}) %collective-permute-start) | collective-permute-done | bytes 98336 | tf_op jit(solution)/shard_map/ppermute | solution.py:47
  12.8 1.8 %lower.1 = (f32[28,80,128]{2,1,0:T(8,128)S(1)}, f32[16,64,128]{2,1,0:T(8,128)S(1)}, bf16[16,64,128]{2,1,0:T(8,128)(2,1)S(1)}, bf16[16,64,128]{2,1,0:T(8,128)(2,1...) custom-call(bf16[16,64,128]{2,1,0:T(8,128)(2,1)S(1)} %get-tuple-elem, ...), custom_call_target="tpu_custom_call" | custom-call | flops 100000000 | bytes 3773952 | tf_op jit(solution)/shard_map/lower/pallas_call | solution.py:457
  14.7 0.0 collective-permute-done.1
  14.7 0.0 collective-permute-done.3.refs_0_.refs_11_
  14.7 0.0 collective-permute-done.2.near.refs_9_
  14.7 1.6 %collective-permute-start.4 = (bf16[6,16,128]{2,1,0:T(8,128)(2,1)S(1)}, bf16[6,16,128]{2,1,0:T(8,128)(2,1)S(1)}, u32[]{:S(2)}, u32[]{:S(2)}) collective-permute-start(bf16[6,16,128]{2,1,0:T(8,128)(2,1)S(1)} %corners.1), channel_id=1, source_target_pairs={{0,4},{4,0},{1,5},{5,1},{2,6},{6,2},{3,7},{7,3},{8,12},{12,8},{9,1... | collective-permute-start | bytes 73736 | tf_op jit(solution)/shard_map/ppermute | solution.py:47
  16.3 1.6 %upper.1 = (f32[28,80,128]{2,1,0:T(8,128)S(1)}, f32[16,64,128]{2,1,0:T(8,128)S(1)}, bf16[16,64,128]{2,1,0:T(8,128)(2,1)S(1)}, bf16[16,64,128]{2,1,0:T(8,128)(2,1...) custom-call(f32[28,80,128]{2,1,0:T(8,128)S(1)} %get-tuple-element.57, ...), custom_call_target="tpu_custom_call", output_to_operand_aliasing={{0}: (0, {}), {1}: (1, {}), {2}: (2, {}), {3}: (3, {}), {4}... | custom-call | flops 2000000000 | bytes 6075904 | tf_op jit(solution)/shard_map/upper/pallas_call | solution.py:457
  17.9 0.7 %collective-permute-done.4.refs_12_.refs_13_ = bf16[6,16,128]{2,1,0:T(8,128)(2,1)S(1)} collective-permute-done((bf16[6,16,128]{2,1,0:T(8,128)(2,1)S(1)}, bf16[6,16,128]{2,1,0:T(8,128)(2,1)S(1)}, u32[]{:S(2)}, u32[]{:S(2)}) %collective-permute-start.4) | collective-permute-done | bytes 24608 | tf_op jit(solution)/shard_map/ppermute | solution.py:47
  18.6 1.5 %edge.1 = (f32[28,80,128]{2,1,0:T(8,128)S(1)}, f32[16,64,128]{2,1,0:T(8,128)S(1)}, bf16[16,64,128]{2,1,0:T(8,128)(2,1)S(1)}, bf16[16,64,128]{2,1,0:T(8,128)(2,1)...) custom-call(f32[28,80,128]{2,1,0:T(8,128)S(1)} %get-tuple-element.67, ...), custom_call_target="tpu_custom_call", output_to_operand_aliasing={{0}: (0, {}), {1}: (1, {}), {2}: (2, {}), {3}: (3, {}), {4}... | custom-call | flops 1000000000 | bytes 6215168 | tf_op jit(solution)/shard_map/edge/pallas_call | solution.py:457
  20.1 1.6 %collective-permute-start.5 = (bf16[6,64,128]{2,1,0:T(8,128)(2,1)S(1)}, bf16[6,64,128]{2,1,0:T(8,128)(2,1)S(1)}, u32[]{:S(2)}, u32[]{:S(2)}) collective-permute-start(bf16[6,64,128]{2,1,0:T(8,128)(2,1)S(1)} %get-tuple-element.84), channel_id=1, source_target_pairs={{0,4},{4,0},{1,5},{5,1},{2,6},{6,2},{3,7},{7,3},{8,12},{12,8},{9,1... | collective-permute-start | bytes 294920 | tf_op jit(solution)/shard_map/ppermute | solution.py:47
  21.7 0.0 collective-permute-start.6
  21.7 0.6 %collective-permute-start.9 = (bf16[16,8,128]{2,1,0:T(8,128)(2,1)S(1)}, bf16[16,8,128]{2,1,0:T(8,128)(2,1)S(1)}, u32[]{:S(2)}, u32[]{:S(2)}) collective-permute-start(bf16[16,8,128]{2,1,0:T(8,128)(2,1)S(1)} %get-tuple-element.89), channel_id=1, source_target_pairs={{0,8},{8,0},{16,24},{24,16},{1,9},{9,1},{17,25},{25,17},{2,10},{10... | collective-permute-start | bytes 98312 | tf_op jit(solution)/shard_map/ppermute | solution.py:47
  22.3 1.8 %collective-permute-start.8 = (bf16[16,8,128]{2,1,0:T(8,128)(2,1)S(1)}, bf16[16,8,128]{2,1,0:T(8,128)(2,1)S(1)}, u32[]{:S(2)}, u32[]{:S(2)}) collective-permute-start(bf16[16,8,128]{2,1,0:T(8,128)(2,1)S(1)} %get-tuple-element.85.far), channel_id=1, source_target_pairs={{0,24},{8,16},{16,8},{24,0},{1,25},{9,17},{17,9},{25,1},{2,26},{10... | collective-permute-start | bytes 98312 | tf_op jit(solution)/shard_map/ppermute | solution.py:47
  24.1 1.9 %kernel_gradient.1 = (bf16[16,64,128]{2,1,0:T(8,128)(2,1)}, f32[64,128]{1,0:T(8,128)S(1)}) custom-call(f32[28,80,128]{2,1,0:T(8,128)S(1)} %get-tuple-element.78.wide, f32[16,64,128]{2,1,0:T(8,128)S(1)} %get-tuple-element.79.mixed, bf16[16,64,128]{2,1,0:T(8,128)(2,1)S(1)} %get-tuple-element.80.result, f32[2,8,128]{2,1,0:T(8,128)S(1)} %get-tuple-element.81.norm), custom_call_target="tpu_custom_call" | custom-call | flops 100000000 | bytes 2236416 | tf_op jit(solution)/shard_map/kernel_gradient/pallas_call | solution.py:457
  25.9 0.0 collective-permute-done.6.refs_1_.core
  25.9 0.0 collective-permute-done.5.refs_0_.below.above
  25.9 0.2 fold.3
  26.1 0.0 collective-permute-done.9.near
  26.1 1.9 %collective-permute-done.8.far = bf16[16,8,128]{2,1,0:T(8,128)(2,1)S(1)} collective-permute-done((bf16[16,8,128]{2,1,0:T(8,128)(2,1)S(1)}, bf16[16,8,128]{2,1,0:T(8,128)(2,1)S(1)}, u32[]{:S(2)}, u32[]{:S(2)}) %collective-permute-start.8) | collective-permute-done | bytes 32800 | tf_op jit(solution)/shard_map/ppermute | solution.py:47
  28.0 1.6 %collective-permute-start.11 = (bf16[416,128]{1,0:T(8,128)(2,1)S(1)}, bf16[416,128]{1,0:T(8,128)(2,1)S(1)}, u32[]{:S(2)}, u32[]{:S(2)}) collective-permute-start(bf16[416,128]{1,0:T(8,128)(2,1)S(1)} %get-tuple-element.93), channel_id=1, source_target_pairs={{0,4},{4,0},{1,5},{5,1},{2,6},{6,2},{3,7},{7,3},{8,12},{12,8},{9,1... | collective-permute-start | bytes 319496 | tf_op jit(solution)/shard_map/ppermute | solution.py:165
  29.6 0.8 %collective-permute-start.7 = (bf16[384,128]{1,0:T(8,128)(2,1)S(1)}, bf16[384,128]{1,0:T(8,128)(2,1)S(1)}, u32[]{:S(2)}, u32[]{:S(2)}) collective-permute-start(bf16[384,128]{1,0:T(8,128)(2,1)S(1)} %get-tuple-element.88), channel_id=1, source_target_pairs={{0,24},{8,16},{16,8},{24,0},{1,25},{9,17},{17,9},{25,1},{2,26},{10... | collective-permute-start | bytes 294920 | tf_op jit(solution)/shard_map/ppermute | solution.py:47
  30.4 2.5 %collective-permute-start.13 = (bf16[320,128]{1,0:T(8,128)(2,1)S(1)}, bf16[320,128]{1,0:T(8,128)(2,1)S(1)}, u32[]{:S(2)}, u32[]{:S(2)}) collective-permute-start(bf16[320,128]{1,0:T(8,128)(2,1)S(1)} %get-tuple-element.96.refs_0_), channel_id=1, source_target_pairs={{0,6},{1,7},{2,4},{3,5},{4,2},{5,3},{6,0},{7,1},{8,14},{9,15},{10,... | collective-permute-start | bytes 245768 | tf_op jit(solution)/shard_map/ppermute | solution.py:165
  32.9 0.5 %collective-permute-start.12 = (bf16[320,128]{1,0:T(8,128)(2,1)S(1)}, bf16[320,128]{1,0:T(8,128)(2,1)S(1)}, u32[]{:S(2)}, u32[]{:S(2)}) collective-permute-start(bf16[320,128]{1,0:T(8,128)(2,1)S(1)} %get-tuple-element.96.refs_0_), channel_id=1, source_target_pairs={{0,2},{1,3},{2,0},{3,1},{4,6},{5,7},{6,4},{7,5},{8,10},{9,11},{10,... | collective-permute-start | bytes 245768 | tf_op jit(solution)/shard_map/ppermute | solution.py:165
  33.4 0.0 collective-permute-start.10
  33.4 2.5 %collective-permute-done.13.refs_3_ = bf16[320,128]{1,0:T(8,128)(2,1)S(1)} collective-permute-done((bf16[320,128]{1,0:T(8,128)(2,1)S(1)}, bf16[320,128]{1,0:T(8,128)(2,1)S(1)}, u32[]{:S(2)}, u32[]{:S(2)}) %collective-permute-start.13) | collective-permute-done | bytes 81952 | tf_op jit(solution)/shard_map/ppermute | solution.py:165
  35.8 1.5 %collective-permute-done.12.refs_1_ = bf16[320,128]{1,0:T(8,128)(2,1)S(1)} collective-permute-done((bf16[320,128]{1,0:T(8,128)(2,1)S(1)}, bf16[320,128]{1,0:T(8,128)(2,1)S(1)}, u32[]{:S(2)}, u32[]{:S(2)}) %collective-permute-start.12) | collective-permute-done | bytes 81952 | tf_op jit(solution)/shard_map/ppermute | solution.py:165
  37.3 0.0 collective-permute-done.7
  37.3 0.0 collective-permute-done.11.refs_2_
  37.4 2.4 %collective-permute-start.16 = (bf16[320,128]{1,0:T(8,128)(2,1)S(1)}, bf16[320,128]{1,0:T(8,128)(2,1)S(1)}, u32[]{:S(2)}, u32[]{:S(2)}) collective-permute-start(bf16[320,128]{1,0:T(8,128)(2,1)S(1)} %add.34.refs_0_), channel_id=1, source_target_pairs={{0,24},{8,16},{16,8},{24,0},{1,25},{9,17},{17,9},{25,1},{2,26},{10... | collective-permute-start | bytes 245768 | tf_op jit(solution)/shard_map/ppermute | solution.py:165
  39.8 0.0 collective-permute-start.15
  39.8 2.0 %collective-permute-start.14 = (bf16[320,128]{1,0:T(8,128)(2,1)S(1)}, bf16[320,128]{1,0:T(8,128)(2,1)S(1)}, u32[]{:S(2)}, u32[]{:S(2)}) collective-permute-start(bf16[320,128]{1,0:T(8,128)(2,1)S(1)} %add.34.refs_0_), channel_id=1, source_target_pairs={{0,8},{8,0},{16,24},{24,16},{1,9},{9,1},{17,25},{25,17},{2,10},{10... | collective-permute-start | bytes 245768 | tf_op jit(solution)/shard_map/ppermute | solution.py:165
  41.8 0.0 collective-permute-done.10.corner
  41.8 2.9 %backward.1 = (bf16[16,64,128]{2,1,0:T(8,128)(2,1)}, f32[8,128]{1,0:T(8,128)S(1)}) custom-call(bf16[16,64,128]{2,1,0:T(8,128)(2,1)S(1)} %get-tuple-element.83.block, bf16[6,64,128]{2,1,0:T(8,128)(2,1)S(1)} %collective-permute-done.5.refs_0_.below.above, bf16[6,64,128]{2,1,0:T(8,128)(2,1)S(1)} %collective-permute-done.5.refs_0_.below.above, ...), custom_call_target="tpu_custom_call" | custom-call | flops 3000000000 | bytes 1516032 | tf_op jit(solution)/shard_map/backward/pallas_call | solution.py:457
  44.7 0.0 collective-permute-done.16.refs_3_
  44.7 1.2 %collective-permute-done.15.refs_2_ = bf16[320,128]{1,0:T(8,128)(2,1)S(1)} collective-permute-done((bf16[320,128]{1,0:T(8,128)(2,1)S(1)}, bf16[320,128]{1,0:T(8,128)(2,1)S(1)}, u32[]{:S(2)}, u32[]{:S(2)}) %collective-permute-start.15) | collective-permute-done | bytes 81952 | tf_op jit(solution)/shard_map/ppermute | solution.py:165
  45.8 0.0 collective-permute-done.14.refs_1_
  45.9 0.1 collective-permute-start.17
  46.0 1.4 %collective-permute-done.17.back = f32[320,128]{1,0:T(8,128)S(1)} collective-permute-done((f32[320,128]{1,0:T(8,128)S(1)}, f32[320,128]{1,0:T(8,128)S(1)}, u32[]{:S(2)}, u32[]{:S(2)}) %collective-permute-start.17) | collective-permute-done | bytes 163872 | tf_op jit(solution)/shard_map/ppermute | solution.py:165
  47.3 0.7 %final.1 = (f32[49,128]{1,0:T(8,128)}, f32[2,128]{1,0:T(2,128)}, f32[128,256]{1,0:T(8,128)}, f32[256,128]{1,0:T(8,128)}) custom-call(f32[320,128]{1,0:T(8,128)S(1)} %add.35.total, f32[320,128]{1,0:T(8,128)S(1)} %collective-permute-done.17.back, s32[8,128]{1,0:T(8,128)S(1)} %iota.16.flags.refs_11_.refs_15_), custom_call_target="tpu_custom_call" | custom-call | bytes 620032 | tf_op jit(solution)/shard_map/final/pallas_call | solution.py:457
  (24 shorter events, 0.3 us)
Async XLA Ops:
  0.7 1.0 %copy-start.6 = (bf16[1,16,64,128]{3,2,1,0:T(8,128)(2,1)S(1)}, bf16[1,16,64,128]{3,2,1,0:T(8,128)(2,1)}, u32[]{:S(2)}) copy-start(bf16[1,16,64,128]{3,2,1,0:T(8,128)(2,1)} %param.8) | copy-start | bytes 786436
  1.6 0.7 %copy-start.7 = (s32[16,64]{1,0:T(8,128)S(1)}, s32[16,64]{1,0:T(8,128)}, u32[]{:S(2)}) copy-start(s32[16,64]{1,0:T(8,128)} %mask.3) | copy-start | bytes 12292
  2.3 10.5 %copy-start = (bf16[1,16,64,128]{3,2,1,0:T(8,128)(2,1)S(1)}, bf16[1,16,64,128]{3,2,1,0:T(8,128)(2,1)}, u32[]{:S(2)}) copy-start(bf16[1,16,64,128]{3,2,1,0:T(8,128)(2,1)} %param.9) | copy-start | bytes 786436
  2.3 10.5 %copy-start.1 = (bf16[128,256]{1,0:T(8,128)(2,1)S(1)}, bf16[128,256]{1,0:T(8,128)(2,1)}, u32[]{:S(2)}) copy-start(bf16[128,256]{1,0:T(8,128)(2,1)} %refs_19_.1) | copy-start | bytes 196612
  2.3 10.5 %copy-start.2 = (bf16[256,128]{1,0:T(8,128)(2,1)S(1)}, bf16[256,128]{1,0:T(8,128)(2,1)}, u32[]{:S(2)}) copy-start(bf16[256,128]{1,0:T(8,128)(2,1)} %refs_20_.1) | copy-start | bytes 196612
  2.3 10.5 %copy-start.3 = (f32[49,128]{1,0:T(8,128)S(1)}, f32[49,128]{1,0:T(8,128)}, u32[]{:S(2)}) copy-start(f32[49,128]{1,0:T(8,128)} %taps.1) | copy-start | bytes 75268
  2.3 10.5 %copy-start.4 = (f32[128]{0:T(128)S(1)}, f32[128]{0:T(128)}, u32[]{:S(2)}) copy-start(f32[128]{0:T(128)} %param.12) | copy-start | bytes 1540
  2.3 10.5 %copy-start.5 = (f32[128]{0:T(128)S(1)}, f32[128]{0:T(128)}, u32[]{:S(2)}) copy-start(f32[128]{0:T(128)} %param.13) | copy-start | bytes 1540
  3.0 11.6 %collective-permute-start.1 = (bf16[512,128]{1,0:T(8,128)(2,1)S(1)}, bf16[512,128]{1,0:T(8,128)(2,1)S(1)}, u32[]{:S(2)}, u32[]{:S(2)}) collective-permute-start(bf16[512,128]{1,0:T(8,128)(2,1)S(1)} %get-tuple-element.66), channel_id=1, source_target_pairs={{0,24},{8,16},{16,8},{24,0},{1,25},{9,17},{17,9},{25,1},{2,26},{10... | collective-permute-start | bytes 393224 | tf_op jit(solution)/shard_map/ppermute | solution.py:47
  8.1 4.6 %collective-permute-start = (bf16[6,64,128]{2,1,0:T(8,128)(2,1)S(1)}, bf16[6,64,128]{2,1,0:T(8,128)(2,1)S(1)}, u32[]{:S(2)}, u32[]{:S(2)}) collective-permute-start(bf16[6,64,128]{2,1,0:T(8,128)(2,1)S(1)} %get-tuple-element.55), channel_id=1, source_target_pairs={{0,4},{4,0},{1,5},{5,1},{2,6},{6,2},{3,7},{7,3},{8,12},{12,8},{9,1... | collective-permute-start | bytes 294920 | tf_op jit(solution)/shard_map/ppermute | solution.py:47
  9.6 5.0 %collective-permute-start.2 = (bf16[16,8,128]{2,1,0:T(8,128)(2,1)S(1)}, bf16[16,8,128]{2,1,0:T(8,128)(2,1)S(1)}, u32[]{:S(2)}, u32[]{:S(2)}) collective-permute-start(bf16[16,8,128]{2,1,0:T(8,128)(2,1)S(1)} %get-tuple-element.75), channel_id=1, source_target_pairs={{0,8},{8,0},{16,24},{24,16},{1,9},{9,1},{17,25},{25,17},{2,10},{10... | collective-permute-start | bytes 98312 | tf_op jit(solution)/shard_map/ppermute | solution.py:47
  9.6 5.0 %collective-permute-start.3 = (bf16[6,8,128]{2,1,0:T(8,128)(2,1)S(1)}, bf16[6,8,128]{2,1,0:T(8,128)(2,1)S(1)}, u32[]{:S(2)}, u32[]{:S(2)}) collective-permute-start(bf16[6,8,128]{2,1,0:T(8,128)(2,1)S(1)} %get-tuple-element.77), channel_id=1, source_target_pairs={{0,16},{8,24},{16,0},{24,8},{1,17},{9,25},{17,1},{25,9},{2,18},{10... | collective-permute-start | bytes 36872 | tf_op jit(solution)/shard_map/ppermute | solution.py:47
  14.7 3.9 %collective-permute-start.4 = (bf16[6,16,128]{2,1,0:T(8,128)(2,1)S(1)}, bf16[6,16,128]{2,1,0:T(8,128)(2,1)S(1)}, u32[]{:S(2)}, u32[]{:S(2)}) collective-permute-start(bf16[6,16,128]{2,1,0:T(8,128)(2,1)S(1)} %corners.1), channel_id=1, source_target_pairs={{0,4},{4,0},{1,5},{5,1},{2,6},{6,2},{3,7},{7,3},{8,12},{12,8},{9,1... | collective-permute-start | bytes 73736 | tf_op jit(solution)/shard_map/ppermute | solution.py:47
  20.1 5.8 %collective-permute-start.5 = (bf16[6,64,128]{2,1,0:T(8,128)(2,1)S(1)}, bf16[6,64,128]{2,1,0:T(8,128)(2,1)S(1)}, u32[]{:S(2)}, u32[]{:S(2)}) collective-permute-start(bf16[6,64,128]{2,1,0:T(8,128)(2,1)S(1)} %get-tuple-element.84), channel_id=1, source_target_pairs={{0,4},{4,0},{1,5},{5,1},{2,6},{6,2},{3,7},{7,3},{8,12},{12,8},{9,1... | collective-permute-start | bytes 294920 | tf_op jit(solution)/shard_map/ppermute | solution.py:47
  21.7 4.2 %collective-permute-start.6 = (bf16[256,128]{1,0:T(8,128)(2,1)S(1)}, bf16[256,128]{1,0:T(8,128)(2,1)S(1)}, u32[]{:S(2)}, u32[]{:S(2)}) collective-permute-start(bf16[256,128]{1,0:T(8,128)(2,1)S(1)} %get-tuple-element.86), channel_id=1, source_target_pairs={{0,1},{1,0},{2,3},{3,2},{4,5},{5,4},{6,7},{7,6},{8,9},{9,8},{10,11... | collective-permute-start | bytes 196616 | tf_op jit(solution)/shard_map/ppermute | solution.py:165
  21.7 4.4 %collective-permute-start.9 = (bf16[16,8,128]{2,1,0:T(8,128)(2,1)S(1)}, bf16[16,8,128]{2,1,0:T(8,128)(2,1)S(1)}, u32[]{:S(2)}, u32[]{:S(2)}) collective-permute-start(bf16[16,8,128]{2,1,0:T(8,128)(2,1)S(1)} %get-tuple-element.89), channel_id=1, source_target_pairs={{0,8},{8,0},{16,24},{24,16},{1,9},{9,1},{17,25},{25,17},{2,10},{10... | collective-permute-start | bytes 98312 | tf_op jit(solution)/shard_map/ppermute | solution.py:47
  22.3 5.7 %collective-permute-start.8 = (bf16[16,8,128]{2,1,0:T(8,128)(2,1)S(1)}, bf16[16,8,128]{2,1,0:T(8,128)(2,1)S(1)}, u32[]{:S(2)}, u32[]{:S(2)}) collective-permute-start(bf16[16,8,128]{2,1,0:T(8,128)(2,1)S(1)} %get-tuple-element.85.far), channel_id=1, source_target_pairs={{0,24},{8,16},{16,8},{24,0},{1,25},{9,17},{17,9},{25,1},{2,26},{10... | collective-permute-start | bytes 98312 | tf_op jit(solution)/shard_map/ppermute | solution.py:47
  28.0 9.3 %collective-permute-start.11 = (bf16[416,128]{1,0:T(8,128)(2,1)S(1)}, bf16[416,128]{1,0:T(8,128)(2,1)S(1)}, u32[]{:S(2)}, u32[]{:S(2)}) collective-permute-start(bf16[416,128]{1,0:T(8,128)(2,1)S(1)} %get-tuple-element.93), channel_id=1, source_target_pairs={{0,4},{4,0},{1,5},{5,1},{2,6},{6,2},{3,7},{7,3},{8,12},{12,8},{9,1... | collective-permute-start | bytes 319496 | tf_op jit(solution)/shard_map/ppermute | solution.py:165
  29.6 7.7 %collective-permute-start.7 = (bf16[384,128]{1,0:T(8,128)(2,1)S(1)}, bf16[384,128]{1,0:T(8,128)(2,1)S(1)}, u32[]{:S(2)}, u32[]{:S(2)}) collective-permute-start(bf16[384,128]{1,0:T(8,128)(2,1)S(1)} %get-tuple-element.88), channel_id=1, source_target_pairs={{0,24},{8,16},{16,8},{24,0},{1,25},{9,17},{17,9},{25,1},{2,26},{10... | collective-permute-start | bytes 294920 | tf_op jit(solution)/shard_map/ppermute | solution.py:47
  30.4 5.4 %collective-permute-start.13 = (bf16[320,128]{1,0:T(8,128)(2,1)S(1)}, bf16[320,128]{1,0:T(8,128)(2,1)S(1)}, u32[]{:S(2)}, u32[]{:S(2)}) collective-permute-start(bf16[320,128]{1,0:T(8,128)(2,1)S(1)} %get-tuple-element.96.refs_0_), channel_id=1, source_target_pairs={{0,6},{1,7},{2,4},{3,5},{4,2},{5,3},{6,0},{7,1},{8,14},{9,15},{10,... | collective-permute-start | bytes 245768 | tf_op jit(solution)/shard_map/ppermute | solution.py:165
  32.9 4.4 %collective-permute-start.12 = (bf16[320,128]{1,0:T(8,128)(2,1)S(1)}, bf16[320,128]{1,0:T(8,128)(2,1)S(1)}, u32[]{:S(2)}, u32[]{:S(2)}) collective-permute-start(bf16[320,128]{1,0:T(8,128)(2,1)S(1)} %get-tuple-element.96.refs_0_), channel_id=1, source_target_pairs={{0,2},{1,3},{2,0},{3,1},{4,6},{5,7},{6,4},{7,5},{8,10},{9,11},{10,... | collective-permute-start | bytes 245768 | tf_op jit(solution)/shard_map/ppermute | solution.py:165
  33.4 8.5 %collective-permute-start.10 = (bf16[6,8,128]{2,1,0:T(8,128)(2,1)S(1)}, bf16[6,8,128]{2,1,0:T(8,128)(2,1)S(1)}, u32[]{:S(2)}, u32[]{:S(2)}) collective-permute-start(bf16[6,8,128]{2,1,0:T(8,128)(2,1)S(1)} %get-tuple-element.91), channel_id=1, source_target_pairs={{0,16},{8,24},{16,0},{24,8},{1,17},{9,25},{17,1},{25,9},{2,18},{10... | collective-permute-start | bytes 36872 | tf_op jit(solution)/shard_map/ppermute | solution.py:47
  37.4 7.3 %collective-permute-start.16 = (bf16[320,128]{1,0:T(8,128)(2,1)S(1)}, bf16[320,128]{1,0:T(8,128)(2,1)S(1)}, u32[]{:S(2)}, u32[]{:S(2)}) collective-permute-start(bf16[320,128]{1,0:T(8,128)(2,1)S(1)} %add.34.refs_0_), channel_id=1, source_target_pairs={{0,24},{8,16},{16,8},{24,0},{1,25},{9,17},{17,9},{25,1},{2,26},{10... | collective-permute-start | bytes 245768 | tf_op jit(solution)/shard_map/ppermute | solution.py:165
  39.8 6.1 %collective-permute-start.15 = (bf16[320,128]{1,0:T(8,128)(2,1)S(1)}, bf16[320,128]{1,0:T(8,128)(2,1)S(1)}, u32[]{:S(2)}, u32[]{:S(2)}) collective-permute-start(bf16[320,128]{1,0:T(8,128)(2,1)S(1)} %add.34.refs_0_), channel_id=1, source_target_pairs={{0,16},{8,24},{16,0},{24,8},{1,17},{9,25},{17,1},{25,9},{2,18},{10... | collective-permute-start | bytes 245768 | tf_op jit(solution)/shard_map/ppermute | solution.py:165
  39.8 6.1 %collective-permute-start.14 = (bf16[320,128]{1,0:T(8,128)(2,1)S(1)}, bf16[320,128]{1,0:T(8,128)(2,1)S(1)}, u32[]{:S(2)}, u32[]{:S(2)}) collective-permute-start(bf16[320,128]{1,0:T(8,128)(2,1)S(1)} %add.34.refs_0_), channel_id=1, source_target_pairs={{0,8},{8,0},{16,24},{24,16},{1,9},{9,1},{17,25},{25,17},{2,10},{10... | collective-permute-start | bytes 245768 | tf_op jit(solution)/shard_map/ppermute | solution.py:165
  45.9 1.5 %collective-permute-start.17 = (f32[320,128]{1,0:T(8,128)S(1)}, f32[320,128]{1,0:T(8,128)S(1)}, u32[]{:S(2)}, u32[]{:S(2)}) collective-permute-start(f32[320,128]{1,0:T(8,128)S(1)} %add.35.total), channel_id=1, source_target_pairs={{0,1},{1,0},{2,3},{3,2},{4,5},{5,4},{6,7},{7,6},{8,9},{9,8},{10,11... | collective-permute-start | bytes 491528 | tf_op jit(solution)/shard_map/ppermute | solution.py:165

commit v5 on v4

--- a/solution.py
+++ b/solution.py
@@ -47,6 +47,7 @@
     return lax.ppermute(value, axis, [(i, i ^ bits) for i in range(lax.axis_size(axis))])
 
 
+JOIN_TOKEN = 3
 NORTHERN, ODD, INNER, CORE = range(4)
 
 
@@ -77,14 +78,12 @@
 def fold_kernel(block, flags, far, *refs):
     joint, corner, own = refs[-3:]
     rows, cols, channels = block.shape
-    start = 0
+    start = rows * LANE
     odd = on(flags, ODD)
     down = lax.broadcasted_iota(jnp.int32, (cols, cols), 0)
     across = lax.broadcasted_iota(jnp.int32, (cols, cols), 1)
     turn = jnp.where(down + across == cols - 1, 1.0, 0.0).astype(BF16)
-    if joint.shape[0] > REACH * cols:
-        start = rows * LANE
-        joint[:start] = far[...].astype(F32).reshape(start, channels).astype(BF16)
+    joint[:start] = far[...].astype(F32).reshape(start, channels).astype(BF16)
     for k in range(REACH):
         row = jnp.dot(turn, block[rows - 1 - k], preferred_element_type=F32)
         joint[start + k * cols : start + (k + 1) * cols] = row.astype(BF16)
@@ -93,7 +92,8 @@
         own[k] = jnp.where(odd, head, tail).astype(BF16)
 
 
-def put_corners(near, far, flags, facing, start=None):
+def corner_kernel(near, far, flags, *refs):
+    (facing,) = refs[-1:]
     rows = near.shape[0]
     northern, odd = on(flags, NORTHERN), on(flags, ODD)
     for k in range(REACH):
@@ -101,12 +101,7 @@
             jnp.where(northern, a[k].astype(F32), a[rows - REACH + k].astype(F32)) for a in (far, near)
         )
         sides = [jnp.where(odd, two, one), jnp.where(odd, one, two)]
-        at = k if start is None else slice(start + k * 2 * LANE, start + (k + 1) * 2 * LANE)
-        facing[at] = jnp.concatenate(sides, 0).astype(BF16)
-
-
-def corner_kernel(near, far, flags, *refs):
-    put_corners(near, far, flags, refs[-1])
+        facing[k] = jnp.concatenate(sides, 0).astype(BF16)
 
 
 def is_pairs():
@@ -141,18 +136,33 @@
     return [jax.ShapeDtypeStruct((*size, channels), BF16) for size in sizes]
 
 
-def extend(block, flags):
+def extend(field, sea, flags):
+    tile = jax.ShapeDtypeStruct(field.shape, BF16)
     if not is_pairs():
-        return extend_any(block)
-    strip, side, corner, corners = shapes_of(block)
-    cells = side.shape[0] * side.shape[1]
-    facing, near, far = call(rim_kernel, (strip, side, side), (block, flags), name="rim")
-    facing, near = xor_partner(facing, "lat", 1), xor_partner(near, "lon", 1)
-    both = jax.ShapeDtypeStruct((cells + strip.shape[0] * strip.shape[1], block.shape[2]), BF16)
-    both, corner, own = call(fold_kernel, (both, corner, corner), (block, flags, far), name="fold")
-    both, corner = xor_partner(both, "lon", 3), xor_partner(corner, "lon", 2)
-    far, folded = both[:cells].reshape(side.shape), both[cells:].reshape(strip.shape)
-    (corners,) = call(corner_kernel, (corners,), (near, far, flags, corner), name="corners")
+        (block,) = call(mask_kernel, (tile,), (field, sea), name="mask")
+        return block, *extend_any(block)
+    block, *pieces = round_one(mask_rim_kernel, (field, sea, flags), field, (tile,))
+    return block, *round_two(pieces, flags, pieces[4])
+
+
+def round_one(kernel, operands, block, outs=()):
+    strip, side, corner, _ = shapes_of(block)
+    both = jax.ShapeDtypeStruct((side.shape[0] * LANE + REACH * strip.shape[1], block.shape[2]), BF16)
+    *made, facing, near, both, corner, own = call(
+        kernel, (*outs, strip, side, both, corner, corner), operands, [pltpu.VMEM(side.shape, BF16)], work=2 * 10**9, name="rim"
+    )
+    both, facing = xor_partner(both, "lon", 3), xor_partner(facing, "lat", 1)
+    near, corner = xor_partner(near, "lon", 1), xor_partner(corner, "lon", 2)
+    return *made, facing, near, both, own, corner
+
+
+def round_two(pieces, flags, *after):
+    facing, near, both, own, corner = pieces
+    rows, channels = near.shape[0], near.shape[2]
+    cells = rows * LANE
+    far, folded = both[:cells].reshape(near.shape), both[cells:].reshape(facing.shape)
+    corners = jax.ShapeDtypeStruct((REACH, 2 * LANE, channels), BF16)
+    (corners,) = call(corner_kernel, (corners,), (near, far, flags, *after), name="corners")
     corners = xor_partner(corners, "lat", 1)
     return facing, facing, folded, far, near, own, corner, corners, corners
 
@@ -191,13 +201,6 @@
 def add_kernel(*refs):
     rows, out = refs[-1].shape[0], refs[-1]
     out[...] = added([ref[:rows] for ref in refs[:-2]]).astype(out.dtype)
-
-
-def join_corners_kernel(mine, core, small, near, far, flags, token, joined, wider):
-    join_kernel(mine, core, small, joined)
-    rows = joined.shape[0]
-    wider[:rows] = joined[...]
-    put_corners(near, far, flags, wider, rows)
 
 
 def join_kernel(mine, core, small, *refs):
@@ -267,21 +270,29 @@
     lax.fori_loop(0, 2, parity, 0)
 
 
-def mask_kernel(field, mask, masked, sea, state, ocean, sems):
-    rows, cols, channels = state.shape
-    copies = [pltpu.make_async_copy(field, state, sems.at[0]), pltpu.make_async_copy(mask, ocean, sems.at[1])]
-    for copy in copies:
-        copy.start()
-    copies[1].wait()
-    value = ocean[...].astype(BF16)
+def sea_kernel(mask, sea):
+    rows, _, channels = sea.shape
+    value = mask[...].astype(BF16)
     at = lax.broadcasted_iota(jnp.int32, (rows, channels), 0)
     for r in range(rows):
         pick = jnp.where(at == r, 1.0, 0.0).astype(BF16)
         row = lax.dot_general(value, pick, (((0,), (0,)), ((), ())), preferred_element_type=F32)
         sea[r] = row.astype(BF16)
-    copies[0].wait()
-    for r in range(rows):
-        masked[r] = state[r] * sea[r]
+
+
+def mask_kernel(field, sea, masked):
+    masked[...] = field[...] * sea[...]
+
+
+def rim_fold_kernel(block, flags, facing, near, *rest):
+    *rest, far = rest
+    rim_kernel(block, flags, facing, near, far)
+    fold_kernel(block, flags, far, *rest)
+
+
+def mask_rim_kernel(field, sea, flags, masked, *rest):
+    mask_kernel(field, sea, masked)
+    rim_fold_kernel(masked, flags, *rest)
 
 
 def block_pass(first, rows, blocks, spread, sea, weights, state, arrive=None):
@@ -472,18 +483,9 @@
     hidden = up_weight.shape[1]
     shape = jax.ShapeDtypeStruct
     tile = (rows, cols, channels)
-    near = pltpu.VMEM(tile, BF16)
-    masked, sea = call(
-        mask_kernel,
-        (shape(tile, BF16), shape(tile, BF16)),
-        (field[0], land_mask),
-        [near, pltpu.VMEM((rows, cols), jnp.int32), pltpu.SemaphoreType.DMA((2,))],
-        far=(0, 1),
-        work=10**9,
-        name="mask",
-    )
     flags = flags_of()
-    below, above, folded, far, near, own, corner, low, high = extend(masked, flags)
+    (sea,) = call(sea_kernel, (shape(tile, BF16),), (land_mask,), work=2 * 10**9, name="sea")
+    masked, below, above, folded, far, near, own, corner, low, high = extend(field[0], sea, flags)
     wide = (rows + 2 * REACH, cols + 2 * LEFT, channels)
     spread = pltpu.VMEM((TAPS, LANE, channels), F32)
     large, small = (hidden, channels), (64, channels)
@@ -524,32 +526,16 @@
     )
     joined = shape((hidden + small[0], channels), BF16)
     if is_pairs():
-        strip, side, corner, corners = shapes_of(grad)
-        facing, near, far = call(rim_kernel, (strip, side, side), (grad, flags), name="rim")
-        far_sent = far
-        facing, near, far = xor_partner(facing, "lat", 1), xor_partner(near, "lon", 1), xor_partner(far, "lon", 3)
-        folded, corner, own = call(
-            fold_kernel,
-            (shape((strip.shape[0] * strip.shape[1], channels), BF16), corner, corner),
-            (grad, flags, far_sent, facing, received, last_sums),
-            name="fold",
-        )
-        folded, corner = xor_partner(folded, "lon", 3), xor_partner(corner, "lon", 2)
-        wider = shape((joined.shape[0] + corners.shape[0] * corners.shape[1], channels), BF16)
-        sent, wider = call(
-            join_corners_kernel, (joined, wider), (mine, received, last_sums, near, far, flags, own), name="join"
-        )
-        (one, two), cells = rest[0], joined.shape[0]
-        wider = partners(wider, [two])
-        values = [sent, partners(sent, [one]), wider, partners(sent, [one, two])]
-        corners = wider[cells:].reshape(corners.shape)
-        halo = (facing, facing, folded.reshape(strip.shape), far, near, own, corner, corners, corners)
+        block_halo = round_one(rim_fold_kernel, (grad, flags), grad)
+        (sent,) = call(join_kernel, (joined,), (mine, received, last_sums, block_halo[JOIN_TOKEN]), name="join")
+        values = stage(sent, rest[0])
+        halo = round_two(block_halo, flags)
     else:
         (sent,) = call(join_kernel, (joined,), (mine, received, last_sums), name="join")
         values = stage(sent, rest[0])
-        halo = extend(grad, flags)
+        halo = extend_any(grad)
     for pair in rest[1:]:
-        (sent,) = call(add_kernel, (shape(sent.shape, BF16),), (*values, halo[2]), name="add")
+        (sent,) = call(add_kernel, (shape(sent.shape, BF16),), (*values, halo[0]), name="add")
         values = stage(sent, pair)
     field_grad, token = call(
         backward_kernel,

time: 48.3 us -> 45.4 us (0.940)
  waiting for transfers between devices: 11.4 us -> 8.25 us
  starting transfers between devices: 22.7 us -> 23.6 us
    ppermute x10, waiting for transfers between devices: 4.94 us -> 3.05 us  [xor_partner(): lax.ppermute(value, axis, [(i, i ^ bits) for i in range(lax.axis_size(axi...]
    ppermute x10, starting transfers between devices: 13.7 us -> 15.5 us  [xor_partner(): lax.ppermute(value, axis, [(i, i ^ bits) for i in range(lax.axis_size(axi...]
    ppermute x8, waiting for transfers between devices: 6.49 us -> 5.2 us  [partners(): lax.ppermute(value, axes, route(axes, lambda *at: [i ^ flip[a] for a, i i...]
    ppermute x8, starting transfers between devices: 9.05 us -> 8.08 us  [partners(): lax.ppermute(value, axes, route(axes, lambda *at: [i ^ flip[a] for a, i i...]
    pallas_call x15 -> x14, Pallas kernels: 11.3 us -> 11.1 us  [call(): pl.pallas_call(kernel, out_shape=outs, in_specs=[hbm if n in far else vme...]
  transfers between devices with their start and end apart: 18 -> 18, of which waited for: 7 -> 5; matrix products, arithmetic and copies ran while one was open for 0% -> 0% of each run, Pallas kernels for 17% -> 18%
where the time goes in v5:
time: 45.4 us; the launch traced here: 45.2 us
  starting transfers between devices  23.6 us (52%)
  Pallas kernels  11.1 us (24%)
  waiting for transfers between devices  8.25 us (18%)
  local copies, waits for them, and re-layouts  1.41 us (3%)
  between operations  0.87 us (2%)
    ppermute x10, starting transfers between devices, xor_partner(): lax.ppermute(value, axis, [(i, i ^ bits) for i in range(lax.axis_size(axi...  15.5 us
    pallas_call x14, Pallas kernels, call(): pl.pallas_call(kernel, out_shape=outs, in_specs=[hbm if n in far else vme...  11.1 us
    ppermute x8, starting transfers between devices, partners(): lax.ppermute(value, axes, route(axes, lambda *at: [i ^ flip[a] for a, i i...  8.08 us
    ppermute x8, waiting for transfers between devices, partners(): lax.ppermute(value, axes, route(axes, lambda *at: [i ^ flip[a] for a, i i...  5.2 us
    ppermute x10, waiting for transfers between devices, xor_partner(): lax.ppermute(value, axis, [(i, i ^ bits) for i in range(lax.axis_size(axi...  3.05 us
    unnamed x16, local copies, waits for them, and re-layouts  1.32 us
  transfers between devices with their start and end apart: 18, of which 5 were waited for; matrix products, arithmetic and copies ran while one was open for 0% of the time, Pallas kernels for 18%

profile of v5, /device:TPU:0, one launch (start us, length us, event | category | flops | bytes accessed | tf_op | source)
XLA Modules:
  0.0 45.2 jit_solution(6221154685010847871)
XLA Ops:
  0.7 0.7 %copy-done.7 = s32[16,64]{1,0:T(8,128)S(1)} copy-done((s32[16,64]{1,0:T(8,128)S(1)}, s32[16,64]{1,0:T(8,128)}, u32[]{:S(2)}) %copy-start.7) | copy-done | bytes 4120
  1.3 0.2 sea.1.refs_10_.refs_14_
  1.6 0.1 iota.16.flags.refs_11_.refs_15_
  1.7 0.6 %copy-done.6 = bf16[1,16,64,128]{3,2,1,0:T(8,128)(2,1)S(1)} copy-done((bf16[1,16,64,128]{3,2,1,0:T(8,128)(2,1)S(1)}, bf16[1,16,64,128]{3,2,1,0:T(8,128)(2,1)}, u32[]{:S(2)}) %copy-start.6) | copy-done | bytes 262168
  2.3 0.0 copy-start.4
  2.3 0.0 copy-start.5
  2.3 0.2 rim.2
  2.5 5.1 %collective-permute-start.1 = (bf16[512,128]{1,0:T(8,128)(2,1)S(1)}, bf16[512,128]{1,0:T(8,128)(2,1)S(1)}, u32[]{:S(2)}, u32[]{:S(2)}) collective-permute-start(bf16[512,128]{1,0:T(8,128)(2,1)S(1)} %get-tuple-element.59), channel_id=1, source_target_pairs={{0,24},{8,16},{16,8},{24,0},{1,25},{9,17},{17,9},{25,1},{2,26},{10... | collective-permute-start | bytes 393224 | tf_op jit(solution)/shard_map/ppermute | solution.py:47
  7.6 1.5 %collective-permute-start = (bf16[6,64,128]{2,1,0:T(8,128)(2,1)S(1)}, bf16[6,64,128]{2,1,0:T(8,128)(2,1)S(1)}, u32[]{:S(2)}, u32[]{:S(2)}) collective-permute-start(bf16[6,64,128]{2,1,0:T(8,128)(2,1)S(1)} %get-tuple-element.50), channel_id=1, source_target_pairs={{0,4},{4,0},{1,5},{5,1},{2,6},{6,2},{3,7},{7,3},{8,12},{12,8},{9,1... | collective-permute-start | bytes 294920 | tf_op jit(solution)/shard_map/ppermute | solution.py:47
  9.1 0.0 collective-permute-start.3
  9.1 0.8 %collective-permute-start.2 = (bf16[16,8,128]{2,1,0:T(8,128)(2,1)S(1)}, bf16[16,8,128]{2,1,0:T(8,128)(2,1)S(1)}, u32[]{:S(2)}, u32[]{:S(2)}) collective-permute-start(bf16[16,8,128]{2,1,0:T(8,128)(2,1)S(1)} %get-tuple-element.68), channel_id=1, source_target_pairs={{0,8},{8,0},{16,24},{24,16},{1,9},{9,1},{17,25},{25,17},{2,10},{10... | collective-permute-start | bytes 98312 | tf_op jit(solution)/shard_map/ppermute | solution.py:47
  9.9 2.3 %collective-permute-done.below.refs_8_ = bf16[6,64,128]{2,1,0:T(8,128)(2,1)S(1)} collective-permute-done((bf16[6,64,128]{2,1,0:T(8,128)(2,1)S(1)}, bf16[6,64,128]{2,1,0:T(8,128)(2,1)S(1)}, u32[]{:S(2)}, u32[]{:S(2)}) %collective-permute-start) | collective-permute-done | bytes 98336 | tf_op jit(solution)/shard_map/ppermute | solution.py:47
  12.3 1.8 %lower.1 = (f32[28,80,128]{2,1,0:T(8,128)S(1)}, f32[16,64,128]{2,1,0:T(8,128)S(1)}, bf16[16,64,128]{2,1,0:T(8,128)(2,1)S(1)}, bf16[16,64,128]{2,1,0:T(8,128)(2,1...) custom-call(bf16[16,64,128]{2,1,0:T(8,128)(2,1)S(1)} %get-tuple-elem, ...), custom_call_target="tpu_custom_call" | custom-call | flops 100000000 | bytes 3773952 | tf_op jit(solution)/shard_map/lower/pallas_call | solution.py:468
  14.1 0.0 collective-permute-done.1
  14.2 0.0 collective-permute-done.3.refs_0_.refs_11_
  14.2 0.0 collective-permute-done.2.near.refs_9_
  14.2 1.6 %collective-permute-start.4 = (bf16[6,16,128]{2,1,0:T(8,128)(2,1)S(1)}, bf16[6,16,128]{2,1,0:T(8,128)(2,1)S(1)}, u32[]{:S(2)}, u32[]{:S(2)}) collective-permute-start(bf16[6,16,128]{2,1,0:T(8,128)(2,1)S(1)} %corners.2), channel_id=1, source_target_pairs={{0,4},{4,0},{1,5},{5,1},{2,6},{6,2},{3,7},{7,3},{8,12},{12,8},{9,1... | collective-permute-start | bytes 73736 | tf_op jit(solution)/shard_map/ppermute | solution.py:47
  15.8 1.6 %upper.1 = (f32[28,80,128]{2,1,0:T(8,128)S(1)}, f32[16,64,128]{2,1,0:T(8,128)S(1)}, bf16[16,64,128]{2,1,0:T(8,128)(2,1)S(1)}, bf16[16,64,128]{2,1,0:T(8,128)(2,1...) custom-call(f32[28,80,128]{2,1,0:T(8,128)S(1)} %get-tuple-element.51, ...), custom_call_target="tpu_custom_call", output_to_operand_aliasing={{0}: (0, {}), {1}: (1, {}), {2}: (2, {}), {3}: (3, {}), {4}... | custom-call | flops 2000000000 | bytes 6075904 | tf_op jit(solution)/shard_map/upper/pallas_call | solution.py:468
  17.4 0.7 %collective-permute-done.4.refs_12_.refs_13_ = bf16[6,16,128]{2,1,0:T(8,128)(2,1)S(1)} collective-permute-done((bf16[6,16,128]{2,1,0:T(8,128)(2,1)S(1)}, bf16[6,16,128]{2,1,0:T(8,128)(2,1)S(1)}, u32[]{:S(2)}, u32[]{:S(2)}) %collective-permute-start.4) | collective-permute-done | bytes 24608 | tf_op jit(solution)/shard_map/ppermute | solution.py:47
  18.1 1.5 %edge.1 = (f32[28,80,128]{2,1,0:T(8,128)S(1)}, f32[16,64,128]{2,1,0:T(8,128)S(1)}, bf16[16,64,128]{2,1,0:T(8,128)(2,1)S(1)}, bf16[16,64,128]{2,1,0:T(8,128)(2,1)...) custom-call(f32[28,80,128]{2,1,0:T(8,128)S(1)} %get-tuple-element.60, ...), custom_call_target="tpu_custom_call", output_to_operand_aliasing={{0}: (0, {}), {1}: (1, {}), {2}: (2, {}), {3}: (3, {}), {4}... | custom-call | flops 1000000000 | bytes 6215168 | tf_op jit(solution)/shard_map/edge/pallas_call | solution.py:468
  19.6 0.2 rim.3
  19.7 2.0 %collective-permute-start.6 = (bf16[512,128]{1,0:T(8,128)(2,1)S(1)}, bf16[512,128]{1,0:T(8,128)(2,1)S(1)}, u32[]{:S(2)}, u32[]{:S(2)}) collective-permute-start(bf16[512,128]{1,0:T(8,128)(2,1)S(1)} %get-tuple-element.78), channel_id=1, source_target_pairs={{0,24},{8,16},{16,8},{24,0},{1,25},{9,17},{17,9},{25,1},{2,26},{10... | collective-permute-start | bytes 393224 | tf_op jit(solution)/shard_map/ppermute | solution.py:47
  21.7 0.0 collective-permute-start.10
  21.7 0.4 collective-permute-start.7
  22.2 1.1 %collective-permute-start.5 = (bf16[6,64,128]{2,1,0:T(8,128)(2,1)S(1)}, bf16[6,64,128]{2,1,0:T(8,128)(2,1)S(1)}, u32[]{:S(2)}, u32[]{:S(2)}) collective-permute-start(bf16[6,64,128]{2,1,0:T(8,128)(2,1)S(1)} %get-tuple-element.77), channel_id=1, source_target_pairs={{0,4},{4,0},{1,5},{5,1},{2,6},{6,2},{3,7},{7,3},{8,12},{12,8},{9,1... | collective-permute-start | bytes 294920 | tf_op jit(solution)/shard_map/ppermute | solution.py:47
  23.2 1.9 %kernel_gradient.1 = (bf16[16,64,128]{2,1,0:T(8,128)(2,1)}, f32[64,128]{1,0:T(8,128)S(1)}) custom-call(f32[28,80,128]{2,1,0:T(8,128)S(1)} %get-tuple-element.71.wide, f32[16,64,128]{2,1,0:T(8,128)S(1)} %get-tuple-element.72.mixed, bf16[16,64,128]{2,1,0:T(8,128)(2,1)S(1)} %get-tuple-element.73.result, f32[2,8,128]{2,1,0:T(8,128)S(1)} %get-tuple-element.74.norm), custom_call_target="tpu_custom_call" | custom-call | flops 100000000 | bytes 2236416 | tf_op jit(solution)/shard_map/kernel_gradient/pallas_call | solution.py:468
  25.1 0.0 collective-permute-done.10.core
  25.1 2.0 %collective-permute-start.13 = (bf16[320,128]{1,0:T(8,128)(2,1)S(1)}, bf16[320,128]{1,0:T(8,128)(2,1)S(1)}, u32[]{:S(2)}, u32[]{:S(2)}) collective-permute-start(bf16[320,128]{1,0:T(8,128)(2,1)S(1)} %join.1.refs_0_), channel_id=1, source_target_pairs={{0,6},{1,7},{2,4},{3,5},{4,2},{5,3},{6,0},{7,1},{8,14},{9,15},{10,... | collective-permute-start | bytes 245768 | tf_op jit(solution)/shard_map/ppermute | solution.py:175
  27.1 1.1 %collective-permute-start.12 = (bf16[320,128]{1,0:T(8,128)(2,1)S(1)}, bf16[320,128]{1,0:T(8,128)(2,1)S(1)}, u32[]{:S(2)}, u32[]{:S(2)}) collective-permute-start(bf16[320,128]{1,0:T(8,128)(2,1)S(1)} %join.1.refs_0_), channel_id=1, source_target_pairs={{0,4},{4,0},{1,5},{5,1},{2,6},{6,2},{3,7},{7,3},{8,12},{12,8},{9,1... | collective-permute-start | bytes 245768 | tf_op jit(solution)/shard_map/ppermute | solution.py:175
  28.2 0.0 collective-permute-done.6
  28.2 0.5 %collective-permute-start.11 = (bf16[320,128]{1,0:T(8,128)(2,1)S(1)}, bf16[320,128]{1,0:T(8,128)(2,1)S(1)}, u32[]{:S(2)}, u32[]{:S(2)}) collective-permute-start(bf16[320,128]{1,0:T(8,128)(2,1)S(1)} %join.1.refs_0_), channel_id=1, source_target_pairs={{0,2},{1,3},{2,0},{3,1},{4,6},{5,7},{6,4},{7,5},{8,10},{9,11},{10,... | collective-permute-start | bytes 245768 | tf_op jit(solution)/shard_map/ppermute | solution.py:175
  28.7 0.0 collective-permute-done.7.near
  28.7 1.3 %collective-permute-start.9 = (bf16[6,16,128]{2,1,0:T(8,128)(2,1)S(1)}, bf16[6,16,128]{2,1,0:T(8,128)(2,1)S(1)}, u32[]{:S(2)}, u32[]{:S(2)}) collective-permute-start(bf16[6,16,128]{2,1,0:T(8,128)(2,1)S(1)} %corners.3), channel_id=1, source_target_pairs={{0,4},{4,0},{1,5},{5,1},{2,6},{6,2},{3,7},{7,3},{8,12},{12,8},{9,1... | collective-permute-start | bytes 73736 | tf_op jit(solution)/shard_map/ppermute | solution.py:47
  30.0 0.0 collective-permute-done.5.below.above.refs_4_
  30.0 1.8 %collective-permute-start.8 = (bf16[6,8,128]{2,1,0:T(8,128)(2,1)S(1)}, bf16[6,8,128]{2,1,0:T(8,128)(2,1)S(1)}, u32[]{:S(2)}, u32[]{:S(2)}) collective-permute-start(bf16[6,8,128]{2,1,0:T(8,128)(2,1)S(1)} %get-tuple-element.81), channel_id=1, source_target_pairs={{0,16},{8,24},{16,0},{24,8},{1,17},{9,25},{17,1},{25,9},{2,18},{10... | collective-permute-start | bytes 36872 | tf_op jit(solution)/shard_map/ppermute | solution.py:47
  31.8 0.0 collective-permute-done.13.refs_3_
  31.8 0.9 %collective-permute-done.12.refs_2_ = bf16[320,128]{1,0:T(8,128)(2,1)S(1)} collective-permute-done((bf16[320,128]{1,0:T(8,128)(2,1)S(1)}, bf16[320,128]{1,0:T(8,128)(2,1)S(1)}, u32[]{:S(2)}, u32[]{:S(2)}) %collective-permute-start.12) | collective-permute-done | bytes 81952 | tf_op jit(solution)/shard_map/ppermute | solution.py:175
  32.8 2.0 %collective-permute-start.16 = (bf16[320,128]{1,0:T(8,128)(2,1)S(1)}, bf16[320,128]{1,0:T(8,128)(2,1)S(1)}, u32[]{:S(2)}, u32[]{:S(2)}) collective-permute-start(bf16[320,128]{1,0:T(8,128)(2,1)S(1)} %add.34.refs_0_), channel_id=1, source_target_pairs={{0,24},{8,16},{16,8},{24,0},{1,25},{9,17},{17,9},{25,1},{2,26},{10... | collective-permute-start | bytes 245768 | tf_op jit(solution)/shard_map/ppermute | solution.py:175
  34.8 1.4 %collective-permute-start.15 = (bf16[320,128]{1,0:T(8,128)(2,1)S(1)}, bf16[320,128]{1,0:T(8,128)(2,1)S(1)}, u32[]{:S(2)}, u32[]{:S(2)}) collective-permute-start(bf16[320,128]{1,0:T(8,128)(2,1)S(1)} %add.34.refs_0_), channel_id=1, source_target_pairs={{0,16},{8,24},{16,0},{24,8},{1,17},{9,25},{17,1},{25,9},{2,18},{10... | collective-permute-start | bytes 245768 | tf_op jit(solution)/shard_map/ppermute | solution.py:175
  36.2 1.0 %collective-permute-start.14 = (bf16[320,128]{1,0:T(8,128)(2,1)S(1)}, bf16[320,128]{1,0:T(8,128)(2,1)S(1)}, u32[]{:S(2)}, u32[]{:S(2)}) collective-permute-start(bf16[320,128]{1,0:T(8,128)(2,1)S(1)} %add.34.refs_0_), channel_id=1, source_target_pairs={{0,8},{8,0},{16,24},{24,16},{1,9},{9,1},{17,25},{25,17},{2,10},{10... | collective-permute-start | bytes 245768 | tf_op jit(solution)/shard_map/ppermute | solution.py:175
  37.2 0.0 collective-permute-done.8.corner
  37.2 0.0 collective-permute-done.9.low.high
  37.2 2.8 %backward.1 = (bf16[16,64,128]{2,1,0:T(8,128)(2,1)}, f32[8,128]{1,0:T(8,128)S(1)}) custom-call(bf16[16,64,128]{2,1,0:T(8,128)(2,1)S(1)} %get-tuple-element.76.block, bf16[6,64,128]{2,1,0:T(8,128)(2,1)S(1)} %collective-permute-done.5.below.above.refs_4_, bf16[6,64,128]{2,1,0:T(8,128)(2,1)S(1)} %collective-permute-done.5.below.above.refs_4_, ...), custom_call_target="tpu_custom_call" | custom-call | flops 3000000000 | bytes 1516032 | tf_op jit(solution)/shard_map/backward/pallas_call | solution.py:468
  40.1 0.0 collective-permute-done.16.refs_3_
  40.1 2.9 %collective-permute-done.15.refs_2_ = bf16[320,128]{1,0:T(8,128)(2,1)S(1)} collective-permute-done((bf16[320,128]{1,0:T(8,128)(2,1)S(1)}, bf16[320,128]{1,0:T(8,128)(2,1)S(1)}, u32[]{:S(2)}, u32[]{:S(2)}) %collective-permute-start.15) | collective-permute-done | bytes 81952 | tf_op jit(solution)/shard_map/ppermute | solution.py:175
  43.0 0.1 collective-permute-start.17
  43.1 1.4 %collective-permute-done.17.back = f32[320,128]{1,0:T(8,128)S(1)} collective-permute-done((f32[320,128]{1,0:T(8,128)S(1)}, f32[320,128]{1,0:T(8,128)S(1)}, u32[]{:S(2)}, u32[]{:S(2)}) %collective-permute-start.17) | collective-permute-done | bytes 163872 | tf_op jit(solution)/shard_map/ppermute | solution.py:175
  44.5 0.7 %final.1 = (f32[49,128]{1,0:T(8,128)}, f32[2,128]{1,0:T(2,128)}, f32[128,256]{1,0:T(8,128)}, f32[256,128]{1,0:T(8,128)}) custom-call(f32[320,128]{1,0:T(8,128)S(1)} %add.35.total, f32[320,128]{1,0:T(8,128)S(1)} %collective-permute-done.17.back, s32[8,128]{1,0:T(8,128)S(1)} %iota.16.flags.refs_11_.refs_15_), custom_call_target="tpu_custom_call" | custom-call | bytes 620032 | tf_op jit(solution)/shard_map/final/pallas_call | solution.py:468
  (24 shorter events, 0.2 us)
Async XLA Ops:
  0.6 0.7 %copy-start.7 = (s32[16,64]{1,0:T(8,128)S(1)}, s32[16,64]{1,0:T(8,128)}, u32[]{:S(2)}) copy-start(s32[16,64]{1,0:T(8,128)} %mask.1) | copy-start | bytes 12292
  1.3 0.9 %copy-start.6 = (bf16[1,16,64,128]{3,2,1,0:T(8,128)(2,1)S(1)}, bf16[1,16,64,128]{3,2,1,0:T(8,128)(2,1)}, u32[]{:S(2)}) copy-start(bf16[1,16,64,128]{3,2,1,0:T(8,128)(2,1)} %param.8) | copy-start | bytes 786436
  2.3 10.0 %copy-start = (bf16[1,16,64,128]{3,2,1,0:T(8,128)(2,1)S(1)}, bf16[1,16,64,128]{3,2,1,0:T(8,128)(2,1)}, u32[]{:S(2)}) copy-start(bf16[1,16,64,128]{3,2,1,0:T(8,128)(2,1)} %param.9) | copy-start | bytes 786436
  2.3 10.0 %copy-start.1 = (bf16[128,256]{1,0:T(8,128)(2,1)S(1)}, bf16[128,256]{1,0:T(8,128)(2,1)}, u32[]{:S(2)}) copy-start(bf16[128,256]{1,0:T(8,128)(2,1)} %refs_19_.1) | copy-start | bytes 196612
  2.3 10.0 %copy-start.2 = (bf16[256,128]{1,0:T(8,128)(2,1)S(1)}, bf16[256,128]{1,0:T(8,128)(2,1)}, u32[]{:S(2)}) copy-start(bf16[256,128]{1,0:T(8,128)(2,1)} %refs_20_.1) | copy-start | bytes 196612
  2.3 10.0 %copy-start.3 = (f32[49,128]{1,0:T(8,128)S(1)}, f32[49,128]{1,0:T(8,128)}, u32[]{:S(2)}) copy-start(f32[49,128]{1,0:T(8,128)} %taps.1) | copy-start | bytes 75268
  2.3 10.0 %copy-start.4 = (f32[128]{0:T(128)S(1)}, f32[128]{0:T(128)}, u32[]{:S(2)}) copy-start(f32[128]{0:T(128)} %param.12) | copy-start | bytes 1540
  2.3 10.0 %copy-start.5 = (f32[128]{0:T(128)S(1)}, f32[128]{0:T(128)}, u32[]{:S(2)}) copy-start(f32[128]{0:T(128)} %param.13) | copy-start | bytes 1540
  2.5 11.6 %collective-permute-start.1 = (bf16[512,128]{1,0:T(8,128)(2,1)S(1)}, bf16[512,128]{1,0:T(8,128)(2,1)S(1)}, u32[]{:S(2)}, u32[]{:S(2)}) collective-permute-start(bf16[512,128]{1,0:T(8,128)(2,1)S(1)} %get-tuple-element.59), channel_id=1, source_target_pairs={{0,24},{8,16},{16,8},{24,0},{1,25},{9,17},{17,9},{25,1},{2,26},{10... | collective-permute-start | bytes 393224 | tf_op jit(solution)/shard_map/ppermute | solution.py:47
  7.6 4.6 %collective-permute-start = (bf16[6,64,128]{2,1,0:T(8,128)(2,1)S(1)}, bf16[6,64,128]{2,1,0:T(8,128)(2,1)S(1)}, u32[]{:S(2)}, u32[]{:S(2)}) collective-permute-start(bf16[6,64,128]{2,1,0:T(8,128)(2,1)S(1)} %get-tuple-element.50), channel_id=1, source_target_pairs={{0,4},{4,0},{1,5},{5,1},{2,6},{6,2},{3,7},{7,3},{8,12},{12,8},{9,1... | collective-permute-start | bytes 294920 | tf_op jit(solution)/shard_map/ppermute | solution.py:47
  9.1 5.0 %collective-permute-start.3 = (bf16[6,8,128]{2,1,0:T(8,128)(2,1)S(1)}, bf16[6,8,128]{2,1,0:T(8,128)(2,1)S(1)}, u32[]{:S(2)}, u32[]{:S(2)}) collective-permute-start(bf16[6,8,128]{2,1,0:T(8,128)(2,1)S(1)} %get-tuple-element.70), channel_id=1, source_target_pairs={{0,16},{8,24},{16,0},{24,8},{1,17},{9,25},{17,1},{25,9},{2,18},{10... | collective-permute-start | bytes 36872 | tf_op jit(solution)/shard_map/ppermute | solution.py:47
  9.1 5.0 %collective-permute-start.2 = (bf16[16,8,128]{2,1,0:T(8,128)(2,1)S(1)}, bf16[16,8,128]{2,1,0:T(8,128)(2,1)S(1)}, u32[]{:S(2)}, u32[]{:S(2)}) collective-permute-start(bf16[16,8,128]{2,1,0:T(8,128)(2,1)S(1)} %get-tuple-element.68), channel_id=1, source_target_pairs={{0,8},{8,0},{16,24},{24,16},{1,9},{9,1},{17,25},{25,17},{2,10},{10... | collective-permute-start | bytes 98312 | tf_op jit(solution)/shard_map/ppermute | solution.py:47
  14.2 3.9 %collective-permute-start.4 = (bf16[6,16,128]{2,1,0:T(8,128)(2,1)S(1)}, bf16[6,16,128]{2,1,0:T(8,128)(2,1)S(1)}, u32[]{:S(2)}, u32[]{:S(2)}) collective-permute-start(bf16[6,16,128]{2,1,0:T(8,128)(2,1)S(1)} %corners.2), channel_id=1, source_target_pairs={{0,4},{4,0},{1,5},{5,1},{2,6},{6,2},{3,7},{7,3},{8,12},{12,8},{9,1... | collective-permute-start | bytes 73736 | tf_op jit(solution)/shard_map/ppermute | solution.py:47
  19.7 8.4 %collective-permute-start.6 = (bf16[512,128]{1,0:T(8,128)(2,1)S(1)}, bf16[512,128]{1,0:T(8,128)(2,1)S(1)}, u32[]{:S(2)}, u32[]{:S(2)}) collective-permute-start(bf16[512,128]{1,0:T(8,128)(2,1)S(1)} %get-tuple-element.78), channel_id=1, source_target_pairs={{0,24},{8,16},{16,8},{24,0},{1,25},{9,17},{17,9},{25,1},{2,26},{10... | collective-permute-start | bytes 393224 | tf_op jit(solution)/shard_map/ppermute | solution.py:47
  21.7 3.4 %collective-permute-start.10 = (bf16[256,128]{1,0:T(8,128)(2,1)S(1)}, bf16[256,128]{1,0:T(8,128)(2,1)S(1)}, u32[]{:S(2)}, u32[]{:S(2)}) collective-permute-start(bf16[256,128]{1,0:T(8,128)(2,1)S(1)} %get-tuple-element.85), channel_id=1, source_target_pairs={{0,1},{1,0},{2,3},{3,2},{4,5},{5,4},{6,7},{7,6},{8,9},{9,8},{10,11... | collective-permute-start | bytes 196616 | tf_op jit(solution)/shard_map/ppermute | solution.py:175
  21.7 7.0 %collective-permute-start.7 = (bf16[16,8,128]{2,1,0:T(8,128)(2,1)S(1)}, bf16[16,8,128]{2,1,0:T(8,128)(2,1)S(1)}, u32[]{:S(2)}, u32[]{:S(2)}) collective-permute-start(bf16[16,8,128]{2,1,0:T(8,128)(2,1)S(1)} %get-tuple-element.79), channel_id=1, source_target_pairs={{0,8},{8,0},{16,24},{24,16},{1,9},{9,1},{17,25},{25,17},{2,10},{10... | collective-permute-start | bytes 98312 | tf_op jit(solution)/shard_map/ppermute | solution.py:47
  22.2 7.8 %collective-permute-start.5 = (bf16[6,64,128]{2,1,0:T(8,128)(2,1)S(1)}, bf16[6,64,128]{2,1,0:T(8,128)(2,1)S(1)}, u32[]{:S(2)}, u32[]{:S(2)}) collective-permute-start(bf16[6,64,128]{2,1,0:T(8,128)(2,1)S(1)} %get-tuple-element.77), channel_id=1, source_target_pairs={{0,4},{4,0},{1,5},{5,1},{2,6},{6,2},{3,7},{7,3},{8,12},{12,8},{9,1... | collective-permute-start | bytes 294920 | tf_op jit(solution)/shard_map/ppermute | solution.py:47
  25.1 6.7 %collective-permute-start.13 = (bf16[320,128]{1,0:T(8,128)(2,1)S(1)}, bf16[320,128]{1,0:T(8,128)(2,1)S(1)}, u32[]{:S(2)}, u32[]{:S(2)}) collective-permute-start(bf16[320,128]{1,0:T(8,128)(2,1)S(1)} %join.1.refs_0_), channel_id=1, source_target_pairs={{0,6},{1,7},{2,4},{3,5},{4,2},{5,3},{6,0},{7,1},{8,14},{9,15},{10,... | collective-permute-start | bytes 245768 | tf_op jit(solution)/shard_map/ppermute | solution.py:175
  27.1 5.6 %collective-permute-start.12 = (bf16[320,128]{1,0:T(8,128)(2,1)S(1)}, bf16[320,128]{1,0:T(8,128)(2,1)S(1)}, u32[]{:S(2)}, u32[]{:S(2)}) collective-permute-start(bf16[320,128]{1,0:T(8,128)(2,1)S(1)} %join.1.refs_0_), channel_id=1, source_target_pairs={{0,4},{4,0},{1,5},{5,1},{2,6},{6,2},{3,7},{7,3},{8,12},{12,8},{9,1... | collective-permute-start | bytes 245768 | tf_op jit(solution)/shard_map/ppermute | solution.py:175
  28.2 4.6 %collective-permute-start.11 = (bf16[320,128]{1,0:T(8,128)(2,1)S(1)}, bf16[320,128]{1,0:T(8,128)(2,1)S(1)}, u32[]{:S(2)}, u32[]{:S(2)}) collective-permute-start(bf16[320,128]{1,0:T(8,128)(2,1)S(1)} %join.1.refs_0_), channel_id=1, source_target_pairs={{0,2},{1,3},{2,0},{3,1},{4,6},{5,7},{6,4},{7,5},{8,10},{9,11},{10,... | collective-permute-start | bytes 245768 | tf_op jit(solution)/shard_map/ppermute | solution.py:175
  28.7 8.5 %collective-permute-start.9 = (bf16[6,16,128]{2,1,0:T(8,128)(2,1)S(1)}, bf16[6,16,128]{2,1,0:T(8,128)(2,1)S(1)}, u32[]{:S(2)}, u32[]{:S(2)}) collective-permute-start(bf16[6,16,128]{2,1,0:T(8,128)(2,1)S(1)} %corners.3), channel_id=1, source_target_pairs={{0,4},{4,0},{1,5},{5,1},{2,6},{6,2},{3,7},{7,3},{8,12},{12,8},{9,1... | collective-permute-start | bytes 73736 | tf_op jit(solution)/shard_map/ppermute | solution.py:47
  30.0 7.3 %collective-permute-start.8 = (bf16[6,8,128]{2,1,0:T(8,128)(2,1)S(1)}, bf16[6,8,128]{2,1,0:T(8,128)(2,1)S(1)}, u32[]{:S(2)}, u32[]{:S(2)}) collective-permute-start(bf16[6,8,128]{2,1,0:T(8,128)(2,1)S(1)} %get-tuple-element.81), channel_id=1, source_target_pairs={{0,16},{8,24},{16,0},{24,8},{1,17},{9,25},{17,1},{25,9},{2,18},{10... | collective-permute-start | bytes 36872 | tf_op jit(solution)/shard_map/ppermute | solution.py:47
  32.8 7.3 %collective-permute-start.16 = (bf16[320,128]{1,0:T(8,128)(2,1)S(1)}, bf16[320,128]{1,0:T(8,128)(2,1)S(1)}, u32[]{:S(2)}, u32[]{:S(2)}) collective-permute-start(bf16[320,128]{1,0:T(8,128)(2,1)S(1)} %add.34.refs_0_), channel_id=1, source_target_pairs={{0,24},{8,16},{16,8},{24,0},{1,25},{9,17},{17,9},{25,1},{2,26},{10... | collective-permute-start | bytes 245768 | tf_op jit(solution)/shard_map/ppermute | solution.py:175
  34.8 8.2 %collective-permute-start.15 = (bf16[320,128]{1,0:T(8,128)(2,1)S(1)}, bf16[320,128]{1,0:T(8,128)(2,1)S(1)}, u32[]{:S(2)}, u32[]{:S(2)}) collective-permute-start(bf16[320,128]{1,0:T(8,128)(2,1)S(1)} %add.34.refs_0_), channel_id=1, source_target_pairs={{0,16},{8,24},{16,0},{24,8},{1,17},{9,25},{17,1},{25,9},{2,18},{10... | collective-permute-start | bytes 245768 | tf_op jit(solution)/shard_map/ppermute | solution.py:175
  36.2 6.8 %collective-permute-start.14 = (bf16[320,128]{1,0:T(8,128)(2,1)S(1)}, bf16[320,128]{1,0:T(8,128)(2,1)S(1)}, u32[]{:S(2)}, u32[]{:S(2)}) collective-permute-start(bf16[320,128]{1,0:T(8,128)(2,1)S(1)} %add.34.refs_0_), channel_id=1, source_target_pairs={{0,8},{8,0},{16,24},{24,16},{1,9},{9,1},{17,25},{25,17},{2,10},{10... | collective-permute-start | bytes 245768 | tf_op jit(solution)/shard_map/ppermute | solution.py:175
  43.0 1.5 %collective-permute-start.17 = (f32[320,128]{1,0:T(8,128)S(1)}, f32[320,128]{1,0:T(8,128)S(1)}, u32[]{:S(2)}, u32[]{:S(2)}) collective-permute-start(f32[320,128]{1,0:T(8,128)S(1)} %add.35.total), channel_id=1, source_target_pairs={{0,1},{1,0},{2,3},{3,2},{4,5},{5,4},{6,7},{7,6},{8,9},{9,8},{10,11... | collective-permute-start | bytes 491528 | tf_op jit(solution)/shard_map/ppermute | solution.py:175

commit v6 on v5

--- a/solution.py
+++ b/solution.py
@@ -176,8 +176,7 @@
 
 
 def add_kernel(*refs):
-    rows, out = refs[-1].shape[0], refs[-1]
-    out[...] = added([ref[:rows] for ref in refs[:-2]]).astype(out.dtype)
+    refs[-1][...] = added([ref[...] for ref in refs[:4]]).astype(refs[-1].dtype)
 
 
 def stages():
@@ -199,8 +198,7 @@
 
 
 def add_kernel(*refs):
-    rows, out = refs[-1].shape[0], refs[-1]
-    out[...] = added([ref[:rows] for ref in refs[:-2]]).astype(out.dtype)
+    refs[-1][...] = added([ref[...] for ref in refs[:4]]).astype(refs[-1].dtype)
 
 
 def join_kernel(mine, core, small, *refs):
@@ -208,6 +206,33 @@
     half = mine.shape[0]
     joined[:half] = (mine[...] + core[...].astype(F32)).astype(BF16)
     joined[half:] = small[...].astype(BF16)
+
+
+def cut_kernel(mine, core, small, flags, token, keep, away):
+    quarter, eighth = mine.shape[0] // 2, small.shape[0] // 2
+    northern = on(flags, NORTHERN)
+    large, little = mine[...] + core[...].astype(F32), small[...]
+    for ref, flag in ((keep, northern), (away, jnp.logical_not(northern))):
+        ref[:quarter] = jnp.where(flag, large[quarter:], large[:quarter]).astype(BF16)
+        ref[quarter:] = jnp.where(flag, little[eighth:], little[:eighth]).astype(BF16)
+
+
+def gather_kernel(own, core, lat, both, flags, kernel_grad, norm_grad, up_grad, down_grad, *, factor):
+    hidden, channels = down_grad.shape
+    northern, odd = on(flags, NORTHERN), on(flags, CORE)
+    own, core, lat, both = (ref[...].astype(F32) * factor for ref in (own, core, lat, both))
+    here = jnp.where(odd, core, own), jnp.where(odd, own, core)
+    there = jnp.where(odd, both, lat), jnp.where(odd, lat, both)
+    low = [jnp.where(northern, b, a) for a, b in zip(here, there)]
+    high = [jnp.where(northern, a, b) for a, b in zip(here, there)]
+    quarter = hidden // 2
+    down_grad[...] = jnp.concatenate([low[0][:quarter], high[0][:quarter]], 0)
+    up = jnp.concatenate([low[1][:quarter], high[1][:quarter]], 0)
+    for n in range(hidden // channels):
+        up_grad[:, n * channels : (n + 1) * channels] = up[n * channels : (n + 1) * channels]
+    small = jnp.concatenate([a[0][quarter:] + a[1][quarter:] for a in (low, high)], 0)
+    kernel_grad[...] = small[:TAPS]
+    norm_grad[...] = small[TAPS : TAPS + 2]
 
 
 def fill_own(wide, flags, block, below):
@@ -524,36 +549,46 @@
         work=KERNEL_WORK,
         name="kernel_gradient",
     )
-    joined = shape((hidden + small[0], channels), BF16)
+    grads = (shape((TAPS, channels), F32), shape((2, channels), F32), shape((channels, hidden), F32), shape((hidden, channels), F32))
+    count = rows * cols * lax.axis_size("lon") * lax.axis_size("lat") * lax.axis_size("ens")
+    factor = 1.0 / math.sqrt(count)
+
+    def backward(halo):
+        return call(
+            backward_kernel,
+            (shape(tile, BF16), shape((LANE, channels), F32)),
+            (grad, *halo, upstream, sea, kernel_taps, flags),
+            [pltpu.VMEM(wide, F32), spread, spread],
+            work=3 * 10**9,
+            name="backward",
+        )
+
     if is_pairs():
-        block_halo = round_one(rim_fold_kernel, (grad, flags), grad)
-        (sent,) = call(join_kernel, (joined,), (mine, received, last_sums, block_halo[JOIN_TOKEN]), name="join")
-        values = stage(sent, rest[0])
-        halo = round_two(block_halo, flags)
+        pieces = round_one(rim_fold_kernel, (grad, flags), grad)
+        part = shape(((hidden + small[0]) // 2, channels), BF16)
+        keep, away = call(cut_kernel, (part, part), (mine, received, last_sums, flags, pieces[JOIN_TOKEN]), name="cut")
+        y, x = rest[0]
+        values = [keep, partners(keep, [y]), partners(away, [x]), partners(away, [y, x])]
+        halo = round_two(pieces, flags)
+        (total,) = call(add_kernel, (part,), (*values, halo[0]), name="add")
+        values = stage(total, rest[1])
+        field_grad, token = backward(halo)
+        (total,) = call(add_kernel, (part,), (*values, token), name="add")
+        over_lat, size = partners(total, [x]), total.shape[0]
+        both = partners(jnp.concatenate([total, over_lat]), core)
+        parts = (total, both[:size], over_lat, both[size:])
+        weight_grads = call(functools.partial(gather_kernel, factor=factor), grads, (*parts, flags), name="final")
     else:
-        (sent,) = call(join_kernel, (joined,), (mine, received, last_sums), name="join")
-        values = stage(sent, rest[0])
-        halo = extend_any(grad)
-    for pair in rest[1:]:
-        (sent,) = call(add_kernel, (shape(sent.shape, BF16),), (*values, halo[0]), name="add")
-        values = stage(sent, pair)
-    field_grad, token = call(
-        backward_kernel,
-        (shape(tile, BF16), shape((LANE, channels), F32)),
-        (grad, *halo, upstream, sea, kernel_taps, flags),
-        [pltpu.VMEM(wide, F32), spread, spread],
-        work=3 * 10**9,
-        name="backward",
-    )
-    (total,) = call(add_kernel, (shape(joined.shape, F32),), (*values, token), name="add")
-    back = partners(total, core)
-    count = rows * cols * lax.axis_size("lon") * lax.axis_size("lat") * lax.axis_size("ens")
-    kernel_grad, norm_grad, up_grad, down_grad = call(
-        functools.partial(final_kernel, factor=1.0 / math.sqrt(count)),
-        (shape((TAPS, channels), F32), shape((2, channels), F32), shape((channels, hidden), F32), shape((hidden, channels), F32)),
-        (total, back, flags),
-        name="final",
-    )
+        joined = shape((hidden + small[0], channels), BF16)
+        (total,) = call(join_kernel, (joined,), (mine, received, last_sums), name="join")
+        for pair in rest:
+            values = stage(total.astype(BF16), pair)
+            total = added(values)
+        weight_grads = call(
+            functools.partial(final_kernel, factor=factor), grads, (total, partners(total, core), flags), name="final"
+        )
+        field_grad, _ = backward(extend_any(grad))
+    kernel_grad, norm_grad, up_grad, down_grad = weight_grads
     return output[None], field_grad[None], kernel_grad, norm_grad, up_grad, down_grad
 
 

time: 45.4 us -> 46.1 us (1.015)
  starting transfers between devices: 23.6 us -> 24.5 us
    ppermute x8 -> x9, starting transfers between devices: 8.08 us -> 9.05 us  [partners(): lax.ppermute(value, axes, route(axes, lambda *at: [i ^ flip[a] for a, i i...]
    ppermute x8 -> x9, waiting for transfers between devices: 5.2 us -> 4.92 us  [partners(): lax.ppermute(value, axes, route(axes, lambda *at: [i ^ flip[a] for a, i i...]
  transfers between devices with their start and end apart: 18 -> 19, of which waited for: 5 -> 6; matrix products, arithmetic and copies ran while one was open for 0% -> 0% of each run, Pallas kernels for 18% -> 18%
where the time goes in v6:
time: 46.1 us; the launch traced here: 45.9 us
  starting transfers between devices  24.5 us (53%)
  Pallas kernels  11.1 us (24%)
  waiting for transfers between devices  7.98 us (17%)
  local copies, waits for them, and re-layouts  1.42 us (3%)
  between operations  0.88 us (2%)
    ppermute x10, starting transfers between devices, xor_partner(): lax.ppermute(value, axis, [(i, i ^ bits) for i in range(lax.axis_size(axi...  15.5 us
    pallas_call x14, Pallas kernels, call(): pl.pallas_call(kernel, out_shape=outs, in_specs=[hbm if n in far else vme...  11.1 us
    ppermute x9, starting transfers between devices, partners(): lax.ppermute(value, axes, route(axes, lambda *at: [i ^ flip[a] for a, i i...  9.05 us
    ppermute x9, waiting for transfers between devices, partners(): lax.ppermute(value, axes, route(axes, lambda *at: [i ^ flip[a] for a, i i...  4.92 us
    ppermute x10, waiting for transfers between devices, xor_partner(): lax.ppermute(value, axis, [(i, i ^ bits) for i in range(lax.axis_size(axi...  3.05 us
    unnamed x16, local copies, waits for them, and re-layouts  1.32 us
  transfers between devices with their start and end apart: 19, of which 6 were waited for; matrix products, arithmetic and copies ran while one was open for 0% of the time, Pallas kernels for 18%

profile of v6, /device:TPU:0, one launch (start us, length us, event | category | flops | bytes accessed | tf_op | source)
XLA Modules:
  0.0 45.9 jit_solution(930097347946123795)
XLA Ops:
  0.7 0.7 %copy-done.7 = s32[16,64]{1,0:T(8,128)S(1)} copy-done((s32[16,64]{1,0:T(8,128)S(1)}, s32[16,64]{1,0:T(8,128)}, u32[]{:S(2)}) %copy-start.7) | copy-done | bytes 4120
  1.3 0.2 sea.1.refs_10_.refs_14_
  1.6 0.1 iota.16.flags.refs_11_.refs_15_
  1.7 0.6 %copy-done.6 = bf16[1,16,64,128]{3,2,1,0:T(8,128)(2,1)S(1)} copy-done((bf16[1,16,64,128]{3,2,1,0:T(8,128)(2,1)S(1)}, bf16[1,16,64,128]{3,2,1,0:T(8,128)(2,1)}, u32[]{:S(2)}) %copy-start.6) | copy-done | bytes 262168
  2.3 0.0 copy-start.4
  2.3 0.0 copy-start.5
  2.3 0.2 rim.2
  2.5 5.1 %collective-permute-start.1 = (bf16[512,128]{1,0:T(8,128)(2,1)S(1)}, bf16[512,128]{1,0:T(8,128)(2,1)S(1)}, u32[]{:S(2)}, u32[]{:S(2)}) collective-permute-start(bf16[512,128]{1,0:T(8,128)(2,1)S(1)} %get-tuple-element.61), channel_id=1, source_target_pairs={{0,24},{8,16},{16,8},{24,0},{1,25},{9,17},{17,9},{25,1},{2,26},{10... | collective-permute-start | bytes 393224 | tf_op jit(solution)/shard_map/ppermute | solution.py:47
  7.6 1.5 %collective-permute-start = (bf16[6,64,128]{2,1,0:T(8,128)(2,1)S(1)}, bf16[6,64,128]{2,1,0:T(8,128)(2,1)S(1)}, u32[]{:S(2)}, u32[]{:S(2)}) collective-permute-start(bf16[6,64,128]{2,1,0:T(8,128)(2,1)S(1)} %get-tuple-element.52), channel_id=1, source_target_pairs={{0,4},{4,0},{1,5},{5,1},{2,6},{6,2},{3,7},{7,3},{8,12},{12,8},{9,1... | collective-permute-start | bytes 294920 | tf_op jit(solution)/shard_map/ppermute | solution.py:47
  9.1 0.0 collective-permute-start.3
  9.1 0.8 %collective-permute-start.2 = (bf16[16,8,128]{2,1,0:T(8,128)(2,1)S(1)}, bf16[16,8,128]{2,1,0:T(8,128)(2,1)S(1)}, u32[]{:S(2)}, u32[]{:S(2)}) collective-permute-start(bf16[16,8,128]{2,1,0:T(8,128)(2,1)S(1)} %get-tuple-element.70), channel_id=1, source_target_pairs={{0,8},{8,0},{16,24},{24,16},{1,9},{9,1},{17,25},{25,17},{2,10},{10... | collective-permute-start | bytes 98312 | tf_op jit(solution)/shard_map/ppermute | solution.py:47
  9.9 2.3 %collective-permute-done.below.refs_8_ = bf16[6,64,128]{2,1,0:T(8,128)(2,1)S(1)} collective-permute-done((bf16[6,64,128]{2,1,0:T(8,128)(2,1)S(1)}, bf16[6,64,128]{2,1,0:T(8,128)(2,1)S(1)}, u32[]{:S(2)}, u32[]{:S(2)}) %collective-permute-start) | collective-permute-done | bytes 98336 | tf_op jit(solution)/shard_map/ppermute | solution.py:47
  12.3 1.8 %lower.1 = (f32[28,80,128]{2,1,0:T(8,128)S(1)}, f32[16,64,128]{2,1,0:T(8,128)S(1)}, bf16[16,64,128]{2,1,0:T(8,128)(2,1)S(1)}, bf16[16,64,128]{2,1,0:T(8,128)(2,1...) custom-call(bf16[16,64,128]{2,1,0:T(8,128)(2,1)S(1)} %get-tuple-elem, ...), custom_call_target="tpu_custom_call" | custom-call | flops 100000000 | bytes 3773952 | tf_op jit(solution)/shard_map/lower/pallas_call | solution.py:493
  14.1 0.0 collective-permute-done.1
  14.2 0.0 collective-permute-done.3.refs_0_.refs_11_
  14.2 0.0 collective-permute-done.2.near.refs_9_
  14.2 1.6 %collective-permute-start.4 = (bf16[6,16,128]{2,1,0:T(8,128)(2,1)S(1)}, bf16[6,16,128]{2,1,0:T(8,128)(2,1)S(1)}, u32[]{:S(2)}, u32[]{:S(2)}) collective-permute-start(bf16[6,16,128]{2,1,0:T(8,128)(2,1)S(1)} %corners.2), channel_id=1, source_target_pairs={{0,4},{4,0},{1,5},{5,1},{2,6},{6,2},{3,7},{7,3},{8,12},{12,8},{9,1... | collective-permute-start | bytes 73736 | tf_op jit(solution)/shard_map/ppermute | solution.py:47
  15.8 1.6 %upper.1 = (f32[28,80,128]{2,1,0:T(8,128)S(1)}, f32[16,64,128]{2,1,0:T(8,128)S(1)}, bf16[16,64,128]{2,1,0:T(8,128)(2,1)S(1)}, bf16[16,64,128]{2,1,0:T(8,128)(2,1...) custom-call(f32[28,80,128]{2,1,0:T(8,128)S(1)} %get-tuple-element.53, ...), custom_call_target="tpu_custom_call", output_to_operand_aliasing={{0}: (0, {}), {1}: (1, {}), {2}: (2, {}), {3}: (3, {}), {4}... | custom-call | flops 2000000000 | bytes 6075904 | tf_op jit(solution)/shard_map/upper/pallas_call | solution.py:493
  17.4 0.7 %collective-permute-done.4.refs_12_.refs_13_ = bf16[6,16,128]{2,1,0:T(8,128)(2,1)S(1)} collective-permute-done((bf16[6,16,128]{2,1,0:T(8,128)(2,1)S(1)}, bf16[6,16,128]{2,1,0:T(8,128)(2,1)S(1)}, u32[]{:S(2)}, u32[]{:S(2)}) %collective-permute-start.4) | collective-permute-done | bytes 24608 | tf_op jit(solution)/shard_map/ppermute | solution.py:47
  18.1 1.5 %edge.1 = (f32[28,80,128]{2,1,0:T(8,128)S(1)}, f32[16,64,128]{2,1,0:T(8,128)S(1)}, bf16[16,64,128]{2,1,0:T(8,128)(2,1)S(1)}, bf16[16,64,128]{2,1,0:T(8,128)(2,1)...) custom-call(f32[28,80,128]{2,1,0:T(8,128)S(1)} %get-tuple-element.62, ...), custom_call_target="tpu_custom_call", output_to_operand_aliasing={{0}: (0, {}), {1}: (1, {}), {2}: (2, {}), {3}: (3, {}), {4}... | custom-call | flops 1000000000 | bytes 6215168 | tf_op jit(solution)/shard_map/edge/pallas_call | solution.py:493
  19.6 0.2 rim.3
  19.7 2.0 %collective-permute-start.6 = (bf16[512,128]{1,0:T(8,128)(2,1)S(1)}, bf16[512,128]{1,0:T(8,128)(2,1)S(1)}, u32[]{:S(2)}, u32[]{:S(2)}) collective-permute-start(bf16[512,128]{1,0:T(8,128)(2,1)S(1)} %get-tuple-element.80), channel_id=1, source_target_pairs={{0,24},{8,16},{16,8},{24,0},{1,25},{9,17},{17,9},{25,1},{2,26},{10... | collective-permute-start | bytes 393224 | tf_op jit(solution)/shard_map/ppermute | solution.py:47
  21.7 0.0 collective-permute-start.10
  21.7 0.4 collective-permute-start.7
  22.2 1.1 %collective-permute-start.5 = (bf16[6,64,128]{2,1,0:T(8,128)(2,1)S(1)}, bf16[6,64,128]{2,1,0:T(8,128)(2,1)S(1)}, u32[]{:S(2)}, u32[]{:S(2)}) collective-permute-start(bf16[6,64,128]{2,1,0:T(8,128)(2,1)S(1)} %get-tuple-element.79), channel_id=1, source_target_pairs={{0,4},{4,0},{1,5},{5,1},{2,6},{6,2},{3,7},{7,3},{8,12},{12,8},{9,1... | collective-permute-start | bytes 294920 | tf_op jit(solution)/shard_map/ppermute | solution.py:47
  23.2 1.9 %kernel_gradient.1 = (bf16[16,64,128]{2,1,0:T(8,128)(2,1)}, f32[64,128]{1,0:T(8,128)S(1)}) custom-call(f32[28,80,128]{2,1,0:T(8,128)S(1)} %get-tuple-element.73.wide, f32[16,64,128]{2,1,0:T(8,128)S(1)} %get-tuple-element.74.mixed, bf16[16,64,128]{2,1,0:T(8,128)(2,1)S(1)} %get-tuple-element.75.result, f32[2,8,128]{2,1,0:T(8,128)S(1)} %get-tuple-element.76.norm), custom_call_target="tpu_custom_call" | custom-call | flops 100000000 | bytes 2236416 | tf_op jit(solution)/shard_map/kernel_gradient/pallas_call | solution.py:493
  25.1 0.0 collective-permute-done.10.core
  25.1 2.0 %collective-permute-start.13 = (bf16[160,128]{1,0:T(8,128)(2,1)S(1)}, bf16[160,128]{1,0:T(8,128)(2,1)S(1)}, u32[]{:S(2)}, u32[]{:S(2)}) collective-permute-start(bf16[160,128]{1,0:T(8,128)(2,1)S(1)} %get-tuple-element.90), channel_id=1, source_target_pairs={{0,6},{1,7},{2,4},{3,5},{4,2},{5,3},{6,0},{7,1},{8,14},{9,15},{10,... | collective-permute-start | bytes 122888 | tf_op jit(solution)/shard_map/ppermute | solution.py:175
  27.1 1.1 %collective-permute-start.12 = (bf16[160,128]{1,0:T(8,128)(2,1)S(1)}, bf16[160,128]{1,0:T(8,128)(2,1)S(1)}, u32[]{:S(2)}, u32[]{:S(2)}) collective-permute-start(bf16[160,128]{1,0:T(8,128)(2,1)S(1)} %get-tuple-element.90), channel_id=1, source_target_pairs={{0,4},{4,0},{1,5},{5,1},{2,6},{6,2},{3,7},{7,3},{8,12},{12,8},{9,1... | collective-permute-start | bytes 122888 | tf_op jit(solution)/shard_map/ppermute | solution.py:175
  28.2 0.0 collective-permute-done.6
  28.2 0.5 %collective-permute-start.11 = (bf16[160,128]{1,0:T(8,128)(2,1)S(1)}, bf16[160,128]{1,0:T(8,128)(2,1)S(1)}, u32[]{:S(2)}, u32[]{:S(2)}) collective-permute-start(bf16[160,128]{1,0:T(8,128)(2,1)S(1)} %get-tuple-element.89.refs_0_), channel_id=1, source_target_pairs={{0,2},{1,3},{2,0},{3,1},{4,6},{5,7},{6,4},{7,5},{8,10},{9,11},{10,... | collective-permute-start | bytes 122888 | tf_op jit(solution)/shard_map/ppermute | solution.py:175
  28.7 1.3 %collective-permute-start.9 = (bf16[6,16,128]{2,1,0:T(8,128)(2,1)S(1)}, bf16[6,16,128]{2,1,0:T(8,128)(2,1)S(1)}, u32[]{:S(2)}, u32[]{:S(2)}) collective-permute-start(bf16[6,16,128]{2,1,0:T(8,128)(2,1)S(1)} %corners.3), channel_id=1, source_target_pairs={{0,4},{4,0},{1,5},{5,1},{2,6},{6,2},{3,7},{7,3},{8,12},{12,8},{9,1... | collective-permute-start | bytes 73736 | tf_op jit(solution)/shard_map/ppermute | solution.py:47
  30.0 1.8 %collective-permute-start.8 = (bf16[6,8,128]{2,1,0:T(8,128)(2,1)S(1)}, bf16[6,8,128]{2,1,0:T(8,128)(2,1)S(1)}, u32[]{:S(2)}, u32[]{:S(2)}) collective-permute-start(bf16[6,8,128]{2,1,0:T(8,128)(2,1)S(1)} %get-tuple-element.83), channel_id=1, source_target_pairs={{0,16},{8,24},{16,0},{24,8},{1,17},{9,25},{17,1},{25,9},{2,18},{10... | collective-permute-start | bytes 36872 | tf_op jit(solution)/shard_map/ppermute | solution.py:47
  31.8 0.4 collective-permute-done.11.refs_1_
  32.2 0.0 collective-permute-done.13.refs_3_
  32.2 0.0 collective-permute-done.12.refs_2_
  32.2 2.0 %collective-permute-start.16 = (bf16[160,128]{1,0:T(8,128)(2,1)S(1)}, bf16[160,128]{1,0:T(8,128)(2,1)S(1)}, u32[]{:S(2)}, u32[]{:S(2)}) collective-permute-start(bf16[160,128]{1,0:T(8,128)(2,1)S(1)} %add.34.refs_0_), channel_id=1, source_target_pairs={{0,24},{8,16},{16,8},{24,0},{1,25},{9,17},{17,9},{25,1},{2,26},{10... | collective-permute-start | bytes 122888 | tf_op jit(solution)/shard_map/ppermute | solution.py:175
  34.2 1.6 %collective-permute-start.15 = (bf16[160,128]{1,0:T(8,128)(2,1)S(1)}, bf16[160,128]{1,0:T(8,128)(2,1)S(1)}, u32[]{:S(2)}, u32[]{:S(2)}) collective-permute-start(bf16[160,128]{1,0:T(8,128)(2,1)S(1)} %add.34.refs_0_), channel_id=1, source_target_pairs={{0,16},{8,24},{16,0},{24,8},{1,17},{9,25},{17,1},{25,9},{2,18},{10... | collective-permute-start | bytes 122888 | tf_op jit(solution)/shard_map/ppermute | solution.py:175
  35.8 0.9 %collective-permute-start.14 = (bf16[160,128]{1,0:T(8,128)(2,1)S(1)}, bf16[160,128]{1,0:T(8,128)(2,1)S(1)}, u32[]{:S(2)}, u32[]{:S(2)}) collective-permute-start(bf16[160,128]{1,0:T(8,128)(2,1)S(1)} %add.34.refs_0_), channel_id=1, source_target_pairs={{0,8},{8,0},{16,24},{24,16},{1,9},{9,1},{17,25},{25,17},{2,10},{10... | collective-permute-start | bytes 122888 | tf_op jit(solution)/shard_map/ppermute | solution.py:175
  36.7 0.0 collective-permute-done.8.corner
  36.7 2.8 %backward.1 = (bf16[16,64,128]{2,1,0:T(8,128)(2,1)}, f32[8,128]{1,0:T(8,128)S(1)}) custom-call(bf16[16,64,128]{2,1,0:T(8,128)(2,1)S(1)} %get-tuple-element.78.block, bf16[6,64,128]{2,1,0:T(8,128)(2,1)S(1)} %collective-permute-done.5.below.above.refs_4_, bf16[6,64,128]{2,1,0:T(8,128)(2,1)S(1)} %collective-permute-done.5.below.above.refs_4_, ...), custom_call_target="tpu_custom_call" | custom-call | flops 3000000000 | bytes 1516032 | tf_op jit(solution)/shard_map/backward/pallas_call | solution.py:493
  39.5 0.0 collective-permute-done.16.refs_3_
  39.5 0.2 collective-permute-done.14.refs_1_
  39.8 1.0 %collective-permute-start.17 = (bf16[160,128]{1,0:T(8,128)(2,1)S(1)}, bf16[160,128]{1,0:T(8,128)(2,1)S(1)}, u32[]{:S(2)}, u32[]{:S(2)}) collective-permute-start(bf16[160,128]{1,0:T(8,128)(2,1)S(1)} %add.35.own), channel_id=1, source_target_pairs={{0,4},{4,0},{1,5},{5,1},{2,6},{6,2},{3,7},{7,3},{8,12},{12,8},{9,1... | collective-permute-start | bytes 122888 | tf_op jit(solution)/shard_map/ppermute | solution.py:175
  40.8 3.0 %collective-permute-done.17.lat = bf16[160,128]{1,0:T(8,128)(2,1)S(1)} collective-permute-done((bf16[160,128]{1,0:T(8,128)(2,1)S(1)}, bf16[160,128]{1,0:T(8,128)(2,1)S(1)}, u32[]{:S(2)}, u32[]{:S(2)}) %collective-permute-start.17) | collective-permute-done | bytes 40992 | tf_op jit(solution)/shard_map/ppermute | solution.py:175
  43.9 0.0 collective-permute-start.18
  43.9 1.3 %collective-permute-done.18 = bf16[320,128]{1,0:T(8,128)(2,1)S(1)} collective-permute-done((bf16[320,128]{1,0:T(8,128)(2,1)S(1)}, bf16[320,128]{1,0:T(8,128)(2,1)S(1)}, u32[]{:S(2)}, u32[]{:S(2)}) %collective-permute-start.18) | collective-permute-done | bytes 81952 | tf_op jit(solution)/shard_map/ppermute | solution.py:175
  45.2 0.7 %final.1 = (f32[49,128]{1,0:T(8,128)}, f32[2,128]{1,0:T(2,128)}, f32[128,256]{1,0:T(8,128)}, f32[256,128]{1,0:T(8,128)}) custom-call(bf16[160,128]{1,0:T(8,128)(2,1)S(1)} %add.35.own, bf16[160,128]{1,0:T(8,128)(2,1)S(1)} %get-tuple-element.97.core, bf16[160,128]{1,0:T(8,128)(2,1)S(1)} %collective-permute-done.17.lat, ...), custom_call_target="tpu_custom_call" | custom-call | bytes 456192 | tf_op jit(solution)/shard_map/final/pallas_call | solution.py:493
  (28 shorter events, 0.2 us)
Async XLA Ops:
  0.6 0.7 %copy-start.7 = (s32[16,64]{1,0:T(8,128)S(1)}, s32[16,64]{1,0:T(8,128)}, u32[]{:S(2)}) copy-start(s32[16,64]{1,0:T(8,128)} %mask.1) | copy-start | bytes 12292
  1.3 0.9 %copy-start.6 = (bf16[1,16,64,128]{3,2,1,0:T(8,128)(2,1)S(1)}, bf16[1,16,64,128]{3,2,1,0:T(8,128)(2,1)}, u32[]{:S(2)}) copy-start(bf16[1,16,64,128]{3,2,1,0:T(8,128)(2,1)} %param.8) | copy-start | bytes 786436
  2.3 10.0 %copy-start = (bf16[1,16,64,128]{3,2,1,0:T(8,128)(2,1)S(1)}, bf16[1,16,64,128]{3,2,1,0:T(8,128)(2,1)}, u32[]{:S(2)}) copy-start(bf16[1,16,64,128]{3,2,1,0:T(8,128)(2,1)} %param.9) | copy-start | bytes 786436
  2.3 10.0 %copy-start.1 = (bf16[128,256]{1,0:T(8,128)(2,1)S(1)}, bf16[128,256]{1,0:T(8,128)(2,1)}, u32[]{:S(2)}) copy-start(bf16[128,256]{1,0:T(8,128)(2,1)} %refs_19_.1) | copy-start | bytes 196612
  2.3 10.0 %copy-start.2 = (bf16[256,128]{1,0:T(8,128)(2,1)S(1)}, bf16[256,128]{1,0:T(8,128)(2,1)}, u32[]{:S(2)}) copy-start(bf16[256,128]{1,0:T(8,128)(2,1)} %refs_20_.1) | copy-start | bytes 196612
  2.3 10.0 %copy-start.3 = (f32[49,128]{1,0:T(8,128)S(1)}, f32[49,128]{1,0:T(8,128)}, u32[]{:S(2)}) copy-start(f32[49,128]{1,0:T(8,128)} %taps.1) | copy-start | bytes 75268
  2.3 10.0 %copy-start.4 = (f32[128]{0:T(128)S(1)}, f32[128]{0:T(128)}, u32[]{:S(2)}) copy-start(f32[128]{0:T(128)} %param.12) | copy-start | bytes 1540
  2.3 10.0 %copy-start.5 = (f32[128]{0:T(128)S(1)}, f32[128]{0:T(128)}, u32[]{:S(2)}) copy-start(f32[128]{0:T(128)} %param.13) | copy-start | bytes 1540
  2.5 11.6 %collective-permute-start.1 = (bf16[512,128]{1,0:T(8,128)(2,1)S(1)}, bf16[512,128]{1,0:T(8,128)(2,1)S(1)}, u32[]{:S(2)}, u32[]{:S(2)}) collective-permute-start(bf16[512,128]{1,0:T(8,128)(2,1)S(1)} %get-tuple-element.61), channel_id=1, source_target_pairs={{0,24},{8,16},{16,8},{24,0},{1,25},{9,17},{17,9},{25,1},{2,26},{10... | collective-permute-start | bytes 393224 | tf_op jit(solution)/shard_map/ppermute | solution.py:47
  7.6 4.6 %collective-permute-start = (bf16[6,64,128]{2,1,0:T(8,128)(2,1)S(1)}, bf16[6,64,128]{2,1,0:T(8,128)(2,1)S(1)}, u32[]{:S(2)}, u32[]{:S(2)}) collective-permute-start(bf16[6,64,128]{2,1,0:T(8,128)(2,1)S(1)} %get-tuple-element.52), channel_id=1, source_target_pairs={{0,4},{4,0},{1,5},{5,1},{2,6},{6,2},{3,7},{7,3},{8,12},{12,8},{9,1... | collective-permute-start | bytes 294920 | tf_op jit(solution)/shard_map/ppermute | solution.py:47
  9.1 5.0 %collective-permute-start.3 = (bf16[6,8,128]{2,1,0:T(8,128)(2,1)S(1)}, bf16[6,8,128]{2,1,0:T(8,128)(2,1)S(1)}, u32[]{:S(2)}, u32[]{:S(2)}) collective-permute-start(bf16[6,8,128]{2,1,0:T(8,128)(2,1)S(1)} %get-tuple-element.72), channel_id=1, source_target_pairs={{0,16},{8,24},{16,0},{24,8},{1,17},{9,25},{17,1},{25,9},{2,18},{10... | collective-permute-start | bytes 36872 | tf_op jit(solution)/shard_map/ppermute | solution.py:47
  9.1 5.0 %collective-permute-start.2 = (bf16[16,8,128]{2,1,0:T(8,128)(2,1)S(1)}, bf16[16,8,128]{2,1,0:T(8,128)(2,1)S(1)}, u32[]{:S(2)}, u32[]{:S(2)}) collective-permute-start(bf16[16,8,128]{2,1,0:T(8,128)(2,1)S(1)} %get-tuple-element.70), channel_id=1, source_target_pairs={{0,8},{8,0},{16,24},{24,16},{1,9},{9,1},{17,25},{25,17},{2,10},{10... | collective-permute-start | bytes 98312 | tf_op jit(solution)/shard_map/ppermute | solution.py:47
  14.2 3.9 %collective-permute-start.4 = (bf16[6,16,128]{2,1,0:T(8,128)(2,1)S(1)}, bf16[6,16,128]{2,1,0:T(8,128)(2,1)S(1)}, u32[]{:S(2)}, u32[]{:S(2)}) collective-permute-start(bf16[6,16,128]{2,1,0:T(8,128)(2,1)S(1)} %corners.2), channel_id=1, source_target_pairs={{0,4},{4,0},{1,5},{5,1},{2,6},{6,2},{3,7},{7,3},{8,12},{12,8},{9,1... | collective-permute-start | bytes 73736 | tf_op jit(solution)/shard_map/ppermute | solution.py:47
  19.7 8.4 %collective-permute-start.6 = (bf16[512,128]{1,0:T(8,128)(2,1)S(1)}, bf16[512,128]{1,0:T(8,128)(2,1)S(1)}, u32[]{:S(2)}, u32[]{:S(2)}) collective-permute-start(bf16[512,128]{1,0:T(8,128)(2,1)S(1)} %get-tuple-element.80), channel_id=1, source_target_pairs={{0,24},{8,16},{16,8},{24,0},{1,25},{9,17},{17,9},{25,1},{2,26},{10... | collective-permute-start | bytes 393224 | tf_op jit(solution)/shard_map/ppermute | solution.py:47
  21.7 3.4 %collective-permute-start.10 = (bf16[256,128]{1,0:T(8,128)(2,1)S(1)}, bf16[256,128]{1,0:T(8,128)(2,1)S(1)}, u32[]{:S(2)}, u32[]{:S(2)}) collective-permute-start(bf16[256,128]{1,0:T(8,128)(2,1)S(1)} %get-tuple-element.87), channel_id=1, source_target_pairs={{0,1},{1,0},{2,3},{3,2},{4,5},{5,4},{6,7},{7,6},{8,9},{9,8},{10,11... | collective-permute-start | bytes 196616 | tf_op jit(solution)/shard_map/ppermute | solution.py:175
  21.7 7.0 %collective-permute-start.7 = (bf16[16,8,128]{2,1,0:T(8,128)(2,1)S(1)}, bf16[16,8,128]{2,1,0:T(8,128)(2,1)S(1)}, u32[]{:S(2)}, u32[]{:S(2)}) collective-permute-start(bf16[16,8,128]{2,1,0:T(8,128)(2,1)S(1)} %get-tuple-element.81), channel_id=1, source_target_pairs={{0,8},{8,0},{16,24},{24,16},{1,9},{9,1},{17,25},{25,17},{2,10},{10... | collective-permute-start | bytes 98312 | tf_op jit(solution)/shard_map/ppermute | solution.py:47
  22.2 7.8 %collective-permute-start.5 = (bf16[6,64,128]{2,1,0:T(8,128)(2,1)S(1)}, bf16[6,64,128]{2,1,0:T(8,128)(2,1)S(1)}, u32[]{:S(2)}, u32[]{:S(2)}) collective-permute-start(bf16[6,64,128]{2,1,0:T(8,128)(2,1)S(1)} %get-tuple-element.79), channel_id=1, source_target_pairs={{0,4},{4,0},{1,5},{5,1},{2,6},{6,2},{3,7},{7,3},{8,12},{12,8},{9,1... | collective-permute-start | bytes 294920 | tf_op jit(solution)/shard_map/ppermute | solution.py:47
  25.1 7.1 %collective-permute-start.13 = (bf16[160,128]{1,0:T(8,128)(2,1)S(1)}, bf16[160,128]{1,0:T(8,128)(2,1)S(1)}, u32[]{:S(2)}, u32[]{:S(2)}) collective-permute-start(bf16[160,128]{1,0:T(8,128)(2,1)S(1)} %get-tuple-element.90), channel_id=1, source_target_pairs={{0,6},{1,7},{2,4},{3,5},{4,2},{5,3},{6,0},{7,1},{8,14},{9,15},{10,... | collective-permute-start | bytes 122888 | tf_op jit(solution)/shard_map/ppermute | solution.py:175
  27.1 5.1 %collective-permute-start.12 = (bf16[160,128]{1,0:T(8,128)(2,1)S(1)}, bf16[160,128]{1,0:T(8,128)(2,1)S(1)}, u32[]{:S(2)}, u32[]{:S(2)}) collective-permute-start(bf16[160,128]{1,0:T(8,128)(2,1)S(1)} %get-tuple-element.90), channel_id=1, source_target_pairs={{0,4},{4,0},{1,5},{5,1},{2,6},{6,2},{3,7},{7,3},{8,12},{12,8},{9,1... | collective-permute-start | bytes 122888 | tf_op jit(solution)/shard_map/ppermute | solution.py:175
  28.2 4.0 %collective-permute-start.11 = (bf16[160,128]{1,0:T(8,128)(2,1)S(1)}, bf16[160,128]{1,0:T(8,128)(2,1)S(1)}, u32[]{:S(2)}, u32[]{:S(2)}) collective-permute-start(bf16[160,128]{1,0:T(8,128)(2,1)S(1)} %get-tuple-element.89.refs_0_), channel_id=1, source_target_pairs={{0,2},{1,3},{2,0},{3,1},{4,6},{5,7},{6,4},{7,5},{8,10},{9,11},{10,... | collective-permute-start | bytes 122888 | tf_op jit(solution)/shard_map/ppermute | solution.py:175
  28.7 8.0 %collective-permute-start.9 = (bf16[6,16,128]{2,1,0:T(8,128)(2,1)S(1)}, bf16[6,16,128]{2,1,0:T(8,128)(2,1)S(1)}, u32[]{:S(2)}, u32[]{:S(2)}) collective-permute-start(bf16[6,16,128]{2,1,0:T(8,128)(2,1)S(1)} %corners.3), channel_id=1, source_target_pairs={{0,4},{4,0},{1,5},{5,1},{2,6},{6,2},{3,7},{7,3},{8,12},{12,8},{9,1... | collective-permute-start | bytes 73736 | tf_op jit(solution)/shard_map/ppermute | solution.py:47
  30.0 6.7 %collective-permute-start.8 = (bf16[6,8,128]{2,1,0:T(8,128)(2,1)S(1)}, bf16[6,8,128]{2,1,0:T(8,128)(2,1)S(1)}, u32[]{:S(2)}, u32[]{:S(2)}) collective-permute-start(bf16[6,8,128]{2,1,0:T(8,128)(2,1)S(1)} %get-tuple-element.83), channel_id=1, source_target_pairs={{0,16},{8,24},{16,0},{24,8},{1,17},{9,25},{17,1},{25,9},{2,18},{10... | collective-permute-start | bytes 36872 | tf_op jit(solution)/shard_map/ppermute | solution.py:47
  32.2 7.3 %collective-permute-start.16 = (bf16[160,128]{1,0:T(8,128)(2,1)S(1)}, bf16[160,128]{1,0:T(8,128)(2,1)S(1)}, u32[]{:S(2)}, u32[]{:S(2)}) collective-permute-start(bf16[160,128]{1,0:T(8,128)(2,1)S(1)} %add.34.refs_0_), channel_id=1, source_target_pairs={{0,24},{8,16},{16,8},{24,0},{1,25},{9,17},{17,9},{25,1},{2,26},{10... | collective-permute-start | bytes 122888 | tf_op jit(solution)/shard_map/ppermute | solution.py:175
  34.2 5.3 %collective-permute-start.15 = (bf16[160,128]{1,0:T(8,128)(2,1)S(1)}, bf16[160,128]{1,0:T(8,128)(2,1)S(1)}, u32[]{:S(2)}, u32[]{:S(2)}) collective-permute-start(bf16[160,128]{1,0:T(8,128)(2,1)S(1)} %add.34.refs_0_), channel_id=1, source_target_pairs={{0,16},{8,24},{16,0},{24,8},{1,17},{9,25},{17,1},{25,9},{2,18},{10... | collective-permute-start | bytes 122888 | tf_op jit(solution)/shard_map/ppermute | solution.py:175
  35.8 4.0 %collective-permute-start.14 = (bf16[160,128]{1,0:T(8,128)(2,1)S(1)}, bf16[160,128]{1,0:T(8,128)(2,1)S(1)}, u32[]{:S(2)}, u32[]{:S(2)}) collective-permute-start(bf16[160,128]{1,0:T(8,128)(2,1)S(1)} %add.34.refs_0_), channel_id=1, source_target_pairs={{0,8},{8,0},{16,24},{24,16},{1,9},{9,1},{17,25},{25,17},{2,10},{10... | collective-permute-start | bytes 122888 | tf_op jit(solution)/shard_map/ppermute | solution.py:175
  39.8 4.1 %collective-permute-start.17 = (bf16[160,128]{1,0:T(8,128)(2,1)S(1)}, bf16[160,128]{1,0:T(8,128)(2,1)S(1)}, u32[]{:S(2)}, u32[]{:S(2)}) collective-permute-start(bf16[160,128]{1,0:T(8,128)(2,1)S(1)} %add.35.own), channel_id=1, source_target_pairs={{0,4},{4,0},{1,5},{5,1},{2,6},{6,2},{3,7},{7,3},{8,12},{12,8},{9,1... | collective-permute-start | bytes 122888 | tf_op jit(solution)/shard_map/ppermute | solution.py:175
  43.9 1.3 %collective-permute-start.18 = (bf16[320,128]{1,0:T(8,128)(2,1)S(1)}, bf16[320,128]{1,0:T(8,128)(2,1)S(1)}, u32[]{:S(2)}, u32[]{:S(2)}) collective-permute-start(bf16[320,128]{1,0:T(8,128)(2,1)S(1)} %pad_maximum_fusion), channel_id=1, source_target_pairs={{0,1},{1,0},{2,3},{3,2},{4,5},{5,4},{6,7},{7,6},{8,9},{9,8},{10,11... | collective-permute-start | bytes 245768 | tf_op jit(solution)/shard_map/ppermute | solution.py:175
